TPU v7x, 128 devices: a whole 4x4x4 slice. The times are simulated.
128 devices in a mesh: seq: 8 (over z, x_lo), user: 16 (over y, x_hi, core).
Axes of the slice: x: 4 (x_hi: 2, x_lo: 2; x = x_hi * 2 + x_lo), y: 4, z: 4, core: 2. Of those that a mesh axis runs over, the one named last changes fastest.
Arguments:
- history: bfloat16 [16, 2048, 1024], P('user', 'seq'), may hold values from -6 to 6
- segment_ids: int32 [16, 2048], P('user', 'seq'), may hold values from 0 to 3, as said below
- w_in: bfloat16 [1024, 4096], replicated, may hold values from -0.1875 to 0.1875
- w_out: bfloat16 [1024, 1024], replicated, may hold values from -0.1875 to 0.1875
- cotangent: bfloat16 [16, 2048, 1024], P('user', 'seq'), may hold values from -6 to 6
Outputs:
- layer_out: bfloat16 [16, 2048, 1024], P('user', 'seq')
- grad_history: bfloat16 [16, 2048, 1024], P('user', 'seq')
- grad_w_in: float32 [1024, 4096], P(('seq', 'user'))
- grad_w_out: float32 [1024, 1024], P(('seq', 'user'))
Inputs may be any that keep to these rules, and one draw needn't show every extreme that they name: `segment_ids`: in each group the ids never fall along places (time order); each user has 1 to 1536 events and one has exactly 1536.
All inputs are finite; a program needn't handle non-finite values.
Results may differ from a plain program's by a relative error of at most 0.0083.
Values may be sent and summed in bfloat16 or wider, within the bound.
No kernel may reach another device: no remote copies, remote signals or barrier semaphores. Data moves between devices by JAX's collectives and lax.ppermute only.
A program may use at most 192 MiB of HBM per device.

v0:
```python
import functools

import jax
import jax.numpy as jnp
from jax import lax
from jax.experimental import pallas as pl
from jax.experimental.pallas import tpu as pltpu
from jax.sharding import PartitionSpec as P

F32 = jnp.float32
BF16 = jnp.bfloat16
EPS = 1e-05
H = 8
HD = 128
NZ, NX = 4, 2
NY, NXH, NC = 4, 2, 2


def seq_perm(dz, dx):
    return [
        (((z + dz) % NZ) * NX + (x ^ dx), z * NX + x) for z in range(NZ) for x in range(NX)
    ]


def user_perm(dy, dh, dc):
    return [
        ((((y + dy) % NY) * NXH + (h ^ dh)) * NC + (c ^ dc), (y * NXH + h) * NC + c)
        for y in range(NY)
        for h in range(NXH)
        for c in range(NC)
    ]


def from_seq(a, dz, dx):
    return lax.ppermute(a, "seq", seq_perm(dz, dx))


def from_user(a, dy, dh, dc):
    return lax.ppermute(a, "user", user_perm(dy, dh, dc))


def from_both(a, dh, dx):
    pairs = []
    for s in range(NZ * NX):
        for u in range(NY * NXH * NC):
            pairs.append(((s ^ dx) * NY * NXH * NC + (u ^ (dh * NC)), s * NY * NXH * NC + u))
    return lax.ppermute(a, ("seq", "user"), pairs)


def layer_norm(entries):
    centre = jnp.mean(entries, axis=-1, keepdims=True)
    centred = entries - centre
    inverse = lax.rsqrt(jnp.mean(centred * centred, axis=-1, keepdims=True) + EPS)
    return centred * inverse, inverse


def norm_back(normed, inverse, upstream):
    first_term = jnp.mean(upstream, axis=-1, keepdims=True)
    second_term = jnp.mean(upstream * normed, axis=-1, keepdims=True)
    return inverse * (upstream - first_term - normed * second_term)


def dot(a, b):
    return jnp.dot(a, b, preferred_element_type=F32)


def dot_nt(a, b):
    return lax.dot_general(a, b, (((1,), (1,)), ((), ())), preferred_element_type=F32)


def dot_tn(a, b):
    return lax.dot_general(a, b, (((0,), (0,)), ((), ())), preferred_element_type=F32)


LIMIT = 56


def params(limit):
    return pltpu.CompilerParams(vmem_limit_bytes=limit << 20)


def ln_proj_kernel(count, at_ref, *refs):
    w_ref = refs[count]
    normed_ref, act_ref, slope_ref = refs[-3:]
    half = act_ref.shape[2]
    for k in range(count):

        @pl.when(pl.program_id(0) == k)
        def _():
            normed, _ = layer_norm(refs[k][...].astype(F32))
            normed_b = normed.astype(BF16)
            normed_ref[...] = normed_b.T
            projected = dot(normed_b, w_ref[...])
            tanh = jnp.tanh(0.5 * projected)
            sig = 0.5 + 0.5 * tanh
            silu = projected * sig
            act = silu.astype(BF16)
            slope = sig + silu * (1.0 - sig)
            for i in range(2):
                act_ref[i, 0] = act[i * half : (i + 1) * half]
                slope_ref[i, 0] = slope[i * half : (i + 1) * half]


def ln_proj(at, blocks, w_head, outs):
    rows, width = blocks[0].shape
    cols = w_head.shape[1]
    half, shards = rows // 2, NZ * NX
    by_half = pl.BlockSpec((2, 1, half, cols), lambda i, at_ref: (0, at_ref[i], 0, 0))
    in_specs = [pl.BlockSpec((rows, width), lambda i, at_ref: (0, 0))] * len(blocks)
    in_specs.append(pl.BlockSpec((width, cols), lambda i, at_ref: (0, 0)))
    aliases = {}
    if outs:
        in_specs += [pl.BlockSpec(memory_space=pl.ANY)] * 3
        aliases = {len(in_specs) + k - 2: k for k in range(3)}
    return pl.pallas_call(
        functools.partial(ln_proj_kernel, len(blocks)),
        grid_spec=pltpu.PrefetchScalarGridSpec(
            num_scalar_prefetch=1,
            grid=(len(blocks),),
            in_specs=in_specs,
            out_specs=(
                pl.BlockSpec((width, rows), lambda i, at_ref: (0, at_ref[i])),
                by_half,
                by_half,
            ),
        ),
        out_shape=(
            jax.ShapeDtypeStruct((width, rows * shards), BF16),
            jax.ShapeDtypeStruct((2, shards, half, cols), BF16),
            jax.ShapeDtypeStruct((2, shards, half, cols), F32),
        ),
        input_output_aliases=aliases,
        compiler_params=params(LIMIT),
        cost_estimate=pl.CostEstimate(
            flops=2 * rows * width * cols * len(blocks),
            bytes_accessed=3 * len(blocks) << 20,
            transcendentals=rows * cols * len(blocks),
        ),
        name="ln_proj",
    )(at, *blocks, w_head, *outs)


FQ, FK = 512, 512
BQ, BK = 512, 256
SCALE = HD ** (-0.5)
UNSEEN = -1024.0


def tile_place(block):
    last = 2 * NZ * NX - 1
    return (block, 0) if block < NZ * NX else (last - block, HD)


def time_rows(ref, first, count, column, columns=1):
    parts = []
    for block in range(first // HD, (first + count) // HD):
        shard, row = tile_place(block)
        parts.append(ref[row // HD, shard, :, column * HD : (column + columns) * HD])
    return parts[0] if len(parts) == 1 else jnp.concatenate(parts, axis=0)


def tiles(length, rows, cols):
    key_row = lax.broadcasted_iota(jnp.int32, (cols, rows), 0)
    query_col = lax.broadcasted_iota(jnp.int32, (1, rows), 1)

    def seen(i, j, start):
        mask = key_row >= start - j
        if j + cols > i:
            mask = mask & (key_row <= query_col + (i - j))
        return mask

    return [(i, range(0, i + rows, cols)) for i in range(0, length, rows)], seen


def forward_kernel(act_ref, head_ref, att_ref, gate_ref, gg_ref, stats_ref, start_ref):
    length = att_ref.shape[1]
    rows = length // (NZ * NX)
    users = [head_ref[shard, rows:, :].astype(F32) for shard in range(NZ * NX)]
    places = [tile_place(block) for block in range(length // HD)]
    ids = jnp.concatenate([users[s][r // HD : r // HD + 1] for s, r in places], axis=1)
    first = jnp.zeros((1, length), F32)
    for v in range(3):
        count = jnp.sum(jnp.where(ids == v, 1.0, 0.0), axis=1, keepdims=True)
        first = first + jnp.where(ids > v, count, 0.0)
    start_ref[...] = first.astype(jnp.int32)
    values_t = [time_rows(act_ref, j, FK, 1).T for j in range(0, length, FK)]
    keys = [time_rows(act_ref, j, FK, 3) for j in range(0, length, FK)]
    queries_in, seen = tiles(length, FQ, FK)
    for i, keys_in in queries_in:
        at = slice(i, i + FQ)
        queries = time_rows(act_ref, i, FQ, 2)
        start = start_ref[:, at]
        total = None
        for j in keys_in:
            half = dot_nt(keys[j // FK], queries) * (0.5 * SCALE)
            half = jnp.where(seen(i, j, start), half, UNSEEN)
            weights = (half + half * jnp.tanh(half)).astype(BF16)
            term = dot(values_t[j // FK], weights)
            total = term if total is None else total + term
        att_ref[:, at] = total
        gate = time_rows(act_ref, i, FQ, 0).T
        parts = []
        for block in range(i // HD, (i + FQ) // HD):
            shard, row = tile_place(block)
            parts.append(head_ref[shard, row : row + HD, :])
        gg = jnp.concatenate(parts, axis=0).T
        gate_ref[:, at] = gate
        gg_ref[:, at] = gg
        grad_mixed = gg.astype(F32) * gate.astype(F32)
        mean = jnp.sum(total, axis=0, keepdims=True) * (1.0 / HD)
        centred = total - mean
        stats_ref[0:1, at] = mean
        stats_ref[1:2, at] = jnp.sum(centred * centred, axis=0, keepdims=True)
        stats_ref[2:3, at] = jnp.sum(grad_mixed, axis=0, keepdims=True)
        stats_ref[3:4, at] = jnp.sum(grad_mixed * centred, axis=0, keepdims=True)


def vmem():
    return pl.BlockSpec(memory_space=pltpu.VMEM)


def smem():
    return pl.BlockSpec(memory_space=pltpu.SMEM)


def forward(act, at_head):
    length = HD * 2 * NZ * NX
    return pl.pallas_call(
        forward_kernel,
        in_specs=[vmem()] * 2,
        out_specs=[vmem()] * 5,
        out_shape=(
            jax.ShapeDtypeStruct((HD, length), F32),
            jax.ShapeDtypeStruct((HD, length), BF16),
            jax.ShapeDtypeStruct((HD, length), BF16),
            jax.ShapeDtypeStruct((4, length), F32),
            jax.ShapeDtypeStruct((1, length), jnp.int32),
        ),
        compiler_params=params(LIMIT),
        cost_estimate=pl.CostEstimate(
            flops=8 * HD * length * length, bytes_accessed=6 << 20, transcendentals=length * length // 2
        ),
        name="attention_forward",
    )(act, at_head)


def mix_kernel(own_ref, one_ref, three_ref, two_ref, att_ref, gate_ref, gg_ref, slope_ref, early_ref, go_ref, got_ref):
    length = att_ref.shape[1]
    width = H * HD
    tile = 2 * HD
    heads = [ref[k] for ref in (own_ref, one_ref, three_ref, two_ref) for k in range(NX)]
    mean_all = sum(a[0:1] for a in heads) * (1.0 / H)
    apart = [a[0:1] - mean_all for a in heads]
    spread = sum(a[1:2] for a in heads) + HD * sum(d * d for d in apart)
    inverse_all = lax.rsqrt(spread * (1.0 / width) + EPS)
    first_all = sum(a[2:3] for a in heads) * (1.0 / width)
    second_all = inverse_all * sum(a[3:4] + d * a[2:3] for a, d in zip(heads, apart)) * (1.0 / width)
    for i in range(0, length, tile):
        at = slice(i, i + tile)
        gate = gate_ref[:, at].astype(F32)
        gg = gg_ref[:, at].astype(F32)
        inverse = inverse_all[:, at]
        mixed = (att_ref[:, at] - mean_all[:, at]) * inverse
        grad_att = inverse * (gg * gate - first_all[:, at] - mixed * second_all[:, at])
        got_ref[:, at] = grad_att.astype(BF16)
        go_ref[at, :] = grad_att.T.astype(BF16)
        gated = (mixed * gate).astype(BF16).T
        grad_u = ((gg * mixed).T * time_rows(slope_ref, i, tile, 0)).astype(BF16)
        for k in range(2):
            shard, row = tile_place(i // HD + k)
            early_ref[shard, row : row + HD, :HD] = gated[k * HD : (k + 1) * HD]
            early_ref[shard, row : row + HD, HD:] = grad_u[k * HD : (k + 1) * HD]


def mix(own, one, three, two, att, gate, gg, slope):
    length = att.shape[1]
    shards = NZ * NX
    whole = lambda shape: pl.BlockSpec(shape, lambda i: (0,) * len(shape))
    return pl.pallas_call(
        mix_kernel,
        grid=(1,),
        in_specs=[whole(own.shape)] * 4
        + [whole(att.shape)] * 3
        + [pl.BlockSpec(slope.shape[:3] + (HD,), lambda i: (0, 0, 0, 0))],
        out_specs=[whole((shards, length // shards, 2 * HD)), whole((length, HD)), whole((HD, length))],
        out_shape=(
            jax.ShapeDtypeStruct((shards, length // shards, 2 * HD), BF16),
            jax.ShapeDtypeStruct((length, HD), BF16),
            jax.ShapeDtypeStruct((HD, length), BF16),
        ),
        compiler_params=params(LIMIT),
        cost_estimate=pl.CostEstimate(flops=20 * HD * length, bytes_accessed=6 << 20, transcendentals=0),
        name="mix",
    )(own, one, three, two, att, gate, gg, slope)


def backward_kernel(act_ref, go_ref, got_ref, start_ref, early_ref, slope_hbm, back_ref, dk_ref, dv_ref, slope_ref, sem):
    length = go_ref.shape[0]
    copy = pltpu.make_async_copy(slope_hbm, slope_ref, sem)
    copy.start()
    back_ref[:, :, :HD] = early_ref[:, :, HD:]
    back_ref[:, :, 4 * HD :] = early_ref[:, :, :HD]
    keys = [time_rows(act_ref, j, BK, 3) for j in range(0, length, BK)]
    keys_t = [k.T for k in keys]
    values = [time_rows(act_ref, j, BK, 1) for j in range(0, length, BK)]
    queries_in, seen = tiles(length, BQ, BK)

    def put(first, column, value):
        value = (value * time_rows(slope_ref, first, value.shape[0], column)).astype(BF16)
        for k in range(value.shape[0] // HD):
            shard, row = tile_place(first // HD + k)
            back_ref[shard, row : row + HD, column * HD : (column + 1) * HD] = value[
                k * HD : (k + 1) * HD
            ]

    started = set()
    for i, keys_in in queries_in:
        at = slice(i, i + BQ)
        queries = time_rows(act_ref, i, BQ, 2)
        grad_out = go_ref[at, :]
        grad_out_t = got_ref[:, at]
        start = start_ref[:, at]
        total = None
        for j in keys_in:
            here = slice(j, j + BK)
            half = dot_nt(keys[j // BK], queries) * (0.5 * SCALE)
            half = jnp.where(seen(i, j, start), half, UNSEEN)
            tanh = jnp.tanh(half)
            weights = half + half * tanh
            sig = 0.5 + 0.5 * tanh
            slope = sig + weights * (1.0 - sig)
            ahead = dot(values[j // BK], grad_out_t)
            weights = weights.astype(BF16)
            slopes = (ahead * slope).astype(BF16)
            dv = dot(weights, grad_out)
            dk = dot(slopes, queries)
            if j in started:
                dv_ref[here, :] += dv
                dk_ref[here, :] += dk
            else:
                dv_ref[here, :] = dv
                dk_ref[here, :] = dk
                started.add(j)
            term = dot(keys_t[j // BK], slopes)
            total = term if total is None else total + term
        if i == 0:
            copy.wait()
        put(i, 2, total.T * SCALE)
    for j in range(0, length, BK):
        put(j, 1, dv_ref[j : j + BK, :])
        put(j, 3, dk_ref[j : j + BK, :] * SCALE)


def backward(act, grad_out, grad_out_t, start, early, slope):
    length = start.shape[1]
    shards = NZ * NX
    return pl.pallas_call(
        backward_kernel,
        in_specs=[vmem()] * 5 + [pl.BlockSpec(memory_space=pl.ANY)],
        out_specs=vmem(),
        out_shape=jax.ShapeDtypeStruct((shards, length // shards, 5 * HD), BF16),
        scratch_shapes=[pltpu.VMEM((length, HD), F32)] * 2
        + [pltpu.VMEM(slope.shape, F32), pltpu.SemaphoreType.DMA],
        compiler_params=params(LIMIT),
        cost_estimate=pl.CostEstimate(
            flops=15 * HD * length * length, bytes_accessed=10 << 20, transcendentals=length * length // 2
        ),
        name="attention_backward",
    )(act, grad_out, grad_out_t, start, early, slope)


def terms_in_kernel(core_ref, normed_ref, grad_ref, keep_ref, send_ref, res_ref):
    shards, rows, cols = grad_ref.shape
    res_ref[...] = dot(normed_ref[...], grad_ref[...].reshape(shards * rows, cols))
    core = core_ref[0]
    for k in range(res_ref.shape[0] // HD):
        for pair in range(NY * NXH):
            mine = pl.multiple_of(k * HD + (pair * NC + core) * 8, 8)
            other = pl.multiple_of(k * HD + (pair * NC + 1 - core) * 8, 8)
            keep_ref[pair, k * 8 : (k + 1) * 8, :] = res_ref[pl.ds(mine, 8), :]
            send_ref[pair, k * 8 : (k + 1) * 8, :] = res_ref[pl.ds(other, 8), :]


def terms_in(core, normed_t, back):
    width, length = normed_t.shape
    shards, rows, _ = back.shape
    shape = jax.ShapeDtypeStruct((NY * NXH, 64, 4 * HD), F32)
    out_spec = pl.BlockSpec((NY * NXH, 16, 4 * HD), lambda g: (0, g, 0))
    return pl.pallas_call(
        terms_in_kernel,
        grid=(4,),
        in_specs=[
            smem(),
            pl.BlockSpec((width // 4, length), lambda g: (g, 0)),
            pl.BlockSpec((shards, rows, 4 * HD), lambda g: (0, 0, 0)),
        ],
        out_specs=[out_spec] * 2,
        out_shape=[shape] * 2,
        scratch_shapes=[pltpu.VMEM((width // 4, 4 * HD), F32)],
        compiler_params=params(LIMIT),
        cost_estimate=pl.CostEstimate(
            flops=2 * width * length * 4 * HD, bytes_accessed=9 << 20, transcendentals=0
        ),
        name="terms_in",
    )(core, normed_t, back)


def terms_out_kernel(core_ref, at_ref, gated_ref, *refs):
    keep_ref, send_ref, res_ref, gated_t_ref = refs[-4:]
    shards, rows, _ = gated_ref.shape

    @pl.when(pl.program_id(0) == 0)
    def _():
        for shard in range(shards):
            gated_t_ref[:, shard * rows : (shard + 1) * rows] = gated_ref[shard].T

    total = None
    for r in range(shards):
        here = pl.ds(pl.multiple_of(at_ref[r] * rows, rows), rows)
        term = dot(gated_t_ref[:, here], refs[r][...])
        total = term if total is None else total + term
    res_ref[...] = total
    core = core_ref[0]
    for pair in range(NY * NXH):
        for out_ref, who in ((keep_ref, core), (send_ref, 1 - core)):
            out_ref[pair] = res_ref[pl.ds(pl.multiple_of((pair * NC + who) * 8, 8), 8), :]


def terms_out(core, at, back, cots):
    shards, rows, _ = back.shape
    width = cots[0].shape[1]
    length = shards * rows
    out_spec = pl.BlockSpec((NY * NXH, 8, 4 * HD), lambda g: (0, g, 0))
    return pl.pallas_call(
        terms_out_kernel,
        grid=(2,),
        in_specs=[smem(), smem(), pl.BlockSpec((shards, rows, HD), lambda g: (0, 0, 4))]
        + [pl.BlockSpec((rows, width // 2), lambda g: (0, g))] * shards,
        out_specs=[out_spec] * 2,
        out_shape=[jax.ShapeDtypeStruct((NY * NXH, 16, 4 * HD), F32)] * 2,
        scratch_shapes=[pltpu.VMEM((HD, width // 2), F32), pltpu.VMEM((HD, length), BF16)],
        compiler_params=params(LIMIT),
        cost_estimate=pl.CostEstimate(
            flops=2 * HD * width * length, bytes_accessed=6 << 20, transcendentals=0
        ),
        name="terms_out",
    )(core, at, back, *cots)


def small(kernel, name, scalars, arrays, outs, scratch=(), limit=12):
    size = sum(a.size * a.dtype.itemsize for a in arrays)
    return pl.pallas_call(
        kernel,
        in_specs=[smem()] + [vmem()] * len(arrays),
        out_specs=[vmem()] * len(outs),
        out_shape=[jax.ShapeDtypeStruct(shape, dtype) for shape, dtype in outs],
        scratch_shapes=list(scratch),
        compiler_params=params(limit),
        cost_estimate=pl.CostEstimate(flops=size, bytes_accessed=2 * size, transcendentals=0),
        name=name,
    )(scalars, *arrays)


def core_sum_kernel(pos_ref, keep_ref, got_ref, keep_out_ref, got_out_ref, own_ref, one_ref, three_ref, two_ref):
    y = pos_ref[0]
    for d, to_ref in ((0, own_ref), (1, one_ref), (3, three_ref), (2, two_ref)):
        here = pl.ds(((y - d + NY) % NY) * NXH, NXH)
        to_ref[:, :64, :] = (keep_ref[here] + got_ref[here]).astype(to_ref.dtype)
        to_ref[:, 64:, :] = (keep_out_ref[here] + got_out_ref[here]).astype(to_ref.dtype)


def y_sum_kernel(pos_ref, own_ref, a_ref, b_ref, c_ref, keep_ref, same_ref, one_ref, two_ref, sum_ref):
    xh, x = pos_ref[1], pos_ref[2]
    sum_ref[...] = own_ref[...] + (
        a_ref[...].astype(F32) + b_ref[...].astype(F32) + c_ref[...].astype(F32)
    )

    def slab(out_ref, h, l):
        for k in range(NZ):
            out_ref[k * 8 : (k + 1) * 8, :] = sum_ref[
                h, pl.ds(pl.multiple_of((k * NX + l) * 8, 8), 8), :
            ]

    slab(keep_ref, xh, x)
    keep_ref[32:, :] = sum_ref[xh, 64:, :]
    slab(same_ref, 1 - xh, x)
    same_ref[32:, :] = sum_ref[1 - xh, 64:, :]
    slab(one_ref, xh, 1 - x)
    slab(two_ref, 1 - xh, 1 - x)


def x_sum_kernel(pos_ref, keep_ref, same_ref, a_ref, b_ref, own_ref, one_ref, three_ref, two_ref, out_ref, sum_ref):
    z, x = pos_ref[3], pos_ref[2]
    mine = keep_ref[...] + same_ref[...]
    sum_ref[x] = mine[:32]
    sum_ref[1 - x] = a_ref[...] + b_ref[...]
    out_ref[...] = mine[32:]
    for d, to_ref in ((0, own_ref), (1, one_ref), (3, three_ref), (2, two_ref)):
        here = pl.ds(pl.multiple_of(((z - d + NZ) % NZ) * 8, 8), 8)
        for l in range(NX):
            to_ref[l * 8 : (l + 1) * 8, :] = sum_ref[l, here, :]


def z_place_kernel(factor, pos_ref, own_ref, one_ref, three_ref, two_ref, out_ref, w_in_ref, w_out_ref):
    z = pos_ref[3]
    for d, ref in ((0, own_ref), (1, one_ref), (3, three_ref), (2, two_ref)):
        for l in range(NX):
            for k in range(4):
                at = pl.multiple_of((k * H + ((z + d) % NZ) * NX + l) * HD, HD)
                w_in_ref[:, pl.ds(at, HD)] = (
                    ref[l * 8 : (l + 1) * 8, k * HD : (k + 1) * HD] * factor
                )
    w_out_ref[:, : 4 * HD] = out_ref[:8] * factor
    w_out_ref[:, 4 * HD :] = out_ref[8:] * factor


def columns(ref):
    return jnp.concatenate([ref[h] for h in range(H)], axis=1)


def shard_out_kernel(gated_ref, grad_ref, w_in_ref, w_out_ref, hist_ref, layer_ref, acc_ref):
    term = dot_nt(columns(grad_ref), w_in_ref[...])

    @pl.when(pl.program_id(0) == 0)
    def _():
        hist = hist_ref[...].astype(F32)
        layer_ref[...] = (hist + dot(columns(gated_ref), w_out_ref[...])).astype(BF16)
        acc_ref[...] = term

    @pl.when(pl.program_id(0) > 0)
    def _():
        acc_ref[...] += term


def shard_grad_kernel(grad_ref, w_in_ref, hist_ref, cot_ref, half_ref, grad_hist_ref, acc_ref):
    term = dot_nt(columns(grad_ref), w_in_ref[...])

    @pl.when(pl.program_id(0) == 0)
    def _():
        acc_ref[...] = half_ref[...] + term

    @pl.when(pl.program_id(0) > 0)
    def _():
        normed, inverse = layer_norm(hist_ref[...].astype(F32))
        grad = norm_back(normed, inverse, acc_ref[...] + term)
        grad_hist_ref[...] = (cot_ref[...].astype(F32) + grad).astype(BF16)


def shard_out(back, w_in, w_out, hist):
    rows, width = hist.shape
    whole = lambda a: pl.BlockSpec(a.shape, lambda k: (0,) * a.ndim)
    return pl.pallas_call(
        shard_out_kernel,
        grid=(2,),
        in_specs=[
            pl.BlockSpec((H, rows, HD), lambda k: (0, 0, 4)),
            pl.BlockSpec((H, rows, HD), lambda k: (0, 0, k)),
            pl.BlockSpec((width, width), lambda k: (0, k)),
            whole(w_out),
            whole(hist),
        ],
        out_specs=[whole(hist)] * 2,
        out_shape=[jax.ShapeDtypeStruct(hist.shape, BF16), jax.ShapeDtypeStruct(hist.shape, F32)],
        compiler_params=params(LIMIT),
        cost_estimate=pl.CostEstimate(
            flops=6 * rows * width * width, bytes_accessed=8 << 20, transcendentals=0
        ),
        name="shard_out",
    )(back, back, w_in, w_out, hist)


def shard_grad(back, w_in, hist, cot, half):
    rows, width = hist.shape
    whole = lambda a: pl.BlockSpec(a.shape, lambda k: (0,) * a.ndim)
    return pl.pallas_call(
        shard_grad_kernel,
        grid=(2,),
        in_specs=[
            pl.BlockSpec((H, rows, HD), lambda k: (0, 0, 2 + k)),
            pl.BlockSpec((width, width), lambda k: (0, 2 + k)),
            whole(hist),
            whole(cot),
            whole(half),
        ],
        out_specs=whole(hist),
        out_shape=jax.ShapeDtypeStruct(hist.shape, BF16),
        scratch_shapes=[pltpu.VMEM((rows, width), F32)],
        compiler_params=params(LIMIT),
        cost_estimate=pl.CostEstimate(
            flops=4 * rows * width * width, bytes_accessed=8 << 20, transcendentals=0
        ),
        name="shard_grad",
    )(back, w_in, hist, cot, half)


def local(history, segment_ids, w_in, w_out, cotangent):
    hist = history[0]
    cot = cotangent[0]
    rows, width = hist.shape
    length = rows * NZ * NX
    s = lax.axis_index("seq")
    u = lax.axis_index("user")
    z, x = s // NX, s % NX
    y, xh, core = u // (NXH * NC), (u // NC) % NXH, u % NC

    users = NY * NXH * NC
    tie = lax.optimization_barrier
    w_head = jnp.concatenate(
        [lax.dynamic_slice(w_in, (0, i * width + s * HD), (width, HD)) for i in range(4)], axis=1
    )

    def place_of(key):
        return ((z + key[0]) % NZ) * NX + (x ^ key[1])

    def project(got, outs):
        at = jnp.stack([place_of(key) for key in got])
        return ln_proj(at, list(got.values()), w_head, outs)

    got = {
        (1, 0): from_seq(hist, 1, 0),
        (3, 0): from_seq(hist, 3, 0),
        (0, 1): from_seq(hist, 0, 1),
    }
    outs = project({(0, 0): hist}, ())
    grad_gated_own = dot_nt(cot, w_out).astype(BF16).reshape(rows, H, HD).transpose(1, 0, 2)
    got, outs, grad_gated_own = tie((got, outs, grad_gated_own))
    ids = segment_ids[0].astype(BF16).reshape(2, HD)
    ids = jnp.pad(ids, ((0, 14), (0, 0)))
    to_heads = jnp.concatenate(
        [
            grad_gated_own,
            jnp.broadcast_to(ids[None], (H, 16, HD)),
        ],
        axis=1,
    )
    at_head = lax.all_to_all(to_heads, "seq", 0, 0, tiled=True)
    more = {
        (2, 0): from_seq(got[1, 0], 1, 0),
        (3, 1): from_seq(got[0, 1], 3, 0),
        (1, 1): from_seq(got[1, 0], 0, 1),
    }
    outs = project(got, outs)
    more, outs, cot_next = tie((more, outs, cot))
    last = {(2, 1): from_seq(more[2, 0], 0, 1)}
    cots = {(1, 0): from_seq(cot_next, 1, 0), (3, 0): from_seq(cot_next, 3, 0)}
    outs, at_head = tie((outs, at_head))
    outs = project(more, outs)
    last, cots, outs = tie((last, cots, outs))
    fresh = {(0, 1): from_seq(cot_next, 0, 1), (2, 0): from_seq(cots[1, 0], 1, 0)}
    normed_t, act, slope = project(last, outs)
    att, gate_t, gg_t, stats, start = forward(act, at_head)
    stats, fresh = tie((stats, fresh))
    cots.update(fresh)
    pair = jnp.stack([stats, from_seq(stats, 0, 1)])
    others = [from_seq(pair, dz, 0) for dz in (1, 3, 2)]
    early, grad_out, grad_out_t = mix(pair, *others, att, gate_t, gg_t, slope)
    early, grad_out, grad_out_t, cots = tie((early, grad_out, grad_out_t, cots))
    fresh = {
        (2, 1): from_seq(cots[2, 0], 0, 1),
        (1, 1): from_seq(cots[0, 1], 1, 0),
        (3, 1): from_seq(cots[0, 1], 3, 0),
    }
    back = backward(act, grad_out, grad_out_t, start, early, slope)
    back, fresh = tie((back, fresh))
    cots.update(fresh)
    cots[0, 0] = cot
    back_tok = lax.all_to_all(back, "seq", 0, 0, tiled=True)

    at_core = core.reshape(1)
    keep, send = terms_in(at_core, normed_t, back)
    places = jnp.stack([place_of(key) for key in cots])
    got = from_user(send, 0, 0, 1)
    keep_out, send_out = terms_out(at_core, places, back, list(cots.values()))
    got_out = from_user(send_out, 0, 0, 1)
    at = jnp.stack([y, xh, x, z])
    n = 4 * HD
    own, *sends = small(
        core_sum_kernel,
        "core_sum",
        at,
        [keep, got, keep_out, got_out],
        [((NXH, 80, n), F32)] + [((NXH, 80, n), BF16)] * 3,
        limit=LIMIT,
    )
    own, sends = tie((own, sends))
    sends = [from_user(a, d, 0, 0) for a, d in zip(sends, (1, 3, 2))]
    layer_out, half = shard_out(back_tok, w_in, w_out, hist)
    sends, layer_out, half = tie((sends, layer_out, half))
    keep, same, one, two = small(
        y_sum_kernel,
        "y_sum",
        at,
        [own, *sends],
        [((48, n), F32)] * 2 + [((32, n), F32)] * 2,
        [pltpu.VMEM((NXH, 80, n), F32)],
    )
    same = from_both(same, 1, 0)
    one = from_both(one, 0, 1)
    two = from_both(two, 1, 1)
    grad_history = shard_grad(back_tok, w_in, hist, cot, half)
    same, one, two, grad_history = tie((same, one, two, grad_history))
    own, *sends, own_out = small(
        x_sum_kernel,
        "x_sum",
        at,
        [keep, same, one, two],
        [((16, n), F32)] * 5,
        [pltpu.VMEM((NX, 32, n), F32)],
    )
    sends = [from_seq(a, d, 0) for a, d in zip(sends, (1, 3, 2))]
    factor = (length * users) ** (-0.5)
    grad_w_in, grad_w_out = small(
        functools.partial(z_place_kernel, factor),
        "z_place",
        at,
        [own, *sends, own_out],
        [((8, 4 * width), F32), ((8, width), F32)],
    )
    return layer_out[None], grad_history[None], grad_w_in, grad_w_out


def solution(mesh):
    in_specs = (P("user", "seq", None), P("user", "seq"), P(), P(), P("user", "seq", None))
    out_specs = (
        P("user", "seq", None),
        P("user", "seq", None),
        P(("seq", "user"), None),
        P(("seq", "user"), None),
    )
    return jax.shard_map(local, mesh=mesh, in_specs=in_specs, out_specs=out_specs, check_vma=False)
```

profile of v0, /device:TPU:0, one launch (start us, length us, event | category | flops | bytes accessed | tf_op | source)
XLA Modules:
  0.0 157.3 jit_solution(12100116867339577900)
XLA Ops:
  0.6 1.7 %collective-permute-start = (bf16[256,1024]{1,0:T(8,128)(2,1)}, bf16[256,1024]{1,0:T(8,128)(2,1)S(1)}, u32[]{:S(2)}, u32[]{:S(2)}) collective-permute-start(bf16[256,1024]{1,0:T(8,128)(2,1)} %bitcast.25), channel_id=1, source_target_pairs={{16,0},{0,16},{48,32},{32,48},{80,64},{64,80},{112,96},{96,112},{1... | collective-permute-start | bytes 1572872 | tf_op jit(solution)/shard_map/ppermute | solution.py:35
  2.3 4.0 %collective-permute-start.1 = (bf16[256,1024]{1,0:T(8,128)(2,1)}, bf16[256,1024]{1,0:T(8,128)(2,1)S(1)}, u32[]{:S(2)}, u32[]{:S(2)}) collective-permute-start(bf16[256,1024]{1,0:T(8,128)(2,1)} %bitcast.26), channel_id=1, source_target_pairs={{32,0},{48,16},{64,32},{80,48},{96,64},{112,80},{0,96},{16,112},{3... | collective-permute-start | bytes 1572872 | tf_op jit(solution)/shard_map/ppermute | solution.py:35
  6.3 2.5 %convolution_convert_fusion = bf16[256,1024]{1,0:T(8,128)(2,1)S(1)} fusion(bf16[1024,1024]{1,0:T(8,128)(2,1)} %w_out_ref.1, bf16[1,256,1024]{2,1,0:T(8,128)(2,1)} %param.9), kind=kOutput, calls=%fused_computation | convolution fusion | flops 537133056 | bytes 3145728 | tf_op jit(solution)/shard_map/dot_general | solution.py:68
  9.3 1.3 constant_dynamic-slice_fusion.3
  10.7 1.1 pad_maximum_fusion.refs_1_.refs_3_
  11.7 3.1 %ln_proj.4 = (bf16[1024,2048]{1,0:T(8,128)(2,1)}, bf16[2,8,128,512]{3,2,1,0:T(8,128)(2,1)}, f32[2,8,128,512]{3,2,1,0:T(8,128)}) custom-call(s32[1]{0:T(128)} %bitcast.7.at_ref, bf16[256,1024]{1,0:T(8,128)(2,1)} %bitcast.28, bf16[1024,512]{1,0:T(8,128)(2,1)} %pad_maximum_fusion.refs_1_.refs_3_), custom_call_target="tpu_custom_call" | custom-call | flops 268435456 | bytes 3145728 | tf_op jit(solution)/shard_map/ln_proj/pallas_call | solution.py:115
  14.8 2.7 %collective-permute-done.1.refs_1_ = bf16[256,1024]{1,0:T(8,128)(2,1)S(1)} collective-permute-done((bf16[256,1024]{1,0:T(8,128)(2,1)}, bf16[256,1024]{1,0:T(8,128)(2,1)S(1)}, u32[]{:S(2)}, u32[]{:S(2)}) %collective-permute-start.1) | collective-permute-done | bytes 524320 | tf_op jit(solution)/shard_map/ppermute | solution.py:35
  17.5 3.3 %collective-permute-done.2.refs_2_ = bf16[256,1024]{1,0:T(8,128)(2,1)S(1)} collective-permute-done((bf16[256,1024]{1,0:T(8,128)(2,1)}, bf16[256,1024]{1,0:T(8,128)(2,1)S(1)}, u32[]{:S(2)}, u32[]{:S(2)}) %collective-permute-start.2) | collective-permute-done | bytes 524320 | tf_op jit(solution)/shard_map/ppermute | solution.py:35
  21.7 1.7 %collective-permute-start.5 = (bf16[256,1024]{1,0:T(8,128)(2,1)S(1)}, bf16[256,1024]{1,0:T(8,128)(2,1)}, u32[]{:S(2)}, u32[]{:S(2)}) collective-permute-start(bf16[256,1024]{1,0:T(8,128)(2,1)S(1)} %collective-permute-done.refs_0_), channel_id=1, source_target_pairs={{96,0},{112,16},{0,32},{16,48},{32,64},{48,80},{64,96},{80,112},{9... | collective-permute-start | bytes 1572872 | tf_op jit(solution)/shard_map/ppermute | solution.py:35
  24.0 0.9 pad_maximum_fusion.1
  24.9 3.8 %all-to-all-start = ((bf16[8,272,128]{2,1,0:T(8,128)(2,1)}), bf16[8,272,128]{2,1,0:T(8,128)(2,1)S(1)}, u32[]{:S(2)}, u32[]{:S(2)}) async-start(bf16[8,272,128]{2,1,0:T(8,128)(2,1)} %pad_maximum_fusion.1), calls=%async_computation | async-start | bytes 1114112 | tf_op jit(solution)/shard_map/all_to_all | solution.py:636
  28.7 6.5 %ln_proj.5 = (bf16[1024,2048]{1,0:T(8,128)(2,1)}, bf16[2,8,128,512]{3,2,1,0:T(8,128)(2,1)}, f32[2,8,128,512]{3,2,1,0:T(8,128)}) custom-call(s32[3]{0:T(128)} %get-tuple-element.184.at_ref, bf16[256,1024]{1,0:T(8,128)(2,1)} %copy-done.5, bf16[256,1024]{1,0:T(8,128)(2,1)} %copy-done.6, ...), custom_call_target="tpu_custom_call", output_to_operand_aliasing={{0}: (5, {}), {1}: (6, {}), {2}: (7, {})} | custom-call | flops 805306368 | bytes 9437184 | tf_op jit(solution)/shard_map/ln_proj/pallas_call | solution.py:115
  35.8 2.6 %collective-permute-done.4.refs_1_ = bf16[256,1024]{1,0:T(8,128)(2,1)} collective-permute-done((bf16[256,1024]{1,0:T(8,128)(2,1)S(1)}, bf16[256,1024]{1,0:T(8,128)(2,1)}, u32[]{:S(2)}, u32[]{:S(2)}) %collective-permute-start.4) | collective-permute-done | bytes 524320 | tf_op jit(solution)/shard_map/ppermute | solution.py:35
  38.7 3.2 %collective-permute-start.6 = (bf16[256,1024]{1,0:T(8,128)(2,1)}, bf16[256,1024]{1,0:T(8,128)(2,1)}, u32[]{:S(2)}, u32[]{:S(2)}) collective-permute-start(bf16[256,1024]{1,0:T(8,128)(2,1)} %collective-permute-done.4.refs_1_), channel_id=1, source_target_pairs={{16,0},{0,16},{48,32},{32,48},{80,64},{64,80},{112,96},{96,112},{1... | collective-permute-start | bytes 1572872 | tf_op jit(solution)/shard_map/ppermute | solution.py:35
  41.9 2.0 %collective-permute-start.8 = (bf16[256,1024]{1,0:T(8,128)(2,1)S(1)}, bf16[256,1024]{1,0:T(8,128)(2,1)S(1)}, u32[]{:S(2)}, u32[]{:S(2)}) collective-permute-start(bf16[256,1024]{1,0:T(8,128)(2,1)S(1)} %bitcast.36), channel_id=1, source_target_pairs={{96,0},{112,16},{0,32},{16,48},{32,64},{48,80},{64,96},{80,112},{9... | collective-permute-start | bytes 1572872 | tf_op jit(solution)/shard_map/ppermute | solution.py:35
  44.0 6.3 %ln_proj.6 = (bf16[1024,2048]{1,0:T(8,128)(2,1)}, bf16[2,8,128,512]{3,2,1,0:T(8,128)(2,1)}, f32[2,8,128,512]{3,2,1,0:T(8,128)}) custom-call(s32[3]{0:T(128)} %get-tuple-element.185.at_ref, bf16[256,1024]{1,0:T(8,128)(2,1)} %collective-permute-done.3.refs_0_, ...), custom_call_target="tpu_custom_call", output_to_operand_aliasing={{0}: (5, {}), {1}: (6, {}), {2}: (7, {})} | custom-call | flops 805306368 | bytes 9437184 | tf_op jit(solution)/shard_map/ln_proj/pallas_call | solution.py:115
  50.3 4.8 %collective-permute-done.6.refs_0_ = bf16[256,1024]{1,0:T(8,128)(2,1)} collective-permute-done((bf16[256,1024]{1,0:T(8,128)(2,1)}, bf16[256,1024]{1,0:T(8,128)(2,1)}, u32[]{:S(2)}, u32[]{:S(2)}) %collective-permute-start.6) | collective-permute-done | bytes 524320 | tf_op jit(solution)/shard_map/ppermute | solution.py:35
  55.4 3.2 %ln_proj.7 = (bf16[1024,2048]{1,0:T(8,128)(2,1)}, bf16[2,8,128,512]{3,2,1,0:T(8,128)(2,1)}, f32[2,8,128,512]{3,2,1,0:T(8,128)}) custom-call(s32[1]{0:T(128)} %bitcast.5.at_ref, bf16[256,1024]{1,0:T(8,128)(2,1)} %collective-permute-done.6.refs_0_, ...), custom_call_target="tpu_custom_call", output_to_operand_aliasing={{0}: (3, {}), {1}: (4, {}), {2}: (5, {})} | custom-call | flops 268435456 | bytes 3145728 | tf_op jit(solution)/shard_map/ln_proj/pallas_call | solution.py:115
  58.5 6.5 %attention_forward.1 = (f32[128,2048]{1,0:T(8,128)}, bf16[128,2048]{1,0:T(8,128)(2,1)}, bf16[128,2048]{1,0:T(8,128)(2,1)}, f32[4,2048]{1,0:T(4,128)}, s32[1,2048]{1,0:T(1,128)}) custom-call(bf16[2,8,128,512]{3,2,1,0:T(8,128)(2,1)} %get-tuple-element.123.act_ref, bf16[8,272,128]{2,1,0:T(8,128)(2,1)} %copy-done.4), custom_call_target="tpu_custom_call" | custom-call | flops 4294967296 | bytes 6291456 | tf_op jit(solution)/shard_map/attention_forward/pallas_call | solution.py:228
  65.0 1.5 collective-permute-start.11
  66.5 2.7 %collective-permute-done.11 = f32[4,2048]{1,0:T(4,128)S(1)} collective-permute-done((f32[4,2048]{1,0:T(4,128)}, f32[4,2048]{1,0:T(4,128)S(1)}, u32[]{:S(2)}, u32[]{:S(2)}) %collective-permute-start.11) | collective-permute-done | bytes 32800 | tf_op jit(solution)/shard_map/ppermute | solution.py:35
  69.2 0.8 pad_maximum_fusion.2.own_ref
  70.7 1.4 collective-permute-start.13
  72.1 2.0 %collective-permute-start.14 = (f32[2,4,2048]{2,1,0:T(4,128)S(1)}, f32[2,4,2048]{2,1,0:T(4,128)S(1)}, u32[]{:S(2)}, u32[]{:S(2)}) collective-permute-start(f32[2,4,2048]{2,1,0:T(4,128)S(1)} %pad_maximum_fusion.2.own_ref), channel_id=1, source_target_pairs={{64,0},{80,16},{96,32},{112,48},{0,64},{16,80},{32,96},{48,112},{6... | collective-permute-start | bytes 196616 | tf_op jit(solution)/shard_map/ppermute | solution.py:35
  74.4 1.9 %collective-permute-done.13.three_ref = f32[2,4,2048]{2,1,0:T(4,128)S(1)} collective-permute-done((f32[2,4,2048]{2,1,0:T(4,128)S(1)}, f32[2,4,2048]{2,1,0:T(4,128)S(1)}, u32[]{:S(2)}, u32[]{:S(2)}) %collective-permute-start.13) | collective-permute-done | bytes 65568 | tf_op jit(solution)/shard_map/ppermute | solution.py:35
  76.2 2.1 %collective-permute-done.14.two_ref = f32[2,4,2048]{2,1,0:T(4,128)S(1)} collective-permute-done((f32[2,4,2048]{2,1,0:T(4,128)S(1)}, f32[2,4,2048]{2,1,0:T(4,128)S(1)}, u32[]{:S(2)}, u32[]{:S(2)}) %collective-permute-start.14) | collective-permute-done | bytes 65568 | tf_op jit(solution)/shard_map/ppermute | solution.py:35
  78.9 4.2 %mix.1 = (bf16[8,256,256]{2,1,0:T(8,128)(2,1)}, bf16[2048,128]{1,0:T(8,128)(2,1)}, bf16[128,2048]{1,0:T(8,128)(2,1)}) custom-call(f32[2,4,2048]{2,1,0:T(4,128)} %copy-done.15, f32[2,4,2048]{2,1,0:T(4,128)} %copy-done.17, f32[2,4,2048]{2,1,0:T(4,128)} %copy-done.18, f32[2,4,2048]{2,1,0:T(4,128)} %copy-done.19, f32[128,2048]{1,0:T(8,128)} %get-tuple-element.128.att_ref, ...), custom_call_target="tpu_custom_call" | custom-call | flops 5242880 | bytes 6291456 | tf_op jit(solution)/shard_map/mix/pallas_call | solution.py:279
  83.1 2.1 %collective-permute-start.15 = (bf16[256,1024]{1,0:T(8,128)(2,1)S(1)}, bf16[256,1024]{1,0:T(8,128)(2,1)S(1)}, u32[]{:S(2)}, u32[]{:S(2)}) collective-permute-start(bf16[256,1024]{1,0:T(8,128)(2,1)S(1)} %collective-permute-done.9.refs_0_), channel_id=1, source_target_pairs={{32,0},{48,16},{64,32},{80,48},{96,64},{112,80},{0,96},{16,112},{3... | collective-permute-start | bytes 1572872 | tf_op jit(solution)/shard_map/ppermute | solution.py:35
  85.5 1.4 collective-permute-start.16
  86.9 13.4 %attention_backward.1.grad_ref.gated_ref = bf16[8,256,640]{2,1,0:T(8,128)(2,1)} custom-call(bf16[2,8,128,512]{3,2,1,0:T(8,128)(2,1)} %get-tuple-element.123.act_ref, bf16[2048,128]{1,0:T(8,128)(2,1)} %get-tuple-element.138.go_ref, bf16[128,2048]{1,0:T(8,128)(2,1)} %get-tuple-element.139.got_ref, s32[1,2048]{1,0:T(1,128)} %get-tuple-element.140.start_ref, ...), custom_call_target="tpu_custom_call" | custom-call | flops 8053063680 | bytes 10485760 | tf_op jit(solution)/shard_map/attention_backward/pallas_call | solution.py:357
  100.3 0.8 copy-done.14
  101.4 4.3 %all-to-all-start.1 = ((bf16[8,256,640]{2,1,0:T(8,128)(2,1)}), bf16[8,256,640]{2,1,0:T(8,128)(2,1)S(1)}, u32[]{:S(2)}, u32[]{:S(2)}) async-start(bf16[8,256,640]{2,1,0:T(8,128)(2,1)} %attention_backward.1.grad_ref.gated_ref), calls=%async_computation.1 | async-start | bytes 5242880 | tf_op jit(solution)/shard_map/all_to_all | solution.py:667
  105.7 6.5 %terms_in.1 = (f32[8,64,512]{2,1,0:T(8,128)}, f32[8,64,512]{2,1,0:T(8,128)}) custom-call(s32[1]{0:T(128)} %bitcast.4.core_ref, bf16[1024,2048]{1,0:T(8,128)(2,1)} %get-tuple-element.122.normed_ref, bf16[8,256,640]{2,1,0:T(8,128)(2,1)} %attention_backward.1.grad_ref.gated_ref), custom_call_target="tpu_custom_call" | custom-call | flops 2147483648 | bytes 9437184 | tf_op jit(solution)/shard_map/terms_in/pallas_call | solution.py:389
  112.9 3.9 %terms_out.1 = (f32[8,16,512]{2,1,0:T(8,128)}, f32[8,16,512]{2,1,0:T(8,128)}) custom-call(s32[1]{0:T(128)} %bitcast.4.core_ref, s32[8]{0:T(128)} %stack.83.at_ref, bf16[8,256,640]{2,1,0:T(8,128)(2,1)} %attention_backward.1.grad_ref.gated_ref, bf16[256,1024]{1,0:T(8,128)(2,1)} %copy-done.10, bf16[256,1024]{1,0:T(8,128)(2,1)} %copy-done.8, ...), custom_call_target="tpu_custom_call" | custom-call | flops 536870912 | bytes 6291456 | tf_op jit(solution)/shard_map/terms_out/pallas_call | solution.py:434
  117.9 0.8 collective-permute-done.19.got_out_ref
  119.4 2.7 %core_sum.1 = (f32[2,80,512]{2,1,0:T(8,128)}, bf16[2,80,512]{2,1,0:T(8,128)(2,1)}, bf16[2,80,512]{2,1,0:T(8,128)(2,1)}, bf16[2,80,512]{2,1,0:T(8,128)(2,1)}) custom-call(s32[4]{0:T(128)} %pad_add_fusion.pos_ref, f32[8,64,512]{2,1,0:T(8,128)} %get-tuple-element.145.keep_ref, f32[8,64,512]{2,1,0:T(8,128)} %collective-permute-done.18.got_ref, ...), custom_call_target="tpu_custom_call" | custom-call | flops 2621440 | bytes 5242880 | tf_op jit(solution)/shard_map/core_sum/pallas_call | solution.py:452
  122.1 3.0 %collective-permute-start.20 = (bf16[2,80,512]{2,1,0:T(8,128)(2,1)}, bf16[2,80,512]{2,1,0:T(8,128)(2,1)S(1)}, u32[]{:S(2)}, u32[]{:S(2)}) collective-permute-start(bf16[2,80,512]{2,1,0:T(8,128)(2,1)} %get-tuple-element.154), channel_id=1, source_target_pairs={{4,0},{5,1},{6,2},{7,3},{8,4},{9,5},{10,6},{11,7},{12,8},{13,9},{1... | collective-permute-start | bytes 491528 | tf_op jit(solution)/shard_map/ppermute | solution.py:39
  125.1 2.2 %collective-permute-start.22 = (bf16[2,80,512]{2,1,0:T(8,128)(2,1)}, bf16[2,80,512]{2,1,0:T(8,128)(2,1)S(1)}, u32[]{:S(2)}, u32[]{:S(2)}) collective-permute-start(bf16[2,80,512]{2,1,0:T(8,128)(2,1)} %get-tuple-element.156), channel_id=1, source_target_pairs={{8,0},{9,1},{10,2},{11,3},{12,4},{13,5},{14,6},{15,7},{0,8},{1,9},... | collective-permute-start | bytes 491528 | tf_op jit(solution)/shard_map/ppermute | solution.py:39
  127.3 1.2 all-to-all-done.1.gated_ref.grad_ref
  128.6 1.5 copy-done.2
  130.0 6.2 %shard_out.1 = (bf16[256,1024]{1,0:T(8,128)(2,1)}, f32[256,1024]{1,0:T(8,128)}) custom-call(bf16[8,256,640]{2,1,0:T(8,128)(2,1)} %copy-done.2, bf16[8,256,640]{2,1,0:T(8,128)(2,1)} %copy-done.2, bf16[1024,4096]{1,0:T(8,128)(2,1)} %w_in_ref.3, bf16[1024,1024]{1,0:T(8,128)(2,1)} %w_out_ref.1, bf16[256,1024]{1,0:T(8,128)(2,1)} %bitcast.29), custom_call_target="tpu_custom_call" | custom-call | flops 1610612736 | bytes 8388608 | tf_op jit(solution)/shard_map/shard_out/pallas_call | solution.py:552
  136.9 3.1 %collective-permute-start.23 = (f32[48,512]{1,0:T(8,128)S(1)}, f32[48,512]{1,0:T(8,128)S(1)}, u32[]{:S(2)}, u32[]{:S(2)}) collective-permute-start(f32[48,512]{1,0:T(8,128)S(1)} %get-tuple-element.164), channel_id=1, source_target_pairs={{2,0},{3,1},{0,2},{1,3},{6,4},{7,5},{4,6},{5,7},{10,8},{11,9},{8,1... | collective-permute-start | bytes 294920 | tf_op jit(solution)/shard_map/ppermute | solution.py:47
  140.0 1.4 collective-permute-start.24
  141.7 5.5 %shard_grad.1 = bf16[256,1024]{1,0:T(8,128)(2,1)} custom-call(bf16[8,256,640]{2,1,0:T(8,128)(2,1)} %copy-done.2, bf16[1024,4096]{1,0:T(8,128)(2,1)} %w_in_ref.3, bf16[256,1024]{1,0:T(8,128)(2,1)} %bitcast.30, bf16[256,1024]{1,0:T(8,128)(2,1)} %bitcast.34, f32[256,1024]{1,0:T(8,128)} %get-tuple-element.167.half_ref), custom_call_target="tpu_custom_call" | custom-call | flops 1073741824 | bytes 8388608 | tf_op jit(solution)/shard_map/shard_grad/pallas_call | solution.py:575
  147.8 2.7 %collective-permute-start.26 = (f32[16,512]{1,0:T(8,128)S(1)}, f32[16,512]{1,0:T(8,128)S(1)}, u32[]{:S(2)}, u32[]{:S(2)}) collective-permute-start(f32[16,512]{1,0:T(8,128)S(1)} %get-tuple-element.174), channel_id=1, source_target_pairs={{32,0},{48,16},{64,32},{80,48},{96,64},{112,80},{0,96},{16,112},{3... | collective-permute-start | bytes 98312 | tf_op jit(solution)/shard_map/ppermute | solution.py:35
  150.5 2.3 %collective-permute-start.28 = (f32[16,512]{1,0:T(8,128)S(1)}, f32[16,512]{1,0:T(8,128)S(1)}, u32[]{:S(2)}, u32[]{:S(2)}) collective-permute-start(f32[16,512]{1,0:T(8,128)S(1)} %get-tuple-element.176), channel_id=1, source_target_pairs={{64,0},{80,16},{96,32},{112,48},{0,64},{16,80},{32,96},{48,112},{6... | collective-permute-start | bytes 98312 | tf_op jit(solution)/shard_map/ppermute | solution.py:35
  152.9 2.8 %collective-permute-done.27.three_ref = f32[16,512]{1,0:T(8,128)S(1)} collective-permute-done((f32[16,512]{1,0:T(8,128)S(1)}, f32[16,512]{1,0:T(8,128)S(1)}, u32[]{:S(2)}, u32[]{:S(2)}) %collective-permute-start.27) | collective-permute-done | bytes 32800 | tf_op jit(solution)/shard_map/ppermute | solution.py:35
  156.0 1.2 z_place.1
  (84 shorter events, 9.9 us)
Async XLA Ops:
  0.6 14.2 %collective-permute-start = (bf16[256,1024]{1,0:T(8,128)(2,1)}, bf16[256,1024]{1,0:T(8,128)(2,1)S(1)}, u32[]{:S(2)}, u32[]{:S(2)}) collective-permute-start(bf16[256,1024]{1,0:T(8,128)(2,1)} %bitcast.25), channel_id=1, source_target_pairs={{16,0},{0,16},{48,32},{32,48},{80,64},{64,80},{112,96},{96,112},{1... | collective-permute-start | bytes 1572872 | tf_op jit(solution)/shard_map/ppermute | solution.py:35
  2.3 15.3 %collective-permute-start.1 = (bf16[256,1024]{1,0:T(8,128)(2,1)}, bf16[256,1024]{1,0:T(8,128)(2,1)S(1)}, u32[]{:S(2)}, u32[]{:S(2)}) collective-permute-start(bf16[256,1024]{1,0:T(8,128)(2,1)} %bitcast.26), channel_id=1, source_target_pairs={{32,0},{48,16},{64,32},{80,48},{96,64},{112,80},{0,96},{16,112},{3... | collective-permute-start | bytes 1572872 | tf_op jit(solution)/shard_map/ppermute | solution.py:35
  6.3 14.5 %collective-permute-start.2 = (bf16[256,1024]{1,0:T(8,128)(2,1)}, bf16[256,1024]{1,0:T(8,128)(2,1)S(1)}, u32[]{:S(2)}, u32[]{:S(2)}) collective-permute-start(bf16[256,1024]{1,0:T(8,128)(2,1)} %bitcast.27), channel_id=1, source_target_pairs={{96,0},{112,16},{0,32},{16,48},{32,64},{48,80},{64,96},{80,112},{9... | collective-permute-start | bytes 1572872 | tf_op jit(solution)/shard_map/ppermute | solution.py:35
  10.6 12.8 %copy-start.20 = (s32[1,256]{1,0:T(1,128)S(1)}, s32[1,256]{1,0:T(1,128)}, u32[]{:S(2)}) copy-start(s32[1,256]{1,0:T(1,128)} %param.6) | copy-start | bytes 3076
  14.8 13.8 %copy-start.5 = (bf16[256,1024]{1,0:T(8,128)(2,1)}, bf16[256,1024]{1,0:T(8,128)(2,1)S(1)}, u32[]{:S(2)}) copy-start(bf16[256,1024]{1,0:T(8,128)(2,1)S(1)} %collective-permute-done.refs_0_) | copy-start | bytes 1572868
  17.5 11.1 %copy-start.6 = (bf16[256,1024]{1,0:T(8,128)(2,1)}, bf16[256,1024]{1,0:T(8,128)(2,1)S(1)}, u32[]{:S(2)}) copy-start(bf16[256,1024]{1,0:T(8,128)(2,1)S(1)} %collective-permute-done.1.refs_1_) | copy-start | bytes 1572868
  20.8 7.8 %copy-start.7 = (bf16[256,1024]{1,0:T(8,128)(2,1)}, bf16[256,1024]{1,0:T(8,128)(2,1)S(1)}, u32[]{:S(2)}) copy-start(bf16[256,1024]{1,0:T(8,128)(2,1)S(1)} %collective-permute-done.2.refs_2_) | copy-start | bytes 1572868
  20.8 15.0 %collective-permute-start.3 = (bf16[256,1024]{1,0:T(8,128)(2,1)S(1)}, bf16[256,1024]{1,0:T(8,128)(2,1)}, u32[]{:S(2)}, u32[]{:S(2)}) collective-permute-start(bf16[256,1024]{1,0:T(8,128)(2,1)S(1)} %collective-permute-done.1.refs_1_), channel_id=1, source_target_pairs={{16,0},{0,16},{48,32},{32,48},{80,64},{64,80},{112,96},{96,112},{1... | collective-permute-start | bytes 1572872 | tf_op jit(solution)/shard_map/ppermute | solution.py:35
  21.4 17.0 %collective-permute-start.4 = (bf16[256,1024]{1,0:T(8,128)(2,1)S(1)}, bf16[256,1024]{1,0:T(8,128)(2,1)}, u32[]{:S(2)}, u32[]{:S(2)}) collective-permute-start(bf16[256,1024]{1,0:T(8,128)(2,1)S(1)} %collective-permute-done.1.refs_1_), channel_id=1, source_target_pairs={{32,0},{48,16},{64,32},{80,48},{96,64},{112,80},{0,96},{16,112},{3... | collective-permute-start | bytes 1572872 | tf_op jit(solution)/shard_map/ppermute | solution.py:35
  21.7 17.0 %collective-permute-start.5 = (bf16[256,1024]{1,0:T(8,128)(2,1)S(1)}, bf16[256,1024]{1,0:T(8,128)(2,1)}, u32[]{:S(2)}, u32[]{:S(2)}) collective-permute-start(bf16[256,1024]{1,0:T(8,128)(2,1)S(1)} %collective-permute-done.refs_0_), channel_id=1, source_target_pairs={{96,0},{112,16},{0,32},{16,48},{32,64},{48,80},{64,96},{80,112},{9... | collective-permute-start | bytes 1572872 | tf_op jit(solution)/shard_map/ppermute | solution.py:35
  24.9 19.1 %all-to-all-start = ((bf16[8,272,128]{2,1,0:T(8,128)(2,1)}), bf16[8,272,128]{2,1,0:T(8,128)(2,1)S(1)}, u32[]{:S(2)}, u32[]{:S(2)}) async-start(bf16[8,272,128]{2,1,0:T(8,128)(2,1)} %pad_maximum_fusion.1), calls=%async_computation | async-start | bytes 1114112 | tf_op jit(solution)/shard_map/all_to_all | solution.py:636
  28.7 13.2 %copy-start.3 = (bf16[1,256,1024]{2,1,0:T(8,128)(2,1)S(1)}, bf16[1,256,1024]{2,1,0:T(8,128)(2,1)}, u32[]{:S(2)}) copy-start(bf16[1,256,1024]{2,1,0:T(8,128)(2,1)} %param.9) | copy-start | bytes 1572868
  38.7 16.4 %collective-permute-start.6 = (bf16[256,1024]{1,0:T(8,128)(2,1)}, bf16[256,1024]{1,0:T(8,128)(2,1)}, u32[]{:S(2)}, u32[]{:S(2)}) collective-permute-start(bf16[256,1024]{1,0:T(8,128)(2,1)} %collective-permute-done.4.refs_1_), channel_id=1, source_target_pairs={{16,0},{0,16},{48,32},{32,48},{80,64},{64,80},{112,96},{96,112},{1... | collective-permute-start | bytes 1572872 | tf_op jit(solution)/shard_map/ppermute | solution.py:35
  41.9 13.2 %collective-permute-start.7 = (bf16[256,1024]{1,0:T(8,128)(2,1)S(1)}, bf16[256,1024]{1,0:T(8,128)(2,1)S(1)}, u32[]{:S(2)}, u32[]{:S(2)}) collective-permute-start(bf16[256,1024]{1,0:T(8,128)(2,1)S(1)} %bitcast.35), channel_id=1, source_target_pairs={{32,0},{48,16},{64,32},{80,48},{96,64},{112,80},{0,96},{16,112},{3... | collective-permute-start | bytes 1572872 | tf_op jit(solution)/shard_map/ppermute | solution.py:35
  41.9 13.2 %collective-permute-start.8 = (bf16[256,1024]{1,0:T(8,128)(2,1)S(1)}, bf16[256,1024]{1,0:T(8,128)(2,1)S(1)}, u32[]{:S(2)}, u32[]{:S(2)}) collective-permute-start(bf16[256,1024]{1,0:T(8,128)(2,1)S(1)} %bitcast.36), channel_id=1, source_target_pairs={{96,0},{112,16},{0,32},{16,48},{32,64},{48,80},{64,96},{80,112},{9... | collective-permute-start | bytes 1572872 | tf_op jit(solution)/shard_map/ppermute | solution.py:35
  44.0 21.0 %collective-permute-start.9 = (bf16[256,1024]{1,0:T(8,128)(2,1)S(1)}, bf16[256,1024]{1,0:T(8,128)(2,1)S(1)}, u32[]{:S(2)}, u32[]{:S(2)}) collective-permute-start(bf16[256,1024]{1,0:T(8,128)(2,1)S(1)} %bitcast.37), channel_id=1, source_target_pairs={{16,0},{0,16},{48,32},{32,48},{80,64},{64,80},{112,96},{96,112},{1... | collective-permute-start | bytes 1572872 | tf_op jit(solution)/shard_map/ppermute | solution.py:35
  44.0 6.3 %copy-start.4 = (bf16[8,272,128]{2,1,0:T(8,128)(2,1)}, bf16[8,272,128]{2,1,0:T(8,128)(2,1)S(1)}, u32[]{:S(2)}) copy-start(bf16[8,272,128]{2,1,0:T(8,128)(2,1)S(1)} %all-to-all-done.head_ref) | copy-start | bytes 1671172
  55.1 3.4 %copy-start.8 = (bf16[256,1024]{1,0:T(8,128)(2,1)}, bf16[256,1024]{1,0:T(8,128)(2,1)S(1)}, u32[]{:S(2)}) copy-start(bf16[256,1024]{1,0:T(8,128)(2,1)S(1)} %collective-permute-done.7.refs_1_) | copy-start | bytes 1572868
  55.1 3.4 %copy-start.9 = (bf16[256,1024]{1,0:T(8,128)(2,1)}, bf16[256,1024]{1,0:T(8,128)(2,1)S(1)}, u32[]{:S(2)}) copy-start(bf16[256,1024]{1,0:T(8,128)(2,1)S(1)} %collective-permute-done.8.refs_3_) | copy-start | bytes 1572868
  55.1 9.9 %collective-permute-start.10 = (bf16[256,1024]{1,0:T(8,128)(2,1)S(1)}, bf16[256,1024]{1,0:T(8,128)(2,1)S(1)}, u32[]{:S(2)}, u32[]{:S(2)}) collective-permute-start(bf16[256,1024]{1,0:T(8,128)(2,1)S(1)} %collective-permute-done.7.refs_1_), channel_id=1, source_target_pairs={{32,0},{48,16},{64,32},{80,48},{96,64},{112,80},{0,96},{16,112},{3... | collective-permute-start | bytes 1572872 | tf_op jit(solution)/shard_map/ppermute | solution.py:35
  65.0 20.2 %copy-start.10 = (bf16[256,1024]{1,0:T(8,128)(2,1)}, bf16[256,1024]{1,0:T(8,128)(2,1)S(1)}, u32[]{:S(2)}) copy-start(bf16[256,1024]{1,0:T(8,128)(2,1)S(1)} %collective-permute-done.9.refs_0_) | copy-start | bytes 1572868
  65.0 20.5 %copy-start.11 = (bf16[256,1024]{1,0:T(8,128)(2,1)}, bf16[256,1024]{1,0:T(8,128)(2,1)S(1)}, u32[]{:S(2)}) copy-start(bf16[256,1024]{1,0:T(8,128)(2,1)S(1)} %collective-permute-done.10.refs_2_) | copy-start | bytes 1572868
  65.0 4.2 %collective-permute-start.11 = (f32[4,2048]{1,0:T(4,128)}, f32[4,2048]{1,0:T(4,128)S(1)}, u32[]{:S(2)}, u32[]{:S(2)}) collective-permute-start(f32[4,2048]{1,0:T(4,128)} %get-tuple-element.127), channel_id=1, source_target_pairs={{16,0},{0,16},{48,32},{32,48},{80,64},{64,80},{112,96},{96,112},{1... | collective-permute-start | bytes 98312 | tf_op jit(solution)/shard_map/ppermute | solution.py:35
  70.0 8.3 %copy-start.15 = (f32[2,4,2048]{2,1,0:T(4,128)}, f32[2,4,2048]{2,1,0:T(4,128)S(1)}, u32[]{:S(2)}) copy-start(f32[2,4,2048]{2,1,0:T(4,128)S(1)} %pad_maximum_fusion.2.own_ref) | copy-start | bytes 196612
  70.0 4.3 %collective-permute-start.12 = (f32[2,4,2048]{2,1,0:T(4,128)S(1)}, f32[2,4,2048]{2,1,0:T(4,128)S(1)}, u32[]{:S(2)}, u32[]{:S(2)}) collective-permute-start(f32[2,4,2048]{2,1,0:T(4,128)S(1)} %pad_maximum_fusion.2.own_ref), channel_id=1, source_target_pairs={{32,0},{48,16},{64,32},{80,48},{96,64},{112,80},{0,96},{16,112},{3... | collective-permute-start | bytes 196616 | tf_op jit(solution)/shard_map/ppermute | solution.py:35
  70.7 5.5 %collective-permute-start.13 = (f32[2,4,2048]{2,1,0:T(4,128)S(1)}, f32[2,4,2048]{2,1,0:T(4,128)S(1)}, u32[]{:S(2)}, u32[]{:S(2)}) collective-permute-start(f32[2,4,2048]{2,1,0:T(4,128)S(1)} %pad_maximum_fusion.2.own_ref), channel_id=1, source_target_pairs={{96,0},{112,16},{0,32},{16,48},{32,64},{48,80},{64,96},{80,112},{9... | collective-permute-start | bytes 196616 | tf_op jit(solution)/shard_map/ppermute | solution.py:35
  72.1 6.2 %collective-permute-start.14 = (f32[2,4,2048]{2,1,0:T(4,128)S(1)}, f32[2,4,2048]{2,1,0:T(4,128)S(1)}, u32[]{:S(2)}, u32[]{:S(2)}) collective-permute-start(f32[2,4,2048]{2,1,0:T(4,128)S(1)} %pad_maximum_fusion.2.own_ref), channel_id=1, source_target_pairs={{64,0},{80,16},{96,32},{112,48},{0,64},{16,80},{32,96},{48,112},{6... | collective-permute-start | bytes 196616 | tf_op jit(solution)/shard_map/ppermute | solution.py:35
  74.4 3.9 %copy-start.17 = (f32[2,4,2048]{2,1,0:T(4,128)}, f32[2,4,2048]{2,1,0:T(4,128)S(1)}, u32[]{:S(2)}) copy-start(f32[2,4,2048]{2,1,0:T(4,128)S(1)} %collective-permute-done.12.one_ref) | copy-start | bytes 196612
  76.2 2.1 %copy-start.18 = (f32[2,4,2048]{2,1,0:T(4,128)}, f32[2,4,2048]{2,1,0:T(4,128)S(1)}, u32[]{:S(2)}) copy-start(f32[2,4,2048]{2,1,0:T(4,128)S(1)} %collective-permute-done.13.three_ref) | copy-start | bytes 196612
  83.1 17.2 %collective-permute-start.15 = (bf16[256,1024]{1,0:T(8,128)(2,1)S(1)}, bf16[256,1024]{1,0:T(8,128)(2,1)S(1)}, u32[]{:S(2)}, u32[]{:S(2)}) collective-permute-start(bf16[256,1024]{1,0:T(8,128)(2,1)S(1)} %collective-permute-done.9.refs_0_), channel_id=1, source_target_pairs={{32,0},{48,16},{64,32},{80,48},{96,64},{112,80},{0,96},{16,112},{3... | collective-permute-start | bytes 1572872 | tf_op jit(solution)/shard_map/ppermute | solution.py:35
  85.2 15.1 %collective-permute-start.17 = (bf16[256,1024]{1,0:T(8,128)(2,1)S(1)}, bf16[256,1024]{1,0:T(8,128)(2,1)S(1)}, u32[]{:S(2)}, u32[]{:S(2)}) collective-permute-start(bf16[256,1024]{1,0:T(8,128)(2,1)S(1)} %collective-permute-done.9.refs_0_), channel_id=1, source_target_pairs={{96,0},{112,16},{0,32},{16,48},{32,64},{48,80},{64,96},{80,112},{9... | collective-permute-start | bytes 1572872 | tf_op jit(solution)/shard_map/ppermute | solution.py:35
  85.5 14.8 %collective-permute-start.16 = (bf16[256,1024]{1,0:T(8,128)(2,1)S(1)}, bf16[256,1024]{1,0:T(8,128)(2,1)S(1)}, u32[]{:S(2)}, u32[]{:S(2)}) collective-permute-start(bf16[256,1024]{1,0:T(8,128)(2,1)S(1)} %collective-permute-done.10.refs_2_), channel_id=1, source_target_pairs={{16,0},{0,16},{48,32},{32,48},{80,64},{64,80},{112,96},{96,112},{1... | collective-permute-start | bytes 1572872 | tf_op jit(solution)/shard_map/ppermute | solution.py:35
  100.3 1.1 copy-start.12
  101.4 27.1 %all-to-all-start.1 = ((bf16[8,256,640]{2,1,0:T(8,128)(2,1)}), bf16[8,256,640]{2,1,0:T(8,128)(2,1)S(1)}, u32[]{:S(2)}, u32[]{:S(2)}) async-start(bf16[8,256,640]{2,1,0:T(8,128)(2,1)} %attention_backward.1.grad_ref.gated_ref), calls=%async_computation.1 | async-start | bytes 5242880 | tf_op jit(solution)/shard_map/all_to_all | solution.py:667
  112.3 6.4 %collective-permute-start.18 = (f32[8,64,512]{2,1,0:T(8,128)}, f32[8,64,512]{2,1,0:T(8,128)}, u32[]{:S(2)}, u32[]{:S(2)}) collective-permute-start(f32[8,64,512]{2,1,0:T(8,128)} %get-tuple-element.146), channel_id=1, source_target_pairs={{1,0},{0,1},{3,2},{2,3},{5,4},{4,5},{7,6},{6,7},{9,8},{8,9},{11,10... | collective-permute-start | bytes 3145736 | tf_op jit(solution)/shard_map/ppermute | solution.py:39
  116.7 2.0 %collective-permute-start.19 = (f32[8,16,512]{2,1,0:T(8,128)}, f32[8,16,512]{2,1,0:T(8,128)S(1)}, u32[]{:S(2)}, u32[]{:S(2)}) collective-permute-start(f32[8,16,512]{2,1,0:T(8,128)} %get-tuple-element.153), channel_id=1, source_target_pairs={{1,0},{0,1},{3,2},{2,3},{5,4},{4,5},{7,6},{6,7},{9,8},{8,9},{11,10... | collective-permute-start | bytes 786440 | tf_op jit(solution)/shard_map/ppermute | solution.py:39
  122.1 14.1 %collective-permute-start.20 = (bf16[2,80,512]{2,1,0:T(8,128)(2,1)}, bf16[2,80,512]{2,1,0:T(8,128)(2,1)S(1)}, u32[]{:S(2)}, u32[]{:S(2)}) collective-permute-start(bf16[2,80,512]{2,1,0:T(8,128)(2,1)} %get-tuple-element.154), channel_id=1, source_target_pairs={{4,0},{5,1},{6,2},{7,3},{8,4},{9,5},{10,6},{11,7},{12,8},{13,9},{1... | collective-permute-start | bytes 491528 | tf_op jit(solution)/shard_map/ppermute | solution.py:39
  125.1 11.1 %collective-permute-start.21 = (bf16[2,80,512]{2,1,0:T(8,128)(2,1)}, bf16[2,80,512]{2,1,0:T(8,128)(2,1)S(1)}, u32[]{:S(2)}, u32[]{:S(2)}) collective-permute-start(bf16[2,80,512]{2,1,0:T(8,128)(2,1)} %get-tuple-element.155), channel_id=1, source_target_pairs={{12,0},{13,1},{14,2},{15,3},{0,4},{1,5},{2,6},{3,7},{4,8},{5,9},{6... | collective-permute-start | bytes 491528 | tf_op jit(solution)/shard_map/ppermute | solution.py:39
  125.1 11.1 %copy-start = (f32[2,80,512]{2,1,0:T(8,128)S(1)}, f32[2,80,512]{2,1,0:T(8,128)}, u32[]{:S(2)}) copy-start(f32[2,80,512]{2,1,0:T(8,128)} %get-tuple-element.160.own_ref) | copy-start | bytes 983044
  125.1 11.1 %copy-start.1 = (s32[4]{0:T(128)S(1)}, s32[4]{0:T(128)}, u32[]{:S(2)}) copy-start(s32[4]{0:T(128)} %pad_add_fusion.pos_ref) | copy-start | bytes 52
  125.1 11.1 %collective-permute-start.22 = (bf16[2,80,512]{2,1,0:T(8,128)(2,1)}, bf16[2,80,512]{2,1,0:T(8,128)(2,1)S(1)}, u32[]{:S(2)}, u32[]{:S(2)}) collective-permute-start(bf16[2,80,512]{2,1,0:T(8,128)(2,1)} %get-tuple-element.156), channel_id=1, source_target_pairs={{8,0},{9,1},{10,2},{11,3},{12,4},{13,5},{14,6},{15,7},{0,8},{1,9},... | collective-permute-start | bytes 491528 | tf_op jit(solution)/shard_map/ppermute | solution.py:39
  128.6 1.5 copy-start.2
  136.9 10.3 %collective-permute-start.23 = (f32[48,512]{1,0:T(8,128)S(1)}, f32[48,512]{1,0:T(8,128)S(1)}, u32[]{:S(2)}, u32[]{:S(2)}) collective-permute-start(f32[48,512]{1,0:T(8,128)S(1)} %get-tuple-element.164), channel_id=1, source_target_pairs={{2,0},{3,1},{0,2},{1,3},{6,4},{7,5},{4,6},{5,7},{10,8},{11,9},{8,1... | collective-permute-start | bytes 294920 | tf_op jit(solution)/shard_map/ppermute | solution.py:47
  140.0 7.2 %collective-permute-start.24 = (f32[32,512]{1,0:T(8,128)S(1)}, f32[32,512]{1,0:T(8,128)S(1)}, u32[]{:S(2)}, u32[]{:S(2)}) collective-permute-start(f32[32,512]{1,0:T(8,128)S(1)} %get-tuple-element.165), channel_id=1, source_target_pairs={{16,0},{17,1},{18,2},{19,3},{20,4},{21,5},{22,6},{23,7},{24,8},{25... | collective-permute-start | bytes 196616 | tf_op jit(solution)/shard_map/ppermute | solution.py:47
  141.4 5.8 %collective-permute-start.25 = (f32[32,512]{1,0:T(8,128)S(1)}, f32[32,512]{1,0:T(8,128)S(1)}, u32[]{:S(2)}, u32[]{:S(2)}) collective-permute-start(f32[32,512]{1,0:T(8,128)S(1)} %get-tuple-element.166), channel_id=1, source_target_pairs={{18,0},{19,1},{16,2},{17,3},{22,4},{23,5},{20,6},{21,7},{26,8},{27... | collective-permute-start | bytes 196616 | tf_op jit(solution)/shard_map/ppermute | solution.py:47
  147.8 5.1 %collective-permute-start.26 = (f32[16,512]{1,0:T(8,128)S(1)}, f32[16,512]{1,0:T(8,128)S(1)}, u32[]{:S(2)}, u32[]{:S(2)}) collective-permute-start(f32[16,512]{1,0:T(8,128)S(1)} %get-tuple-element.174), channel_id=1, source_target_pairs={{32,0},{48,16},{64,32},{80,48},{96,64},{112,80},{0,96},{16,112},{3... | collective-permute-start | bytes 98312 | tf_op jit(solution)/shard_map/ppermute | solution.py:35
  150.5 5.1 %collective-permute-start.27 = (f32[16,512]{1,0:T(8,128)S(1)}, f32[16,512]{1,0:T(8,128)S(1)}, u32[]{:S(2)}, u32[]{:S(2)}) collective-permute-start(f32[16,512]{1,0:T(8,128)S(1)} %get-tuple-element.175), channel_id=1, source_target_pairs={{96,0},{112,16},{0,32},{16,48},{32,64},{48,80},{64,96},{80,112},{9... | collective-permute-start | bytes 98312 | tf_op jit(solution)/shard_map/ppermute | solution.py:35
  150.5 5.5 %collective-permute-start.28 = (f32[16,512]{1,0:T(8,128)S(1)}, f32[16,512]{1,0:T(8,128)S(1)}, u32[]{:S(2)}, u32[]{:S(2)}) collective-permute-start(f32[16,512]{1,0:T(8,128)S(1)} %get-tuple-element.176), channel_id=1, source_target_pairs={{64,0},{80,16},{96,32},{112,48},{0,64},{16,80},{32,96},{48,112},{6... | collective-permute-start | bytes 98312 | tf_op jit(solution)/shard_map/ppermute | solution.py:35
  (4 other events, 3.2 us)
where the time goes:
time: 158 us; the launch traced here: 157 us
  Pallas kernels  70.3 us (44%)
  starting transfers between devices  46.9 us (30%)
  waiting for transfers between devices  26.4 us (17%)
  local copies, waits for them, and re-layouts  6.32 us (4%)
  other arithmetic  3.92 us (2%)
  matrix products  2.51 us (2%)
    ppermute x21, starting transfers between devices, from_seq(): return lax.ppermute(a, 'seq', seq_perm(dz, dx))  28.3 us
    ppermute x21, waiting for transfers between devices, from_seq(): return lax.ppermute(a, 'seq', seq_perm(dz, dx))  24.4 us
    pallas_call x4, Pallas kernels, ln_proj(): pl.pallas_call(functools.partial(ln_proj_kernel, len(blocks)), grid_spec=...  19 us
    pallas_call x1, Pallas kernels, backward(): pl.pallas_call(backward_kernel, in_specs=[vmem()] * 5 + [pl.BlockSpec(mem...  13.4 us
    pallas_call x1, Pallas kernels, terms_in(): pl.pallas_call(terms_in_kernel, grid=(4,), in_specs=[smem(), pl.BlockSpec...  6.53 us
    pallas_call x1, Pallas kernels, forward(): pl.pallas_call(forward_kernel, in_specs=[vmem()] * 2, out_specs=[vmem()]...  6.46 us
    pallas_call x1, Pallas kernels, shard_out(): pl.pallas_call(shard_out_kernel, grid=(2,), in_specs=[pl.BlockSpec((H, ro...  6.18 us
    ppermute x5, starting transfers between devices, from_user(): return lax.ppermute(a, 'user', user_perm(dy, dh, dc))  5.83 us
  transfers between devices with their start and end apart: 31, of which 14 were waited for; matrix products, arithmetic and copies ran while one was open for 5% of the time, Pallas kernels for 40%

commit v1 on v0

--- a/solution.py
+++ b/solution.py
@@ -244,10 +244,11 @@
     )(act, at_head)
 
 
-def mix_kernel(own_ref, one_ref, three_ref, two_ref, att_ref, gate_ref, gg_ref, slope_ref, early_ref, go_ref, got_ref):
+def backward_kernel(own_ref, one_ref, three_ref, two_ref, act_ref, att_ref, gate_ref, gg_ref, start_ref, slope_hbm, back_ref, dk_ref, dv_ref, slope_ref, sem):
     length = att_ref.shape[1]
     width = H * HD
-    tile = 2 * HD
+    copy = pltpu.make_async_copy(slope_hbm, slope_ref, sem)
+    copy.start()
     heads = [ref[k] for ref in (own_ref, one_ref, three_ref, two_ref) for k in range(NX)]
     mean_all = sum(a[0:1] for a in heads) * (1.0 / H)
     apart = [a[0:1] - mean_all for a in heads]
@@ -255,70 +256,34 @@
     inverse_all = lax.rsqrt(spread * (1.0 / width) + EPS)
     first_all = sum(a[2:3] for a in heads) * (1.0 / width)
     second_all = inverse_all * sum(a[3:4] + d * a[2:3] for a, d in zip(heads, apart)) * (1.0 / width)
-    for i in range(0, length, tile):
-        at = slice(i, i + tile)
+
+    keys = [time_rows(act_ref, j, BK, 3) for j in range(0, length, BK)]
+    keys_t = [k.T for k in keys]
+    values = [time_rows(act_ref, j, BK, 1) for j in range(0, length, BK)]
+    queries_in, seen = tiles(length, BQ, BK)
+
+    def put(first, column, value):
+        value = value.astype(BF16)
+        for k in range(value.shape[0] // HD):
+            shard, row = tile_place(first // HD + k)
+            back_ref[shard, row : row + HD, column * HD : (column + 1) * HD] = value[
+                k * HD : (k + 1) * HD
+            ]
+
+    def put_grad(first, column, value):
+        put(first, column, value * time_rows(slope_ref, first, value.shape[0], column))
+
+    started = set()
+    for i, keys_in in queries_in:
+        at = slice(i, i + BQ)
         gate = gate_ref[:, at].astype(F32)
         gg = gg_ref[:, at].astype(F32)
         inverse = inverse_all[:, at]
         mixed = (att_ref[:, at] - mean_all[:, at]) * inverse
         grad_att = inverse * (gg * gate - first_all[:, at] - mixed * second_all[:, at])
-        got_ref[:, at] = grad_att.astype(BF16)
-        go_ref[at, :] = grad_att.T.astype(BF16)
-        gated = (mixed * gate).astype(BF16).T
-        grad_u = ((gg * mixed).T * time_rows(slope_ref, i, tile, 0)).astype(BF16)
-        for k in range(2):
-            shard, row = tile_place(i // HD + k)
-            early_ref[shard, row : row + HD, :HD] = gated[k * HD : (k + 1) * HD]
-            early_ref[shard, row : row + HD, HD:] = grad_u[k * HD : (k + 1) * HD]
-
-
-def mix(own, one, three, two, att, gate, gg, slope):
-    length = att.shape[1]
-    shards = NZ * NX
-    whole = lambda shape: pl.BlockSpec(shape, lambda i: (0,) * len(shape))
-    return pl.pallas_call(
-        mix_kernel,
-        grid=(1,),
-        in_specs=[whole(own.shape)] * 4
-        + [whole(att.shape)] * 3
-        + [pl.BlockSpec(slope.shape[:3] + (HD,), lambda i: (0, 0, 0, 0))],
-        out_specs=[whole((shards, length // shards, 2 * HD)), whole((length, HD)), whole((HD, length))],
-        out_shape=(
-            jax.ShapeDtypeStruct((shards, length // shards, 2 * HD), BF16),
-            jax.ShapeDtypeStruct((length, HD), BF16),
-            jax.ShapeDtypeStruct((HD, length), BF16),
-        ),
-        compiler_params=params(LIMIT),
-        cost_estimate=pl.CostEstimate(flops=20 * HD * length, bytes_accessed=6 << 20, transcendentals=0),
-        name="mix",
-    )(own, one, three, two, att, gate, gg, slope)
-
-
-def backward_kernel(act_ref, go_ref, got_ref, start_ref, early_ref, slope_hbm, back_ref, dk_ref, dv_ref, slope_ref, sem):
-    length = go_ref.shape[0]
-    copy = pltpu.make_async_copy(slope_hbm, slope_ref, sem)
-    copy.start()
-    back_ref[:, :, :HD] = early_ref[:, :, HD:]
-    back_ref[:, :, 4 * HD :] = early_ref[:, :, :HD]
-    keys = [time_rows(act_ref, j, BK, 3) for j in range(0, length, BK)]
-    keys_t = [k.T for k in keys]
-    values = [time_rows(act_ref, j, BK, 1) for j in range(0, length, BK)]
-    queries_in, seen = tiles(length, BQ, BK)
-
-    def put(first, column, value):
-        value = (value * time_rows(slope_ref, first, value.shape[0], column)).astype(BF16)
-        for k in range(value.shape[0] // HD):
-            shard, row = tile_place(first // HD + k)
-            back_ref[shard, row : row + HD, column * HD : (column + 1) * HD] = value[
-                k * HD : (k + 1) * HD
-            ]
-
-    started = set()
-    for i, keys_in in queries_in:
-        at = slice(i, i + BQ)
+        grad_out_t = grad_att.astype(BF16)
+        grad_out = grad_out_t.T
         queries = time_rows(act_ref, i, BQ, 2)
-        grad_out = go_ref[at, :]
-        grad_out_t = got_ref[:, at]
         start = start_ref[:, at]
         total = None
         for j in keys_in:
@@ -345,18 +310,20 @@
             total = term if total is None else total + term
         if i == 0:
             copy.wait()
-        put(i, 2, total.T * SCALE)
+        put(i, 4, (mixed * gate).astype(BF16).T)
+        put_grad(i, 0, (gg * mixed).T)
+        put_grad(i, 2, total.T * SCALE)
     for j in range(0, length, BK):
-        put(j, 1, dv_ref[j : j + BK, :])
-        put(j, 3, dk_ref[j : j + BK, :] * SCALE)
-
-
-def backward(act, grad_out, grad_out_t, start, early, slope):
+        put_grad(j, 1, dv_ref[j : j + BK, :])
+        put_grad(j, 3, dk_ref[j : j + BK, :] * SCALE)
+
+
+def backward(stats, act, att, gate, gg, start, slope):
     length = start.shape[1]
     shards = NZ * NX
     return pl.pallas_call(
         backward_kernel,
-        in_specs=[vmem()] * 5 + [pl.BlockSpec(memory_space=pl.ANY)],
+        in_specs=[vmem()] * 9 + [pl.BlockSpec(memory_space=pl.ANY)],
         out_specs=vmem(),
         out_shape=jax.ShapeDtypeStruct((shards, length // shards, 5 * HD), BF16),
         scratch_shapes=[pltpu.VMEM((length, HD), F32)] * 2
@@ -366,7 +333,7 @@
             flops=15 * HD * length * length, bytes_accessed=10 << 20, transcendentals=length * length // 2
         ),
         name="attention_backward",
-    )(act, grad_out, grad_out_t, start, early, slope)
+    )(*stats, act, att, gate, gg, start, slope)
 
 
 def terms_in_kernel(core_ref, normed_ref, grad_ref, keep_ref, send_ref, res_ref):
@@ -612,9 +579,20 @@
     def place_of(key):
         return ((z + key[0]) % NZ) * NX + (x ^ key[1])
 
+    at_core = core.reshape(1)
+    at = jnp.stack([y, xh, x, z])
+    orders = (
+        ((0, 0),),
+        ((0, 1), (1, 0), (3, 0)),
+        ((1, 1), (2, 0), (3, 1)),
+        ((2, 1),),
+        ((1, 0), (3, 0), (0, 1), (2, 0), (2, 1), (1, 1), (3, 1), (0, 0)),
+    )
+    places = {keys: jnp.stack([place_of(key) for key in keys]) for keys in orders}
+
     def project(got, outs):
-        at = jnp.stack([place_of(key) for key in got])
-        return ln_proj(at, list(got.values()), w_head, outs)
+        keys = tuple(sorted(got))
+        return ln_proj(places[keys], [got[key] for key in keys], w_head, outs)
 
     got = {
         (1, 0): from_seq(hist, 1, 0),
@@ -623,7 +601,10 @@
     }
     outs = project({(0, 0): hist}, ())
     grad_gated_own = dot_nt(cot, w_out).astype(BF16).reshape(rows, H, HD).transpose(1, 0, 2)
-    got, outs, grad_gated_own = tie((got, outs, grad_gated_own))
+    got, outs, grad_gated_own, waiting, at_core, at = tie(
+        (got, outs, grad_gated_own, tuple(places.values()), at_core, at)
+    )
+    places = dict(zip(orders, waiting))
     ids = segment_ids[0].astype(BF16).reshape(2, HD)
     ids = jnp.pad(ids, ((0, 14), (0, 0)))
     to_heads = jnp.concatenate(
@@ -653,26 +634,22 @@
     cots.update(fresh)
     pair = jnp.stack([stats, from_seq(stats, 0, 1)])
     others = [from_seq(pair, dz, 0) for dz in (1, 3, 2)]
-    early, grad_out, grad_out_t = mix(pair, *others, att, gate_t, gg_t, slope)
-    early, grad_out, grad_out_t, cots = tie((early, grad_out, grad_out_t, cots))
+    pair, others, cots = tie((pair, others, cots))
     fresh = {
         (2, 1): from_seq(cots[2, 0], 0, 1),
         (1, 1): from_seq(cots[0, 1], 1, 0),
         (3, 1): from_seq(cots[0, 1], 3, 0),
     }
-    back = backward(act, grad_out, grad_out_t, start, early, slope)
+    back = backward([pair, *others], act, att, gate_t, gg_t, start, slope)
     back, fresh = tie((back, fresh))
     cots.update(fresh)
     cots[0, 0] = cot
     back_tok = lax.all_to_all(back, "seq", 0, 0, tiled=True)
 
-    at_core = core.reshape(1)
     keep, send = terms_in(at_core, normed_t, back)
-    places = jnp.stack([place_of(key) for key in cots])
     got = from_user(send, 0, 0, 1)
-    keep_out, send_out = terms_out(at_core, places, back, list(cots.values()))
+    keep_out, send_out = terms_out(at_core, places[orders[4]], back, [cots[key] for key in orders[4]])
     got_out = from_user(send_out, 0, 0, 1)
-    at = jnp.stack([y, xh, x, z])
     n = 4 * HD
     own, *sends = small(
         core_sum_kernel,

time: 158 us -> 152 us (0.962)
  Pallas kernels: 70.3 us -> 65.7 us
    pallas_call x2 -> x1, Pallas kernels: 17.5 us -> 13 us  [backward(): pl.pallas_call(backward_kernel, in_specs=[vmem()] * 9 + [pl.BlockSpec(mem...]
  transfers between devices with their start and end apart: 31 -> 31, of which waited for: 14 -> 14; matrix products, arithmetic and copies ran while one was open for 5% -> 5% of each run, Pallas kernels for 40% -> 42%
where the time goes in v1:
time: 152 us
  Pallas kernels  65.7 us (43%)
  starting transfers between devices  46.2 us (30%)
  waiting for transfers between devices  26.6 us (18%)
  local copies, waits for them, and re-layouts  5.99 us (4%)
  other arithmetic  3.9 us (3%)
  matrix products  2.51 us (2%)
    ppermute x21, starting transfers between devices, from_seq(): return lax.ppermute(a, 'seq', seq_perm(dz, dx))  27.8 us
    ppermute x21, waiting for transfers between devices, from_seq(): return lax.ppermute(a, 'seq', seq_perm(dz, dx))  23.7 us
    pallas_call x4, Pallas kernels, ln_proj(): pl.pallas_call(functools.partial(ln_proj_kernel, len(blocks)), grid_spec=...  19 us
    pallas_call x1, Pallas kernels, backward(): pl.pallas_call(backward_kernel, in_specs=[vmem()] * 9 + [pl.BlockSpec(mem...  13 us
    pallas_call x1, Pallas kernels, terms_in(): pl.pallas_call(terms_in_kernel, grid=(4,), in_specs=[smem(), pl.BlockSpec...  6.5 us
    pallas_call x1, Pallas kernels, forward(): pl.pallas_call(forward_kernel, in_specs=[vmem()] * 2, out_specs=[vmem()]...  6.49 us
    pallas_call x1, Pallas kernels, shard_out(): pl.pallas_call(shard_out_kernel, grid=(2,), in_specs=[pl.BlockSpec((H, ro...  6.16 us
    ppermute x5, starting transfers between devices, from_user(): return lax.ppermute(a, 'user', user_perm(dy, dh, dc))  5.84 us
  transfers between devices with their start and end apart: 31, of which 14 were waited for; matrix products, arithmetic and copies ran while one was open for 5% of the time, Pallas kernels for 42%

profile of v1, /device:TPU:0, one launch (start us, length us, event | category | flops | bytes accessed | tf_op | source)
XLA Modules:
  0.0 151.8 jit_solution(6939826247835418323)
XLA Ops:
  0.6 1.7 %collective-permute-start = (bf16[256,1024]{1,0:T(8,128)(2,1)}, bf16[256,1024]{1,0:T(8,128)(2,1)S(1)}, u32[]{:S(2)}, u32[]{:S(2)}) collective-permute-start(bf16[256,1024]{1,0:T(8,128)(2,1)} %bitcast.25), channel_id=1, source_target_pairs={{16,0},{0,16},{48,32},{32,48},{80,64},{64,80},{112,96},{96,112},{1... | collective-permute-start | bytes 1572872 | tf_op jit(solution)/shard_map/ppermute | solution.py:35
  2.3 4.0 %collective-permute-start.1 = (bf16[256,1024]{1,0:T(8,128)(2,1)}, bf16[256,1024]{1,0:T(8,128)(2,1)S(1)}, u32[]{:S(2)}, u32[]{:S(2)}) collective-permute-start(bf16[256,1024]{1,0:T(8,128)(2,1)} %bitcast.26), channel_id=1, source_target_pairs={{32,0},{48,16},{64,32},{80,48},{96,64},{112,80},{0,96},{16,112},{3... | collective-permute-start | bytes 1572872 | tf_op jit(solution)/shard_map/ppermute | solution.py:35
  6.3 2.5 %convolution_convert_fusion = bf16[256,1024]{1,0:T(8,128)(2,1)S(1)} fusion(bf16[1024,1024]{1,0:T(8,128)(2,1)} %w_out_ref.1, bf16[1,256,1024]{2,1,0:T(8,128)(2,1)} %param.9), kind=kOutput, calls=%fused_computation | convolution fusion | flops 537133056 | bytes 3145728 | tf_op jit(solution)/shard_map/dot_general | solution.py:68
  10.0 1.3 constant_dynamic-slice_fusion.3
  11.3 1.1 pad_maximum_fusion.refs_1_.refs_3_
  12.4 3.1 %ln_proj.4 = (bf16[1024,2048]{1,0:T(8,128)(2,1)}, bf16[2,8,128,512]{3,2,1,0:T(8,128)(2,1)}, f32[2,8,128,512]{3,2,1,0:T(8,128)}) custom-call(s32[1]{0:T(128)} %bitcast.1.at_ref, bf16[256,1024]{1,0:T(8,128)(2,1)} %bitcast.28, bf16[1024,512]{1,0:T(8,128)(2,1)} %pad_maximum_fusion.refs_1_.refs_3_), custom_call_target="tpu_custom_call" | custom-call | flops 268435456 | bytes 3145728 | tf_op jit(solution)/shard_map/ln_proj/pallas_call | solution.py:115
  16.7 0.9 collective-permute-done.1.refs_1_
  17.5 3.3 %collective-permute-done.2.refs_2_ = bf16[256,1024]{1,0:T(8,128)(2,1)S(1)} collective-permute-done((bf16[256,1024]{1,0:T(8,128)(2,1)}, bf16[256,1024]{1,0:T(8,128)(2,1)S(1)}, u32[]{:S(2)}, u32[]{:S(2)}) %collective-permute-start.2) | collective-permute-done | bytes 524320 | tf_op jit(solution)/shard_map/ppermute | solution.py:35
  21.7 1.7 %collective-permute-start.5 = (bf16[256,1024]{1,0:T(8,128)(2,1)S(1)}, bf16[256,1024]{1,0:T(8,128)(2,1)}, u32[]{:S(2)}, u32[]{:S(2)}) collective-permute-start(bf16[256,1024]{1,0:T(8,128)(2,1)S(1)} %collective-permute-done.refs_0_), channel_id=1, source_target_pairs={{96,0},{112,16},{0,32},{16,48},{32,64},{48,80},{64,96},{80,112},{9... | collective-permute-start | bytes 1572872 | tf_op jit(solution)/shard_map/ppermute | solution.py:35
  23.5 0.9 pad_maximum_fusion.1
  24.3 3.8 %all-to-all-start = ((bf16[8,272,128]{2,1,0:T(8,128)(2,1)}), bf16[8,272,128]{2,1,0:T(8,128)(2,1)S(1)}, u32[]{:S(2)}, u32[]{:S(2)}) async-start(bf16[8,272,128]{2,1,0:T(8,128)(2,1)} %pad_maximum_fusion.1), calls=%async_computation | async-start | bytes 1114112 | tf_op jit(solution)/shard_map/all_to_all | solution.py:617
  28.1 6.4 %ln_proj.5 = (bf16[1024,2048]{1,0:T(8,128)(2,1)}, bf16[2,8,128,512]{3,2,1,0:T(8,128)(2,1)}, f32[2,8,128,512]{3,2,1,0:T(8,128)}) custom-call(s32[3]{0:T(128)} %get-tuple-element.104.at_ref, bf16[256,1024]{1,0:T(8,128)(2,1)} %copy-done.6, bf16[256,1024]{1,0:T(8,128)(2,1)} %copy-done.7, ...), custom_call_target="tpu_custom_call", output_to_operand_aliasing={{0}: (5, {}), {1}: (6, {}), {2}: (7, {})} | custom-call | flops 805306368 | bytes 9437184 | tf_op jit(solution)/shard_map/ln_proj/pallas_call | solution.py:115
  34.6 1.3 collective-permute-done.3.refs_0_
  35.8 2.5 %collective-permute-done.4.refs_1_ = bf16[256,1024]{1,0:T(8,128)(2,1)} collective-permute-done((bf16[256,1024]{1,0:T(8,128)(2,1)S(1)}, bf16[256,1024]{1,0:T(8,128)(2,1)}, u32[]{:S(2)}, u32[]{:S(2)}) %collective-permute-start.4) | collective-permute-done | bytes 524320 | tf_op jit(solution)/shard_map/ppermute | solution.py:35
  38.7 3.2 %collective-permute-start.6 = (bf16[256,1024]{1,0:T(8,128)(2,1)}, bf16[256,1024]{1,0:T(8,128)(2,1)}, u32[]{:S(2)}, u32[]{:S(2)}) collective-permute-start(bf16[256,1024]{1,0:T(8,128)(2,1)} %collective-permute-done.4.refs_1_), channel_id=1, source_target_pairs={{16,0},{0,16},{48,32},{32,48},{80,64},{64,80},{112,96},{96,112},{1... | collective-permute-start | bytes 1572872 | tf_op jit(solution)/shard_map/ppermute | solution.py:35
  41.9 2.0 %collective-permute-start.8 = (bf16[256,1024]{1,0:T(8,128)(2,1)S(1)}, bf16[256,1024]{1,0:T(8,128)(2,1)S(1)}, u32[]{:S(2)}, u32[]{:S(2)}) collective-permute-start(bf16[256,1024]{1,0:T(8,128)(2,1)S(1)} %bitcast.36), channel_id=1, source_target_pairs={{96,0},{112,16},{0,32},{16,48},{32,64},{48,80},{64,96},{80,112},{9... | collective-permute-start | bytes 1572872 | tf_op jit(solution)/shard_map/ppermute | solution.py:35
  44.0 6.3 %ln_proj.6 = (bf16[1024,2048]{1,0:T(8,128)(2,1)}, bf16[2,8,128,512]{3,2,1,0:T(8,128)(2,1)}, f32[2,8,128,512]{3,2,1,0:T(8,128)}) custom-call(s32[3]{0:T(128)} %get-tuple-element.114.at_ref, bf16[256,1024]{1,0:T(8,128)(2,1)} %collective-permute-done.3.refs_0_, ...), custom_call_target="tpu_custom_call", output_to_operand_aliasing={{0}: (5, {}), {1}: (6, {}), {2}: (7, {})} | custom-call | flops 805306368 | bytes 9437184 | tf_op jit(solution)/shard_map/ln_proj/pallas_call | solution.py:115
  50.2 4.8 %collective-permute-done.6.refs_0_ = bf16[256,1024]{1,0:T(8,128)(2,1)} collective-permute-done((bf16[256,1024]{1,0:T(8,128)(2,1)}, bf16[256,1024]{1,0:T(8,128)(2,1)}, u32[]{:S(2)}, u32[]{:S(2)}) %collective-permute-start.6) | collective-permute-done | bytes 524320 | tf_op jit(solution)/shard_map/ppermute | solution.py:35
  55.4 3.2 %ln_proj.7 = (bf16[1024,2048]{1,0:T(8,128)(2,1)}, bf16[2,8,128,512]{3,2,1,0:T(8,128)(2,1)}, f32[2,8,128,512]{3,2,1,0:T(8,128)}) custom-call(s32[1]{0:T(128)} %bitcast.11.at_ref, bf16[256,1024]{1,0:T(8,128)(2,1)} %collective-permute-done.6.refs_0_, ...), custom_call_target="tpu_custom_call", output_to_operand_aliasing={{0}: (3, {}), {1}: (4, {}), {2}: (5, {})} | custom-call | flops 268435456 | bytes 3145728 | tf_op jit(solution)/shard_map/ln_proj/pallas_call | solution.py:115
  58.6 6.5 %attention_forward.1 = (f32[128,2048]{1,0:T(8,128)}, bf16[128,2048]{1,0:T(8,128)(2,1)}, bf16[128,2048]{1,0:T(8,128)(2,1)}, f32[4,2048]{1,0:T(4,128)}, s32[1,2048]{1,0:T(1,128)}) custom-call(bf16[2,8,128,512]{3,2,1,0:T(8,128)(2,1)} %get-tuple-element.132.act_ref, bf16[8,272,128]{2,1,0:T(8,128)(2,1)} %copy-done.5), custom_call_target="tpu_custom_call" | custom-call | flops 4294967296 | bytes 6291456 | tf_op jit(solution)/shard_map/attention_forward/pallas_call | solution.py:228
  65.1 1.5 collective-permute-start.11
  66.6 2.7 %collective-permute-done.11 = f32[4,2048]{1,0:T(4,128)S(1)} collective-permute-done((f32[4,2048]{1,0:T(4,128)}, f32[4,2048]{1,0:T(4,128)S(1)}, u32[]{:S(2)}, u32[]{:S(2)}) %collective-permute-start.11) | collective-permute-done | bytes 32800 | tf_op jit(solution)/shard_map/ppermute | solution.py:35
  70.7 1.4 collective-permute-start.13
  72.2 1.9 %collective-permute-start.14 = (f32[2,4,2048]{2,1,0:T(4,128)S(1)}, f32[2,4,2048]{2,1,0:T(4,128)S(1)}, u32[]{:S(2)}, u32[]{:S(2)}) collective-permute-start(f32[2,4,2048]{2,1,0:T(4,128)S(1)} %pad_maximum_fusion.2.own_ref), channel_id=1, source_target_pairs={{64,0},{80,16},{96,32},{112,48},{0,64},{16,80},{32,96},{48,112},{6... | collective-permute-start | bytes 196616 | tf_op jit(solution)/shard_map/ppermute | solution.py:35
  74.1 1.1 collective-permute-done.12.one_ref
  75.2 1.8 %collective-permute-done.13.three_ref = f32[2,4,2048]{2,1,0:T(4,128)S(1)} collective-permute-done((f32[2,4,2048]{2,1,0:T(4,128)S(1)}, f32[2,4,2048]{2,1,0:T(4,128)S(1)}, u32[]{:S(2)}, u32[]{:S(2)}) %collective-permute-start.13) | collective-permute-done | bytes 65568 | tf_op jit(solution)/shard_map/ppermute | solution.py:35
  77.0 1.8 %collective-permute-done.14.two_ref = f32[2,4,2048]{2,1,0:T(4,128)S(1)} collective-permute-done((f32[2,4,2048]{2,1,0:T(4,128)S(1)}, f32[2,4,2048]{2,1,0:T(4,128)S(1)}, u32[]{:S(2)}, u32[]{:S(2)}) %collective-permute-start.14) | collective-permute-done | bytes 65568 | tf_op jit(solution)/shard_map/ppermute | solution.py:35
  78.7 1.8 %collective-permute-start.15 = (bf16[256,1024]{1,0:T(8,128)(2,1)S(1)}, bf16[256,1024]{1,0:T(8,128)(2,1)S(1)}, u32[]{:S(2)}, u32[]{:S(2)}) collective-permute-start(bf16[256,1024]{1,0:T(8,128)(2,1)S(1)} %collective-permute-done.9.refs_2_), channel_id=1, source_target_pairs={{32,0},{48,16},{64,32},{80,48},{96,64},{112,80},{0,96},{16,112},{3... | collective-permute-start | bytes 1572872 | tf_op jit(solution)/shard_map/ppermute | solution.py:35
  80.8 1.4 collective-permute-start.16
  82.2 13.0 %attention_backward.1.grad_ref.gated_ref = bf16[8,256,640]{2,1,0:T(8,128)(2,1)} custom-call(f32[2,4,2048]{2,1,0:T(4,128)} %copy-done.16, f32[2,4,2048]{2,1,0:T(4,128)} %copy-done.17, f32[2,4,2048]{2,1,0:T(4,128)} %copy-done.18, f32[2,4,2048]{2,1,0:T(4,128)} %copy-done.19, bf16[2,8,128,512]{3,2,1,0:T(8,128)(2,1)} %get-tuple-element.132.act_ref, ...), custom_call_target="tpu_custom_call" | custom-call | flops 8053063680 | bytes 10485760 | tf_op jit(solution)/shard_map/attention_backward/pallas_call | solution.py:324
  95.3 0.8 copy-done.14
  96.2 4.3 %all-to-all-start.1 = ((bf16[8,256,640]{2,1,0:T(8,128)(2,1)}), bf16[8,256,640]{2,1,0:T(8,128)(2,1)S(1)}, u32[]{:S(2)}, u32[]{:S(2)}) async-start(bf16[8,256,640]{2,1,0:T(8,128)(2,1)} %attention_backward.1.grad_ref.gated_ref), calls=%async_computation.1 | async-start | bytes 5242880 | tf_op jit(solution)/shard_map/all_to_all | solution.py:647
  100.5 6.5 %terms_in.1 = (f32[8,64,512]{2,1,0:T(8,128)}, f32[8,64,512]{2,1,0:T(8,128)}) custom-call(s32[1]{0:T(128)} %bitcast.12.core_ref, bf16[1024,2048]{1,0:T(8,128)(2,1)} %get-tuple-element.131.normed_ref, bf16[8,256,640]{2,1,0:T(8,128)(2,1)} %attention_backward.1.grad_ref.gated_ref), custom_call_target="tpu_custom_call" | custom-call | flops 2147483648 | bytes 9437184 | tf_op jit(solution)/shard_map/terms_in/pallas_call | solution.py:356
  107.0 3.9 %terms_out.1 = (f32[8,16,512]{2,1,0:T(8,128)}, f32[8,16,512]{2,1,0:T(8,128)}) custom-call(s32[1]{0:T(128)} %bitcast.12.core_ref, s32[8]{0:T(128)} %stack.75.at_ref, bf16[8,256,640]{2,1,0:T(8,128)(2,1)} %attention_backward.1.grad_ref.gated_ref, bf16[256,1024]{1,0:T(8,128)(2,1)} %copy-done.9, bf16[256,1024]{1,0:T(8,128)(2,1)} %copy-done.10, ...), custom_call_target="tpu_custom_call" | custom-call | flops 536870912 | bytes 6291456 | tf_op jit(solution)/shard_map/terms_out/pallas_call | solution.py:401
  111.5 1.4 collective-permute-done.19.got_out_ref
  113.9 2.7 %core_sum.1 = (f32[2,80,512]{2,1,0:T(8,128)}, bf16[2,80,512]{2,1,0:T(8,128)(2,1)}, bf16[2,80,512]{2,1,0:T(8,128)(2,1)}, bf16[2,80,512]{2,1,0:T(8,128)(2,1)}) custom-call(s32[4]{0:T(128)} %pad_add_fusion.2.pos_ref, f32[8,64,512]{2,1,0:T(8,128)} %get-tuple-element.152.keep_ref, f32[8,64,512]{2,1,0:T(8,128)} %copy-done.4, ...), custom_call_target="tpu_custom_call" | custom-call | flops 2621440 | bytes 5242880 | tf_op jit(solution)/shard_map/core_sum/pallas_call | solution.py:419
  116.6 3.0 %collective-permute-start.20 = (bf16[2,80,512]{2,1,0:T(8,128)(2,1)}, bf16[2,80,512]{2,1,0:T(8,128)(2,1)S(1)}, u32[]{:S(2)}, u32[]{:S(2)}) collective-permute-start(bf16[2,80,512]{2,1,0:T(8,128)(2,1)} %get-tuple-element.162), channel_id=1, source_target_pairs={{4,0},{5,1},{6,2},{7,3},{8,4},{9,5},{10,6},{11,7},{12,8},{13,9},{1... | collective-permute-start | bytes 491528 | tf_op jit(solution)/shard_map/ppermute | solution.py:39
  119.7 2.2 %collective-permute-start.22 = (bf16[2,80,512]{2,1,0:T(8,128)(2,1)}, bf16[2,80,512]{2,1,0:T(8,128)(2,1)S(1)}, u32[]{:S(2)}, u32[]{:S(2)}) collective-permute-start(bf16[2,80,512]{2,1,0:T(8,128)(2,1)} %get-tuple-element.164), channel_id=1, source_target_pairs={{8,0},{9,1},{10,2},{11,3},{12,4},{13,5},{14,6},{15,7},{0,8},{1,9},... | collective-permute-start | bytes 491528 | tf_op jit(solution)/shard_map/ppermute | solution.py:39
  121.9 1.5 all-to-all-done.1.gated_ref.grad_ref
  123.4 1.5 copy-done.2
  124.8 6.2 %shard_out.1 = (bf16[256,1024]{1,0:T(8,128)(2,1)}, f32[256,1024]{1,0:T(8,128)}) custom-call(bf16[8,256,640]{2,1,0:T(8,128)(2,1)} %copy-done.2, bf16[8,256,640]{2,1,0:T(8,128)(2,1)} %copy-done.2, bf16[1024,4096]{1,0:T(8,128)(2,1)} %w_in_ref.3, bf16[1024,1024]{1,0:T(8,128)(2,1)} %w_out_ref.1, bf16[256,1024]{1,0:T(8,128)(2,1)} %bitcast.29), custom_call_target="tpu_custom_call" | custom-call | flops 1610612736 | bytes 8388608 | tf_op jit(solution)/shard_map/shard_out/pallas_call | solution.py:519
  131.7 2.9 %collective-permute-start.23 = (f32[48,512]{1,0:T(8,128)S(1)}, f32[48,512]{1,0:T(8,128)S(1)}, u32[]{:S(2)}, u32[]{:S(2)}) collective-permute-start(f32[48,512]{1,0:T(8,128)S(1)} %get-tuple-element.172), channel_id=1, source_target_pairs={{2,0},{3,1},{0,2},{1,3},{6,4},{7,5},{4,6},{5,7},{10,8},{11,9},{8,1... | collective-permute-start | bytes 294920 | tf_op jit(solution)/shard_map/ppermute | solution.py:47
  134.7 1.1 collective-permute-start.24
  136.2 5.5 %shard_grad.1 = bf16[256,1024]{1,0:T(8,128)(2,1)} custom-call(bf16[8,256,640]{2,1,0:T(8,128)(2,1)} %copy-done.2, bf16[1024,4096]{1,0:T(8,128)(2,1)} %w_in_ref.3, bf16[256,1024]{1,0:T(8,128)(2,1)} %bitcast.30, bf16[256,1024]{1,0:T(8,128)(2,1)} %bitcast.34, f32[256,1024]{1,0:T(8,128)} %get-tuple-element.175.half_ref), custom_call_target="tpu_custom_call" | custom-call | flops 1073741824 | bytes 8388608 | tf_op jit(solution)/shard_map/shard_grad/pallas_call | solution.py:542
  142.3 2.7 %collective-permute-start.26 = (f32[16,512]{1,0:T(8,128)S(1)}, f32[16,512]{1,0:T(8,128)S(1)}, u32[]{:S(2)}, u32[]{:S(2)}) collective-permute-start(f32[16,512]{1,0:T(8,128)S(1)} %get-tuple-element.182), channel_id=1, source_target_pairs={{32,0},{48,16},{64,32},{80,48},{96,64},{112,80},{0,96},{16,112},{3... | collective-permute-start | bytes 98312 | tf_op jit(solution)/shard_map/ppermute | solution.py:35
  145.0 2.3 %collective-permute-start.28 = (f32[16,512]{1,0:T(8,128)S(1)}, f32[16,512]{1,0:T(8,128)S(1)}, u32[]{:S(2)}, u32[]{:S(2)}) collective-permute-start(f32[16,512]{1,0:T(8,128)S(1)} %get-tuple-element.184), channel_id=1, source_target_pairs={{64,0},{80,16},{96,32},{112,48},{0,64},{16,80},{32,96},{48,112},{6... | collective-permute-start | bytes 98312 | tf_op jit(solution)/shard_map/ppermute | solution.py:35
  147.4 2.8 %collective-permute-done.27.three_ref = f32[16,512]{1,0:T(8,128)S(1)} collective-permute-done((f32[16,512]{1,0:T(8,128)S(1)}, f32[16,512]{1,0:T(8,128)S(1)}, u32[]{:S(2)}, u32[]{:S(2)}) %collective-permute-start.27) | collective-permute-done | bytes 32800 | tf_op jit(solution)/shard_map/ppermute | solution.py:35
  150.5 1.2 z_place.1
  (83 shorter events, 9.5 us)
Async XLA Ops:
  0.6 16.0 %collective-permute-start = (bf16[256,1024]{1,0:T(8,128)(2,1)}, bf16[256,1024]{1,0:T(8,128)(2,1)S(1)}, u32[]{:S(2)}, u32[]{:S(2)}) collective-permute-start(bf16[256,1024]{1,0:T(8,128)(2,1)} %bitcast.25), channel_id=1, source_target_pairs={{16,0},{0,16},{48,32},{32,48},{80,64},{64,80},{112,96},{96,112},{1... | collective-permute-start | bytes 1572872 | tf_op jit(solution)/shard_map/ppermute | solution.py:35
  2.3 15.3 %collective-permute-start.1 = (bf16[256,1024]{1,0:T(8,128)(2,1)}, bf16[256,1024]{1,0:T(8,128)(2,1)S(1)}, u32[]{:S(2)}, u32[]{:S(2)}) collective-permute-start(bf16[256,1024]{1,0:T(8,128)(2,1)} %bitcast.26), channel_id=1, source_target_pairs={{32,0},{48,16},{64,32},{80,48},{96,64},{112,80},{0,96},{16,112},{3... | collective-permute-start | bytes 1572872 | tf_op jit(solution)/shard_map/ppermute | solution.py:35
  6.3 14.5 %collective-permute-start.2 = (bf16[256,1024]{1,0:T(8,128)(2,1)}, bf16[256,1024]{1,0:T(8,128)(2,1)S(1)}, u32[]{:S(2)}, u32[]{:S(2)}) collective-permute-start(bf16[256,1024]{1,0:T(8,128)(2,1)} %bitcast.27), channel_id=1, source_target_pairs={{96,0},{112,16},{0,32},{16,48},{32,64},{48,80},{64,96},{80,112},{9... | collective-permute-start | bytes 1572872 | tf_op jit(solution)/shard_map/ppermute | solution.py:35
  11.3 12.1 %copy-start.20 = (s32[1,256]{1,0:T(1,128)S(1)}, s32[1,256]{1,0:T(1,128)}, u32[]{:S(2)}) copy-start(s32[1,256]{1,0:T(1,128)} %param.6) | copy-start | bytes 3076
  16.7 11.4 %copy-start.6 = (bf16[256,1024]{1,0:T(8,128)(2,1)}, bf16[256,1024]{1,0:T(8,128)(2,1)S(1)}, u32[]{:S(2)}) copy-start(bf16[256,1024]{1,0:T(8,128)(2,1)S(1)} %collective-permute-done.refs_0_) | copy-start | bytes 1572868
  17.5 10.6 %copy-start.7 = (bf16[256,1024]{1,0:T(8,128)(2,1)}, bf16[256,1024]{1,0:T(8,128)(2,1)S(1)}, u32[]{:S(2)}) copy-start(bf16[256,1024]{1,0:T(8,128)(2,1)S(1)} %collective-permute-done.1.refs_1_) | copy-start | bytes 1572868
  20.8 7.3 %copy-start.8 = (bf16[256,1024]{1,0:T(8,128)(2,1)}, bf16[256,1024]{1,0:T(8,128)(2,1)S(1)}, u32[]{:S(2)}) copy-start(bf16[256,1024]{1,0:T(8,128)(2,1)S(1)} %collective-permute-done.2.refs_2_) | copy-start | bytes 1572868
  20.8 15.0 %collective-permute-start.3 = (bf16[256,1024]{1,0:T(8,128)(2,1)S(1)}, bf16[256,1024]{1,0:T(8,128)(2,1)}, u32[]{:S(2)}, u32[]{:S(2)}) collective-permute-start(bf16[256,1024]{1,0:T(8,128)(2,1)S(1)} %collective-permute-done.1.refs_1_), channel_id=1, source_target_pairs={{16,0},{0,16},{48,32},{32,48},{80,64},{64,80},{112,96},{96,112},{1... | collective-permute-start | bytes 1572872 | tf_op jit(solution)/shard_map/ppermute | solution.py:35
  21.4 16.9 %collective-permute-start.4 = (bf16[256,1024]{1,0:T(8,128)(2,1)S(1)}, bf16[256,1024]{1,0:T(8,128)(2,1)}, u32[]{:S(2)}, u32[]{:S(2)}) collective-permute-start(bf16[256,1024]{1,0:T(8,128)(2,1)S(1)} %collective-permute-done.1.refs_1_), channel_id=1, source_target_pairs={{32,0},{48,16},{64,32},{80,48},{96,64},{112,80},{0,96},{16,112},{3... | collective-permute-start | bytes 1572872 | tf_op jit(solution)/shard_map/ppermute | solution.py:35
  21.7 17.0 %collective-permute-start.5 = (bf16[256,1024]{1,0:T(8,128)(2,1)S(1)}, bf16[256,1024]{1,0:T(8,128)(2,1)}, u32[]{:S(2)}, u32[]{:S(2)}) collective-permute-start(bf16[256,1024]{1,0:T(8,128)(2,1)S(1)} %collective-permute-done.refs_0_), channel_id=1, source_target_pairs={{96,0},{112,16},{0,32},{16,48},{32,64},{48,80},{64,96},{80,112},{9... | collective-permute-start | bytes 1572872 | tf_op jit(solution)/shard_map/ppermute | solution.py:35
  24.3 19.7 %all-to-all-start = ((bf16[8,272,128]{2,1,0:T(8,128)(2,1)}), bf16[8,272,128]{2,1,0:T(8,128)(2,1)S(1)}, u32[]{:S(2)}, u32[]{:S(2)}) async-start(bf16[8,272,128]{2,1,0:T(8,128)(2,1)} %pad_maximum_fusion.1), calls=%async_computation | async-start | bytes 1114112 | tf_op jit(solution)/shard_map/all_to_all | solution.py:617
  28.1 13.8 %copy-start.3 = (bf16[1,256,1024]{2,1,0:T(8,128)(2,1)S(1)}, bf16[1,256,1024]{2,1,0:T(8,128)(2,1)}, u32[]{:S(2)}) copy-start(bf16[1,256,1024]{2,1,0:T(8,128)(2,1)} %param.9) | copy-start | bytes 1572868
  38.7 16.4 %collective-permute-start.6 = (bf16[256,1024]{1,0:T(8,128)(2,1)}, bf16[256,1024]{1,0:T(8,128)(2,1)}, u32[]{:S(2)}, u32[]{:S(2)}) collective-permute-start(bf16[256,1024]{1,0:T(8,128)(2,1)} %collective-permute-done.4.refs_1_), channel_id=1, source_target_pairs={{16,0},{0,16},{48,32},{32,48},{80,64},{64,80},{112,96},{96,112},{1... | collective-permute-start | bytes 1572872 | tf_op jit(solution)/shard_map/ppermute | solution.py:35
  41.9 13.2 %collective-permute-start.7 = (bf16[256,1024]{1,0:T(8,128)(2,1)S(1)}, bf16[256,1024]{1,0:T(8,128)(2,1)S(1)}, u32[]{:S(2)}, u32[]{:S(2)}) collective-permute-start(bf16[256,1024]{1,0:T(8,128)(2,1)S(1)} %bitcast.35), channel_id=1, source_target_pairs={{32,0},{48,16},{64,32},{80,48},{96,64},{112,80},{0,96},{16,112},{3... | collective-permute-start | bytes 1572872 | tf_op jit(solution)/shard_map/ppermute | solution.py:35
  41.9 13.2 %collective-permute-start.8 = (bf16[256,1024]{1,0:T(8,128)(2,1)S(1)}, bf16[256,1024]{1,0:T(8,128)(2,1)S(1)}, u32[]{:S(2)}, u32[]{:S(2)}) collective-permute-start(bf16[256,1024]{1,0:T(8,128)(2,1)S(1)} %bitcast.36), channel_id=1, source_target_pairs={{96,0},{112,16},{0,32},{16,48},{32,64},{48,80},{64,96},{80,112},{9... | collective-permute-start | bytes 1572872 | tf_op jit(solution)/shard_map/ppermute | solution.py:35
  44.0 21.1 %collective-permute-start.9 = (bf16[256,1024]{1,0:T(8,128)(2,1)S(1)}, bf16[256,1024]{1,0:T(8,128)(2,1)S(1)}, u32[]{:S(2)}, u32[]{:S(2)}) collective-permute-start(bf16[256,1024]{1,0:T(8,128)(2,1)S(1)} %bitcast.37), channel_id=1, source_target_pairs={{16,0},{0,16},{48,32},{32,48},{80,64},{64,80},{112,96},{96,112},{1... | collective-permute-start | bytes 1572872 | tf_op jit(solution)/shard_map/ppermute | solution.py:35
  44.0 6.3 %copy-start.5 = (bf16[8,272,128]{2,1,0:T(8,128)(2,1)}, bf16[8,272,128]{2,1,0:T(8,128)(2,1)S(1)}, u32[]{:S(2)}) copy-start(bf16[8,272,128]{2,1,0:T(8,128)(2,1)S(1)} %all-to-all-done.head_ref) | copy-start | bytes 1671172
  55.1 3.5 %copy-start.9 = (bf16[256,1024]{1,0:T(8,128)(2,1)}, bf16[256,1024]{1,0:T(8,128)(2,1)S(1)}, u32[]{:S(2)}) copy-start(bf16[256,1024]{1,0:T(8,128)(2,1)S(1)} %collective-permute-done.7.refs_0_) | copy-start | bytes 1572868
  55.1 3.5 %copy-start.10 = (bf16[256,1024]{1,0:T(8,128)(2,1)}, bf16[256,1024]{1,0:T(8,128)(2,1)S(1)}, u32[]{:S(2)}) copy-start(bf16[256,1024]{1,0:T(8,128)(2,1)S(1)} %collective-permute-done.8.refs_1_) | copy-start | bytes 1572868
  55.1 10.0 %collective-permute-start.10 = (bf16[256,1024]{1,0:T(8,128)(2,1)S(1)}, bf16[256,1024]{1,0:T(8,128)(2,1)S(1)}, u32[]{:S(2)}, u32[]{:S(2)}) collective-permute-start(bf16[256,1024]{1,0:T(8,128)(2,1)S(1)} %collective-permute-done.7.refs_0_), channel_id=1, source_target_pairs={{32,0},{48,16},{64,32},{80,48},{96,64},{112,80},{0,96},{16,112},{3... | collective-permute-start | bytes 1572872 | tf_op jit(solution)/shard_map/ppermute | solution.py:35
  65.1 30.1 %copy-start.11 = (bf16[256,1024]{1,0:T(8,128)(2,1)}, bf16[256,1024]{1,0:T(8,128)(2,1)S(1)}, u32[]{:S(2)}) copy-start(bf16[256,1024]{1,0:T(8,128)(2,1)S(1)} %collective-permute-done.9.refs_2_) | copy-start | bytes 1572868
  65.1 30.1 %copy-start.12 = (bf16[256,1024]{1,0:T(8,128)(2,1)}, bf16[256,1024]{1,0:T(8,128)(2,1)S(1)}, u32[]{:S(2)}) copy-start(bf16[256,1024]{1,0:T(8,128)(2,1)S(1)} %collective-permute-done.10.refs_3_) | copy-start | bytes 1572868
  65.1 4.2 %collective-permute-start.11 = (f32[4,2048]{1,0:T(4,128)}, f32[4,2048]{1,0:T(4,128)S(1)}, u32[]{:S(2)}, u32[]{:S(2)}) collective-permute-start(f32[4,2048]{1,0:T(4,128)} %get-tuple-element.136), channel_id=1, source_target_pairs={{16,0},{0,16},{48,32},{32,48},{80,64},{64,80},{112,96},{96,112},{1... | collective-permute-start | bytes 98312 | tf_op jit(solution)/shard_map/ppermute | solution.py:35
  70.1 12.1 %copy-start.16 = (f32[2,4,2048]{2,1,0:T(4,128)}, f32[2,4,2048]{2,1,0:T(4,128)S(1)}, u32[]{:S(2)}) copy-start(f32[2,4,2048]{2,1,0:T(4,128)S(1)} %pad_maximum_fusion.2.own_ref) | copy-start | bytes 196612
  70.1 5.1 %collective-permute-start.12 = (f32[2,4,2048]{2,1,0:T(4,128)S(1)}, f32[2,4,2048]{2,1,0:T(4,128)S(1)}, u32[]{:S(2)}, u32[]{:S(2)}) collective-permute-start(f32[2,4,2048]{2,1,0:T(4,128)S(1)} %pad_maximum_fusion.2.own_ref), channel_id=1, source_target_pairs={{32,0},{48,16},{64,32},{80,48},{96,64},{112,80},{0,96},{16,112},{3... | collective-permute-start | bytes 196616 | tf_op jit(solution)/shard_map/ppermute | solution.py:35
  70.7 6.2 %collective-permute-start.13 = (f32[2,4,2048]{2,1,0:T(4,128)S(1)}, f32[2,4,2048]{2,1,0:T(4,128)S(1)}, u32[]{:S(2)}, u32[]{:S(2)}) collective-permute-start(f32[2,4,2048]{2,1,0:T(4,128)S(1)} %pad_maximum_fusion.2.own_ref), channel_id=1, source_target_pairs={{96,0},{112,16},{0,32},{16,48},{32,64},{48,80},{64,96},{80,112},{9... | collective-permute-start | bytes 196616 | tf_op jit(solution)/shard_map/ppermute | solution.py:35
  72.2 6.5 %collective-permute-start.14 = (f32[2,4,2048]{2,1,0:T(4,128)S(1)}, f32[2,4,2048]{2,1,0:T(4,128)S(1)}, u32[]{:S(2)}, u32[]{:S(2)}) collective-permute-start(f32[2,4,2048]{2,1,0:T(4,128)S(1)} %pad_maximum_fusion.2.own_ref), channel_id=1, source_target_pairs={{64,0},{80,16},{96,32},{112,48},{0,64},{16,80},{32,96},{48,112},{6... | collective-permute-start | bytes 196616 | tf_op jit(solution)/shard_map/ppermute | solution.py:35
  75.2 7.0 %copy-start.17 = (f32[2,4,2048]{2,1,0:T(4,128)}, f32[2,4,2048]{2,1,0:T(4,128)S(1)}, u32[]{:S(2)}) copy-start(f32[2,4,2048]{2,1,0:T(4,128)S(1)} %collective-permute-done.12.one_ref) | copy-start | bytes 196612
  77.0 5.2 %copy-start.18 = (f32[2,4,2048]{2,1,0:T(4,128)}, f32[2,4,2048]{2,1,0:T(4,128)S(1)}, u32[]{:S(2)}) copy-start(f32[2,4,2048]{2,1,0:T(4,128)S(1)} %collective-permute-done.13.three_ref) | copy-start | bytes 196612
  78.7 3.5 %copy-start.19 = (f32[2,4,2048]{2,1,0:T(4,128)}, f32[2,4,2048]{2,1,0:T(4,128)S(1)}, u32[]{:S(2)}) copy-start(f32[2,4,2048]{2,1,0:T(4,128)S(1)} %collective-permute-done.14.two_ref) | copy-start | bytes 196612
  78.7 16.5 %collective-permute-start.15 = (bf16[256,1024]{1,0:T(8,128)(2,1)S(1)}, bf16[256,1024]{1,0:T(8,128)(2,1)S(1)}, u32[]{:S(2)}, u32[]{:S(2)}) collective-permute-start(bf16[256,1024]{1,0:T(8,128)(2,1)S(1)} %collective-permute-done.9.refs_2_), channel_id=1, source_target_pairs={{32,0},{48,16},{64,32},{80,48},{96,64},{112,80},{0,96},{16,112},{3... | collective-permute-start | bytes 1572872 | tf_op jit(solution)/shard_map/ppermute | solution.py:35
  80.5 15.6 %collective-permute-start.17 = (bf16[256,1024]{1,0:T(8,128)(2,1)S(1)}, bf16[256,1024]{1,0:T(8,128)(2,1)}, u32[]{:S(2)}, u32[]{:S(2)}) collective-permute-start(bf16[256,1024]{1,0:T(8,128)(2,1)S(1)} %collective-permute-done.9.refs_2_), channel_id=1, source_target_pairs={{96,0},{112,16},{0,32},{16,48},{32,64},{48,80},{64,96},{80,112},{9... | collective-permute-start | bytes 1572872 | tf_op jit(solution)/shard_map/ppermute | solution.py:35
  80.8 14.5 %collective-permute-start.16 = (bf16[256,1024]{1,0:T(8,128)(2,1)S(1)}, bf16[256,1024]{1,0:T(8,128)(2,1)S(1)}, u32[]{:S(2)}, u32[]{:S(2)}) collective-permute-start(bf16[256,1024]{1,0:T(8,128)(2,1)S(1)} %collective-permute-done.10.refs_3_), channel_id=1, source_target_pairs={{16,0},{0,16},{48,32},{32,48},{80,64},{64,80},{112,96},{96,112},{1... | collective-permute-start | bytes 1572872 | tf_op jit(solution)/shard_map/ppermute | solution.py:35
  96.2 27.2 %all-to-all-start.1 = ((bf16[8,256,640]{2,1,0:T(8,128)(2,1)}), bf16[8,256,640]{2,1,0:T(8,128)(2,1)S(1)}, u32[]{:S(2)}, u32[]{:S(2)}) async-start(bf16[8,256,640]{2,1,0:T(8,128)(2,1)} %attention_backward.1.grad_ref.gated_ref), calls=%async_computation.1 | async-start | bytes 5242880 | tf_op jit(solution)/shard_map/all_to_all | solution.py:647
  107.0 5.8 %collective-permute-start.18 = (f32[8,64,512]{2,1,0:T(8,128)}, f32[8,64,512]{2,1,0:T(8,128)S(1)}, u32[]{:S(2)}, u32[]{:S(2)}) collective-permute-start(f32[8,64,512]{2,1,0:T(8,128)} %get-tuple-element.153), channel_id=1, source_target_pairs={{1,0},{0,1},{3,2},{2,3},{5,4},{4,5},{7,6},{6,7},{9,8},{8,9},{11,10... | collective-permute-start | bytes 3145736 | tf_op jit(solution)/shard_map/ppermute | solution.py:39
  110.9 2.0 %collective-permute-start.19 = (f32[8,16,512]{2,1,0:T(8,128)}, f32[8,16,512]{2,1,0:T(8,128)S(1)}, u32[]{:S(2)}, u32[]{:S(2)}) collective-permute-start(f32[8,16,512]{2,1,0:T(8,128)} %get-tuple-element.161), channel_id=1, source_target_pairs={{1,0},{0,1},{3,2},{2,3},{5,4},{4,5},{7,6},{6,7},{9,8},{8,9},{11,10... | collective-permute-start | bytes 786440 | tf_op jit(solution)/shard_map/ppermute | solution.py:39
  116.6 14.4 %collective-permute-start.20 = (bf16[2,80,512]{2,1,0:T(8,128)(2,1)}, bf16[2,80,512]{2,1,0:T(8,128)(2,1)S(1)}, u32[]{:S(2)}, u32[]{:S(2)}) collective-permute-start(bf16[2,80,512]{2,1,0:T(8,128)(2,1)} %get-tuple-element.162), channel_id=1, source_target_pairs={{4,0},{5,1},{6,2},{7,3},{8,4},{9,5},{10,6},{11,7},{12,8},{13,9},{1... | collective-permute-start | bytes 491528 | tf_op jit(solution)/shard_map/ppermute | solution.py:39
  119.7 11.3 %collective-permute-start.21 = (bf16[2,80,512]{2,1,0:T(8,128)(2,1)}, bf16[2,80,512]{2,1,0:T(8,128)(2,1)S(1)}, u32[]{:S(2)}, u32[]{:S(2)}) collective-permute-start(bf16[2,80,512]{2,1,0:T(8,128)(2,1)} %get-tuple-element.163), channel_id=1, source_target_pairs={{12,0},{13,1},{14,2},{15,3},{0,4},{1,5},{2,6},{3,7},{4,8},{5,9},{6... | collective-permute-start | bytes 491528 | tf_op jit(solution)/shard_map/ppermute | solution.py:39
  119.7 11.4 %copy-start = (f32[2,80,512]{2,1,0:T(8,128)S(1)}, f32[2,80,512]{2,1,0:T(8,128)}, u32[]{:S(2)}) copy-start(f32[2,80,512]{2,1,0:T(8,128)} %get-tuple-element.168.own_ref) | copy-start | bytes 983044
  119.7 11.4 %copy-start.1 = (s32[4]{0:T(128)S(1)}, s32[4]{0:T(128)}, u32[]{:S(2)}) copy-start(s32[4]{0:T(128)} %pad_add_fusion.2.pos_ref) | copy-start | bytes 52
  119.7 11.3 %collective-permute-start.22 = (bf16[2,80,512]{2,1,0:T(8,128)(2,1)}, bf16[2,80,512]{2,1,0:T(8,128)(2,1)S(1)}, u32[]{:S(2)}, u32[]{:S(2)}) collective-permute-start(bf16[2,80,512]{2,1,0:T(8,128)(2,1)} %get-tuple-element.164), channel_id=1, source_target_pairs={{8,0},{9,1},{10,2},{11,3},{12,4},{13,5},{14,6},{15,7},{0,8},{1,9},... | collective-permute-start | bytes 491528 | tf_op jit(solution)/shard_map/ppermute | solution.py:39
  123.4 1.5 copy-start.2
  131.7 10.0 %collective-permute-start.23 = (f32[48,512]{1,0:T(8,128)S(1)}, f32[48,512]{1,0:T(8,128)S(1)}, u32[]{:S(2)}, u32[]{:S(2)}) collective-permute-start(f32[48,512]{1,0:T(8,128)S(1)} %get-tuple-element.172), channel_id=1, source_target_pairs={{2,0},{3,1},{0,2},{1,3},{6,4},{7,5},{4,6},{5,7},{10,8},{11,9},{8,1... | collective-permute-start | bytes 294920 | tf_op jit(solution)/shard_map/ppermute | solution.py:47
  134.7 7.0 %collective-permute-start.24 = (f32[32,512]{1,0:T(8,128)S(1)}, f32[32,512]{1,0:T(8,128)S(1)}, u32[]{:S(2)}, u32[]{:S(2)}) collective-permute-start(f32[32,512]{1,0:T(8,128)S(1)} %get-tuple-element.173), channel_id=1, source_target_pairs={{16,0},{17,1},{18,2},{19,3},{20,4},{21,5},{22,6},{23,7},{24,8},{25... | collective-permute-start | bytes 196616 | tf_op jit(solution)/shard_map/ppermute | solution.py:47
  135.8 5.9 %collective-permute-start.25 = (f32[32,512]{1,0:T(8,128)S(1)}, f32[32,512]{1,0:T(8,128)S(1)}, u32[]{:S(2)}, u32[]{:S(2)}) collective-permute-start(f32[32,512]{1,0:T(8,128)S(1)} %get-tuple-element.174), channel_id=1, source_target_pairs={{18,0},{19,1},{16,2},{17,3},{22,4},{23,5},{20,6},{21,7},{26,8},{27... | collective-permute-start | bytes 196616 | tf_op jit(solution)/shard_map/ppermute | solution.py:47
  142.3 5.1 %collective-permute-start.26 = (f32[16,512]{1,0:T(8,128)S(1)}, f32[16,512]{1,0:T(8,128)S(1)}, u32[]{:S(2)}, u32[]{:S(2)}) collective-permute-start(f32[16,512]{1,0:T(8,128)S(1)} %get-tuple-element.182), channel_id=1, source_target_pairs={{32,0},{48,16},{64,32},{80,48},{96,64},{112,80},{0,96},{16,112},{3... | collective-permute-start | bytes 98312 | tf_op jit(solution)/shard_map/ppermute | solution.py:35
  145.0 5.1 %collective-permute-start.27 = (f32[16,512]{1,0:T(8,128)S(1)}, f32[16,512]{1,0:T(8,128)S(1)}, u32[]{:S(2)}, u32[]{:S(2)}) collective-permute-start(f32[16,512]{1,0:T(8,128)S(1)} %get-tuple-element.183), channel_id=1, source_target_pairs={{96,0},{112,16},{0,32},{16,48},{32,64},{48,80},{64,96},{80,112},{9... | collective-permute-start | bytes 98312 | tf_op jit(solution)/shard_map/ppermute | solution.py:35
  145.0 5.5 %collective-permute-start.28 = (f32[16,512]{1,0:T(8,128)S(1)}, f32[16,512]{1,0:T(8,128)S(1)}, u32[]{:S(2)}, u32[]{:S(2)}) collective-permute-start(f32[16,512]{1,0:T(8,128)S(1)} %get-tuple-element.184), channel_id=1, source_target_pairs={{64,0},{80,16},{96,32},{112,48},{0,64},{16,80},{32,96},{48,112},{6... | collective-permute-start | bytes 98312 | tf_op jit(solution)/shard_map/ppermute | solution.py:35
  (4 other events, 3.6 us)

commit v2 on v1

--- a/solution.py
+++ b/solution.py
@@ -485,79 +485,54 @@
     return jnp.concatenate([ref[h] for h in range(H)], axis=1)
 
 
-def shard_out_kernel(gated_ref, grad_ref, w_in_ref, w_out_ref, hist_ref, layer_ref, acc_ref):
+def shard_out_kernel(gated_ref, grad_ref, w_in_ref, w_out_ref, hist_ref, layer_ref, sum_ref):
+    hist = hist_ref[...].astype(F32)
+    layer_ref[...] = (hist + dot(columns(gated_ref), w_out_ref[...])).astype(BF16)
+    sum_ref[...] = dot_nt(columns(grad_ref), w_in_ref[...])
+
+
+def shard_more_kernel(grad_ref, w_in_ref, before_ref, sum_ref):
     term = dot_nt(columns(grad_ref), w_in_ref[...])
 
     @pl.when(pl.program_id(0) == 0)
     def _():
-        hist = hist_ref[...].astype(F32)
-        layer_ref[...] = (hist + dot(columns(gated_ref), w_out_ref[...])).astype(BF16)
-        acc_ref[...] = term
+        sum_ref[...] = before_ref[...] + term
 
     @pl.when(pl.program_id(0) > 0)
     def _():
-        acc_ref[...] += term
-
-
-def shard_grad_kernel(grad_ref, w_in_ref, hist_ref, cot_ref, half_ref, grad_hist_ref, acc_ref):
-    term = dot_nt(columns(grad_ref), w_in_ref[...])
-
-    @pl.when(pl.program_id(0) == 0)
-    def _():
-        acc_ref[...] = half_ref[...] + term
-
-    @pl.when(pl.program_id(0) > 0)
-    def _():
-        normed, inverse = layer_norm(hist_ref[...].astype(F32))
-        grad = norm_back(normed, inverse, acc_ref[...] + term)
-        grad_hist_ref[...] = (cot_ref[...].astype(F32) + grad).astype(BF16)
-
-
-def shard_out(back, w_in, w_out, hist):
-    rows, width = hist.shape
-    whole = lambda a: pl.BlockSpec(a.shape, lambda k: (0,) * a.ndim)
+        sum_ref[...] += term
+
+
+def shard_grad_kernel(grad_ref, w_in_ref, hist_ref, cot_ref, before_ref, grad_hist_ref):
+    grad_normed = before_ref[...] + dot_nt(columns(grad_ref), w_in_ref[...])
+    normed, inverse = layer_norm(hist_ref[...].astype(F32))
+    grad = norm_back(normed, inverse, grad_normed)
+    grad_hist_ref[...] = (cot_ref[...].astype(F32) + grad).astype(BF16)
+
+
+def whole(a):
+    return pl.BlockSpec(a.shape, lambda k: (0,) * a.ndim)
+
+
+def shard_part(kernel, name, back, w_in, first, count, before, after, outs):
+    rows, width = back.shape[1], w_in.shape[0]
     return pl.pallas_call(
-        shard_out_kernel,
-        grid=(2,),
-        in_specs=[
-            pl.BlockSpec((H, rows, HD), lambda k: (0, 0, 4)),
-            pl.BlockSpec((H, rows, HD), lambda k: (0, 0, k)),
-            pl.BlockSpec((width, width), lambda k: (0, k)),
-            whole(w_out),
-            whole(hist),
-        ],
-        out_specs=[whole(hist)] * 2,
-        out_shape=[jax.ShapeDtypeStruct(hist.shape, BF16), jax.ShapeDtypeStruct(hist.shape, F32)],
+        kernel,
+        grid=(count,),
+        in_specs=[pl.BlockSpec((H, rows, HD), lambda k: (0, 0, 4))] * before
+        + [
+            pl.BlockSpec((H, rows, HD), lambda k: (0, 0, first + k)),
+            pl.BlockSpec((width, width), lambda k: (0, first + k)),
+        ]
+        + [whole(a) for a in after],
+        out_specs=[pl.BlockSpec((rows, width), lambda k: (0, 0))] * len(outs),
+        out_shape=[jax.ShapeDtypeStruct((rows, width), dtype) for dtype in outs],
         compiler_params=params(LIMIT),
         cost_estimate=pl.CostEstimate(
-            flops=6 * rows * width * width, bytes_accessed=8 << 20, transcendentals=0
-        ),
-        name="shard_out",
-    )(back, back, w_in, w_out, hist)
-
-
-def shard_grad(back, w_in, hist, cot, half):
-    rows, width = hist.shape
-    whole = lambda a: pl.BlockSpec(a.shape, lambda k: (0,) * a.ndim)
-    return pl.pallas_call(
-        shard_grad_kernel,
-        grid=(2,),
-        in_specs=[
-            pl.BlockSpec((H, rows, HD), lambda k: (0, 0, 2 + k)),
-            pl.BlockSpec((width, width), lambda k: (0, 2 + k)),
-            whole(hist),
-            whole(cot),
-            whole(half),
-        ],
-        out_specs=whole(hist),
-        out_shape=jax.ShapeDtypeStruct(hist.shape, BF16),
-        scratch_shapes=[pltpu.VMEM((rows, width), F32)],
-        compiler_params=params(LIMIT),
-        cost_estimate=pl.CostEstimate(
-            flops=4 * rows * width * width, bytes_accessed=8 << 20, transcendentals=0
-        ),
-        name="shard_grad",
-    )(back, w_in, hist, cot, half)
+            flops=2 * (count + before) * rows * width * width, bytes_accessed=8 << 20, transcendentals=0
+        ),
+        name=name,
+    )(*[back] * (before + 1), w_in, *after)
 
 
 def local(history, segment_ids, w_in, w_out, cotangent):
@@ -601,8 +576,8 @@
     }
     outs = project({(0, 0): hist}, ())
     grad_gated_own = dot_nt(cot, w_out).astype(BF16).reshape(rows, H, HD).transpose(1, 0, 2)
-    got, outs, grad_gated_own, waiting, at_core, at = tie(
-        (got, outs, grad_gated_own, tuple(places.values()), at_core, at)
+    outs, grad_gated_own, waiting, at_core, at = tie(
+        (outs, grad_gated_own, tuple(places.values()), at_core, at)
     )
     places = dict(zip(orders, waiting))
     ids = segment_ids[0].astype(BF16).reshape(2, HD)
@@ -661,8 +636,10 @@
     )
     own, sends = tie((own, sends))
     sends = [from_user(a, d, 0, 0) for a, d in zip(sends, (1, 3, 2))]
-    layer_out, half = shard_out(back_tok, w_in, w_out, hist)
-    sends, layer_out, half = tie((sends, layer_out, half))
+    layer_out, partial = shard_part(
+        shard_out_kernel, "shard_out", back_tok, w_in, 0, 1, 1, [w_out, hist], [BF16, F32]
+    )
+    sends, layer_out, partial = tie((sends, layer_out, partial))
     keep, same, one, two = small(
         y_sum_kernel,
         "y_sum",
@@ -674,8 +651,8 @@
     same = from_both(same, 1, 0)
     one = from_both(one, 0, 1)
     two = from_both(two, 1, 1)
-    grad_history = shard_grad(back_tok, w_in, hist, cot, half)
-    same, one, two, grad_history = tie((same, one, two, grad_history))
+    (partial,) = shard_part(shard_more_kernel, "shard_more", back_tok, w_in, 1, 2, 0, [partial], [F32])
+    same, one, two, partial = tie((same, one, two, partial))
     own, *sends, own_out = small(
         x_sum_kernel,
         "x_sum",
@@ -685,6 +662,10 @@
         [pltpu.VMEM((NX, 32, n), F32)],
     )
     sends = [from_seq(a, d, 0) for a, d in zip(sends, (1, 3, 2))]
+    (grad_history,) = shard_part(
+        shard_grad_kernel, "shard_grad", back_tok, w_in, 3, 1, 0, [hist, cot, partial], [BF16]
+    )
+    sends, grad_history = tie((sends, grad_history))
     factor = (length * users) ** (-0.5)
     grad_w_in, grad_w_out = small(
         functools.partial(z_place_kernel, factor),

time: 152 us -> 153 us (level)
  waiting for transfers between devices: 26.6 us -> 23 us
  starting transfers between devices: 46.2 us -> 48.6 us
  Pallas kernels: 65.7 us -> 68 us
    ppermute x21, waiting for transfers between devices: 23.7 us -> 19.1 us  [from_seq(): return lax.ppermute(a, 'seq', seq_perm(dz, dx))]
    pallas_call x2 -> x3, Pallas kernels: 11.6 us -> 13.9 us  [shard_part(): pl.pallas_call(kernel, grid=(count,), in_specs=[pl.BlockSpec((H, rows, HD...]
    ppermute x5, waiting for transfers between devices: 1.38 us -> 3.47 us  [from_user(): return lax.ppermute(a, 'user', user_perm(dy, dh, dc))]
    unnamed x42 -> x44, local copies, waits for them, and re-layouts: 3.55 us -> 3.81 us
  transfers between devices with their start and end apart: 31 -> 31, of which waited for: 14 -> 11; matrix products, arithmetic and copies ran while one was open for 5% -> 5% of each run, Pallas kernels for 42% -> 43%
where the time goes in v2:
time: 153 us; the launch traced here: 152 us
  Pallas kernels  68 us (44%)
  starting transfers between devices  48.6 us (32%)
  waiting for transfers between devices  23 us (15%)
  local copies, waits for them, and re-layouts  6.15 us (4%)
  other arithmetic  3.91 us (3%)
  matrix products  1.78 us (1%)
    ppermute x21, starting transfers between devices, from_seq(): return lax.ppermute(a, 'seq', seq_perm(dz, dx))  28.7 us
    ppermute x21, waiting for transfers between devices, from_seq(): return lax.ppermute(a, 'seq', seq_perm(dz, dx))  19.1 us
    pallas_call x4, Pallas kernels, ln_proj(): pl.pallas_call(functools.partial(ln_proj_kernel, len(blocks)), grid_spec=...  19 us
    pallas_call x3, Pallas kernels, shard_part(): pl.pallas_call(kernel, grid=(count,), in_specs=[pl.BlockSpec((H, rows, HD...  13.9 us
    pallas_call x1, Pallas kernels, backward(): pl.pallas_call(backward_kernel, in_specs=[vmem()] * 9 + [pl.BlockSpec(mem...  13 us
    pallas_call x1, Pallas kernels, terms_in(): pl.pallas_call(terms_in_kernel, grid=(4,), in_specs=[smem(), pl.BlockSpec...  6.57 us
    pallas_call x1, Pallas kernels, forward(): pl.pallas_call(forward_kernel, in_specs=[vmem()] * 2, out_specs=[vmem()]...  6.49 us
    ppermute x5, starting transfers between devices, from_user(): return lax.ppermute(a, 'user', user_perm(dy, dh, dc))  5.82 us
  transfers between devices with their start and end apart: 31, of which 11 were waited for; matrix products, arithmetic and copies ran while one was open for 5% of the time, Pallas kernels for 43%

profile of v2, /device:TPU:0, one launch (start us, length us, event | category | flops | bytes accessed | tf_op | source)
XLA Modules:
  0.0 152.3 jit_solution(7157238717534490857)
XLA Ops:
  0.6 4.2 %collective-permute-start = (bf16[256,1024]{1,0:T(8,128)(2,1)}, bf16[256,1024]{1,0:T(8,128)(2,1)S(1)}, u32[]{:S(2)}, u32[]{:S(2)}) collective-permute-start(bf16[256,1024]{1,0:T(8,128)(2,1)} %bitcast.25), channel_id=1, source_target_pairs={{32,0},{48,16},{64,32},{80,48},{96,64},{112,80},{0,96},{16,112},{3... | collective-permute-start | bytes 1572872 | tf_op jit(solution)/shard_map/ppermute | solution.py:35
  4.8 1.5 collective-permute-start.3
  6.3 1.3 constant_dynamic-slice_fusion.3
  7.6 1.8 %convolution_convert_fusion = bf16[256,1024]{1,0:T(8,128)(2,1)S(1)} fusion(bf16[1024,1024]{1,0:T(8,128)(2,1)S(1)} %copy-done.3, bf16[1,256,1024]{2,1,0:T(8,128)(2,1)} %param.9), kind=kOutput, calls=%fused_computation | convolution fusion | flops 537133056 | bytes 3145728 | tf_op jit(solution)/shard_map/dot_general | solution.py:68
  9.4 1.1 pad_maximum_fusion.refs_1_.refs_3_
  11.6 3.1 %ln_proj.4 = (bf16[1024,2048]{1,0:T(8,128)(2,1)}, bf16[2,8,128,512]{3,2,1,0:T(8,128)(2,1)}, f32[2,8,128,512]{3,2,1,0:T(8,128)}) custom-call(s32[1]{0:T(128)} %bitcast.at_ref, bf16[256,1024]{1,0:T(8,128)(2,1)} %bitcast.28, bf16[1024,512]{1,0:T(8,128)(2,1)} %pad_maximum_fusion.refs_1_.refs_3_), custom_call_target="tpu_custom_call" | custom-call | flops 268435456 | bytes 3145728 | tf_op jit(solution)/shard_map/ln_proj/pallas_call | solution.py:115
  14.7 1.7 %collective-permute-done.refs_1_ = bf16[256,1024]{1,0:T(8,128)(2,1)S(1)} collective-permute-done((bf16[256,1024]{1,0:T(8,128)(2,1)}, bf16[256,1024]{1,0:T(8,128)(2,1)S(1)}, u32[]{:S(2)}, u32[]{:S(2)}) %collective-permute-start) | collective-permute-done | bytes 524320 | tf_op jit(solution)/shard_map/ppermute | solution.py:35
  16.3 1.5 collective-permute-start.1
  17.8 3.6 %collective-permute-start.2 = (bf16[256,1024]{1,0:T(8,128)(2,1)S(1)}, bf16[256,1024]{1,0:T(8,128)(2,1)}, u32[]{:S(2)}, u32[]{:S(2)}) collective-permute-start(bf16[256,1024]{1,0:T(8,128)(2,1)S(1)} %collective-permute-done.refs_1_), channel_id=1, source_target_pairs={{32,0},{48,16},{64,32},{80,48},{96,64},{112,80},{0,96},{16,112},{3... | collective-permute-start | bytes 1572872 | tf_op jit(solution)/shard_map/ppermute | solution.py:35
  22.6 0.9 pad_maximum_fusion.1
  23.5 4.5 %all-to-all-start = ((bf16[8,272,128]{2,1,0:T(8,128)(2,1)}), bf16[8,272,128]{2,1,0:T(8,128)(2,1)S(1)}, u32[]{:S(2)}, u32[]{:S(2)}) async-start(bf16[8,272,128]{2,1,0:T(8,128)(2,1)} %pad_maximum_fusion.1), calls=%async_computation | async-start | bytes 1114112 | tf_op jit(solution)/shard_map/all_to_all | solution.py:592
  28.0 6.5 %ln_proj.5 = (bf16[1024,2048]{1,0:T(8,128)(2,1)}, bf16[2,8,128,512]{3,2,1,0:T(8,128)(2,1)}, f32[2,8,128,512]{3,2,1,0:T(8,128)}) custom-call(s32[3]{0:T(128)} %get-tuple-element.103.at_ref, bf16[256,1024]{1,0:T(8,128)(2,1)} %collective-permute-done.3.refs_0_, bf16[256,1024]{1,0:T(8,128)(2,1)} %copy-done.7, ...), custom_call_target="tpu_custom_call", output_to_operand_aliasing={{0}: (5, {}), {1}: (6, {}), {2}: (7, {})} | custom-call | flops 805306368 | bytes 9437184 | tf_op jit(solution)/shard_map/ln_proj/pallas_call | solution.py:115
  34.5 2.2 %collective-permute-done.2.refs_1_ = bf16[256,1024]{1,0:T(8,128)(2,1)} collective-permute-done((bf16[256,1024]{1,0:T(8,128)(2,1)S(1)}, bf16[256,1024]{1,0:T(8,128)(2,1)}, u32[]{:S(2)}, u32[]{:S(2)}) %collective-permute-start.2) | collective-permute-done | bytes 524320 | tf_op jit(solution)/shard_map/ppermute | solution.py:35
  36.7 3.6 %collective-permute-done.4.refs_2_ = bf16[256,1024]{1,0:T(8,128)(2,1)S(1)} collective-permute-done((bf16[256,1024]{1,0:T(8,128)(2,1)}, bf16[256,1024]{1,0:T(8,128)(2,1)S(1)}, u32[]{:S(2)}, u32[]{:S(2)}) %collective-permute-start.4) | collective-permute-done | bytes 524320 | tf_op jit(solution)/shard_map/ppermute | solution.py:35
  41.3 1.9 %collective-permute-start.8 = (bf16[256,1024]{1,0:T(8,128)(2,1)S(1)}, bf16[256,1024]{1,0:T(8,128)(2,1)S(1)}, u32[]{:S(2)}, u32[]{:S(2)}) collective-permute-start(bf16[256,1024]{1,0:T(8,128)(2,1)S(1)} %bitcast.36), channel_id=1, source_target_pairs={{96,0},{112,16},{0,32},{16,48},{32,64},{48,80},{64,96},{80,112},{9... | collective-permute-start | bytes 1572872 | tf_op jit(solution)/shard_map/ppermute | solution.py:35
  43.1 1.2 collective-permute-start.9
  44.4 6.3 %ln_proj.6 = (bf16[1024,2048]{1,0:T(8,128)(2,1)}, bf16[2,8,128,512]{3,2,1,0:T(8,128)(2,1)}, f32[2,8,128,512]{3,2,1,0:T(8,128)}) custom-call(s32[3]{0:T(128)} %get-tuple-element.112.at_ref, bf16[256,1024]{1,0:T(8,128)(2,1)} %copy-done.12, ...), custom_call_target="tpu_custom_call", output_to_operand_aliasing={{0}: (5, {}), {1}: (6, {}), {2}: (7, {})} | custom-call | flops 805306368 | bytes 9437184 | tf_op jit(solution)/shard_map/ln_proj/pallas_call | solution.py:115
  50.7 2.4 %collective-permute-done.6.refs_0_ = bf16[256,1024]{1,0:T(8,128)(2,1)} collective-permute-done((bf16[256,1024]{1,0:T(8,128)(2,1)}, bf16[256,1024]{1,0:T(8,128)(2,1)}, u32[]{:S(2)}, u32[]{:S(2)}) %collective-permute-start.6) | collective-permute-done | bytes 524320 | tf_op jit(solution)/shard_map/ppermute | solution.py:35
  53.1 2.9 %collective-permute-start.10 = (bf16[256,1024]{1,0:T(8,128)(2,1)S(1)}, bf16[256,1024]{1,0:T(8,128)(2,1)S(1)}, u32[]{:S(2)}, u32[]{:S(2)}) collective-permute-start(bf16[256,1024]{1,0:T(8,128)(2,1)S(1)} %collective-permute-done.7.refs_0_), channel_id=1, source_target_pairs={{32,0},{48,16},{64,32},{80,48},{96,64},{112,80},{0,96},{16,112},{3... | collective-permute-start | bytes 1572872 | tf_op jit(solution)/shard_map/ppermute | solution.py:35
  56.0 3.1 %ln_proj.7 = (bf16[1024,2048]{1,0:T(8,128)(2,1)}, bf16[2,8,128,512]{3,2,1,0:T(8,128)(2,1)}, f32[2,8,128,512]{3,2,1,0:T(8,128)}) custom-call(s32[1]{0:T(128)} %bitcast.11.at_ref, bf16[256,1024]{1,0:T(8,128)(2,1)} %collective-permute-done.6.refs_0_, ...), custom_call_target="tpu_custom_call", output_to_operand_aliasing={{0}: (3, {}), {1}: (4, {}), {2}: (5, {})} | custom-call | flops 268435456 | bytes 3145728 | tf_op jit(solution)/shard_map/ln_proj/pallas_call | solution.py:115
  59.1 6.5 %attention_forward.1 = (f32[128,2048]{1,0:T(8,128)}, bf16[128,2048]{1,0:T(8,128)(2,1)}, bf16[128,2048]{1,0:T(8,128)(2,1)}, f32[4,2048]{1,0:T(4,128)}, s32[1,2048]{1,0:T(1,128)}) custom-call(bf16[2,8,128,512]{3,2,1,0:T(8,128)(2,1)} %get-tuple-element.130.act_ref, bf16[8,272,128]{2,1,0:T(8,128)(2,1)} %copy-done.6), custom_call_target="tpu_custom_call" | custom-call | flops 4294967296 | bytes 6291456 | tf_op jit(solution)/shard_map/attention_forward/pallas_call | solution.py:228
  66.3 3.6 %collective-permute-done.11 = f32[4,2048]{1,0:T(4,128)S(1)} collective-permute-done((f32[4,2048]{1,0:T(4,128)}, f32[4,2048]{1,0:T(4,128)S(1)}, u32[]{:S(2)}, u32[]{:S(2)}) %collective-permute-start.11) | collective-permute-done | bytes 32800 | tf_op jit(solution)/shard_map/ppermute | solution.py:35
  70.6 1.0 collective-permute-start.12
  71.6 1.1 collective-permute-start.13
  73.1 2.6 %collective-permute-done.12.one_ref = f32[2,4,2048]{2,1,0:T(4,128)S(1)} collective-permute-done((f32[2,4,2048]{2,1,0:T(4,128)S(1)}, f32[2,4,2048]{2,1,0:T(4,128)S(1)}, u32[]{:S(2)}, u32[]{:S(2)}) %collective-permute-start.12) | collective-permute-done | bytes 65568 | tf_op jit(solution)/shard_map/ppermute | solution.py:35
  75.7 2.1 %collective-permute-done.13.three_ref = f32[2,4,2048]{2,1,0:T(4,128)S(1)} collective-permute-done((f32[2,4,2048]{2,1,0:T(4,128)S(1)}, f32[2,4,2048]{2,1,0:T(4,128)S(1)}, u32[]{:S(2)}, u32[]{:S(2)}) %collective-permute-start.13) | collective-permute-done | bytes 65568 | tf_op jit(solution)/shard_map/ppermute | solution.py:35
  77.8 1.0 collective-permute-done.14.two_ref
  78.8 1.8 %collective-permute-start.15 = (bf16[256,1024]{1,0:T(8,128)(2,1)S(1)}, bf16[256,1024]{1,0:T(8,128)(2,1)S(1)}, u32[]{:S(2)}, u32[]{:S(2)}) collective-permute-start(bf16[256,1024]{1,0:T(8,128)(2,1)S(1)} %collective-permute-done.9.refs_2_), channel_id=1, source_target_pairs={{32,0},{48,16},{64,32},{80,48},{96,64},{112,80},{0,96},{16,112},{3... | collective-permute-start | bytes 1572872 | tf_op jit(solution)/shard_map/ppermute | solution.py:35
  80.8 1.0 collective-permute-start.16
  81.8 13.0 %attention_backward.1.grad_ref.gated_ref = bf16[8,256,640]{2,1,0:T(8,128)(2,1)} custom-call(f32[2,4,2048]{2,1,0:T(4,128)} %copy-done.17, f32[2,4,2048]{2,1,0:T(4,128)} %copy-done.18, f32[2,4,2048]{2,1,0:T(4,128)} %copy-done.19, f32[2,4,2048]{2,1,0:T(4,128)} %copy-done.20, bf16[2,8,128,512]{3,2,1,0:T(8,128)(2,1)} %get-tuple-element.130.act_ref, ...), custom_call_target="tpu_custom_call" | custom-call | flops 8053063680 | bytes 10485760 | tf_op jit(solution)/shard_map/attention_backward/pallas_call | solution.py:324
  94.9 0.8 copy-done.15
  95.9 4.7 %all-to-all-start.1 = ((bf16[8,256,640]{2,1,0:T(8,128)(2,1)}), bf16[8,256,640]{2,1,0:T(8,128)(2,1)S(1)}, u32[]{:S(2)}, u32[]{:S(2)}) async-start(bf16[8,256,640]{2,1,0:T(8,128)(2,1)} %attention_backward.1.grad_ref.gated_ref), calls=%async_computation.1 | async-start | bytes 5242880 | tf_op jit(solution)/shard_map/all_to_all | solution.py:622
  100.6 6.6 %terms_in.1 = (f32[8,64,512]{2,1,0:T(8,128)}, f32[8,64,512]{2,1,0:T(8,128)}) custom-call(s32[1]{0:T(128)} %bitcast.12.core_ref, bf16[1024,2048]{1,0:T(8,128)(2,1)} %get-tuple-element.129.normed_ref, bf16[8,256,640]{2,1,0:T(8,128)(2,1)} %attention_backward.1.grad_ref.gated_ref), custom_call_target="tpu_custom_call" | custom-call | flops 2147483648 | bytes 9437184 | tf_op jit(solution)/shard_map/terms_in/pallas_call | solution.py:356
  107.2 3.8 %terms_out.1 = (f32[8,16,512]{2,1,0:T(8,128)}, f32[8,16,512]{2,1,0:T(8,128)}) custom-call(s32[1]{0:T(128)} %bitcast.12.core_ref, s32[8]{0:T(128)} %stack.75.at_ref, bf16[8,256,640]{2,1,0:T(8,128)(2,1)} %attention_backward.1.grad_ref.gated_ref, bf16[256,1024]{1,0:T(8,128)(2,1)} %copy-done.8, bf16[256,1024]{1,0:T(8,128)(2,1)} %copy-done.9, ...), custom_call_target="tpu_custom_call" | custom-call | flops 536870912 | bytes 6291456 | tf_op jit(solution)/shard_map/terms_out/pallas_call | solution.py:401
  111.6 1.4 collective-permute-done.19.got_out_ref
  114.1 2.7 %core_sum.1 = (f32[2,80,512]{2,1,0:T(8,128)}, bf16[2,80,512]{2,1,0:T(8,128)(2,1)}, bf16[2,80,512]{2,1,0:T(8,128)(2,1)}, bf16[2,80,512]{2,1,0:T(8,128)(2,1)}) custom-call(s32[4]{0:T(128)} %pad_add_fusion.2.pos_ref, f32[8,64,512]{2,1,0:T(8,128)} %get-tuple-element.150.keep_ref, f32[8,64,512]{2,1,0:T(8,128)} %copy-done.5, ...), custom_call_target="tpu_custom_call" | custom-call | flops 2621440 | bytes 5242880 | tf_op jit(solution)/shard_map/core_sum/pallas_call | solution.py:419
  116.8 3.0 %collective-permute-start.20 = (bf16[2,80,512]{2,1,0:T(8,128)(2,1)}, bf16[2,80,512]{2,1,0:T(8,128)(2,1)S(1)}, u32[]{:S(2)}, u32[]{:S(2)}) collective-permute-start(bf16[2,80,512]{2,1,0:T(8,128)(2,1)} %get-tuple-element.160), channel_id=1, source_target_pairs={{4,0},{5,1},{6,2},{7,3},{8,4},{9,5},{10,6},{11,7},{12,8},{13,9},{1... | collective-permute-start | bytes 491528 | tf_op jit(solution)/shard_map/ppermute | solution.py:39
  119.8 2.2 %collective-permute-start.22 = (bf16[2,80,512]{2,1,0:T(8,128)(2,1)}, bf16[2,80,512]{2,1,0:T(8,128)(2,1)S(1)}, u32[]{:S(2)}, u32[]{:S(2)}) collective-permute-start(bf16[2,80,512]{2,1,0:T(8,128)(2,1)} %get-tuple-element.162), channel_id=1, source_target_pairs={{8,0},{9,1},{10,2},{11,3},{12,4},{13,5},{14,6},{15,7},{0,8},{1,9},... | collective-permute-start | bytes 491528 | tf_op jit(solution)/shard_map/ppermute | solution.py:39
  122.5 1.5 copy-done.2
  123.9 4.9 %shard_out.1 = (bf16[256,1024]{1,0:T(8,128)(2,1)}, f32[256,1024]{1,0:T(8,128)}) custom-call(bf16[8,256,640]{2,1,0:T(8,128)(2,1)} %copy-done.2, bf16[8,256,640]{2,1,0:T(8,128)(2,1)} %copy-done.2, bf16[1024,4096]{1,0:T(8,128)(2,1)} %w_in_ref.5, bf16[1024,1024]{1,0:T(8,128)(2,1)} %w_out_ref.1, bf16[256,1024]{1,0:T(8,128)(2,1)} %bitcast.29), custom_call_target="tpu_custom_call" | custom-call | flops 1073741824 | bytes 8388608 | tf_op jit(solution)/shard_map/shard_out/pallas_call | solution.py:519
  128.8 2.1 %collective-permute-done.21.b_ref = bf16[2,80,512]{2,1,0:T(8,128)(2,1)S(1)} collective-permute-done((bf16[2,80,512]{2,1,0:T(8,128)(2,1)}, bf16[2,80,512]{2,1,0:T(8,128)(2,1)S(1)}, u32[]{:S(2)}, u32[]{:S(2)}) %collective-permute-start.21) | collective-permute-done | bytes 163872 | tf_op jit(solution)/shard_map/ppermute | solution.py:39
  131.6 2.7 %collective-permute-start.23 = (f32[48,512]{1,0:T(8,128)S(1)}, f32[48,512]{1,0:T(8,128)S(1)}, u32[]{:S(2)}, u32[]{:S(2)}) collective-permute-start(f32[48,512]{1,0:T(8,128)S(1)} %get-tuple-element.171), channel_id=1, source_target_pairs={{2,0},{3,1},{0,2},{1,3},{6,4},{7,5},{4,6},{5,7},{10,8},{11,9},{8,1... | collective-permute-start | bytes 294920 | tf_op jit(solution)/shard_map/ppermute | solution.py:47
  134.3 1.4 collective-permute-start.24
  136.3 4.8 %shard_more.1.before_ref = f32[256,1024]{1,0:T(8,128)} custom-call(bf16[8,256,640]{2,1,0:T(8,128)(2,1)} %copy-done.2, bf16[1024,4096]{1,0:T(8,128)(2,1)} %w_in_ref.5, f32[256,1024]{1,0:T(8,128)} %get-tuple-element.174.before_ref), custom_call_target="tpu_custom_call" | custom-call | flops 1073741824 | bytes 8388608 | tf_op jit(solution)/shard_map/shard_more/pallas_call | solution.py:519
  141.7 2.8 %collective-permute-start.26 = (f32[16,512]{1,0:T(8,128)S(1)}, f32[16,512]{1,0:T(8,128)S(1)}, u32[]{:S(2)}, u32[]{:S(2)}) collective-permute-start(f32[16,512]{1,0:T(8,128)S(1)} %get-tuple-element.178), channel_id=1, source_target_pairs={{32,0},{48,16},{64,32},{80,48},{96,64},{112,80},{0,96},{16,112},{3... | collective-permute-start | bytes 98312 | tf_op jit(solution)/shard_map/ppermute | solution.py:35
  144.5 2.3 %collective-permute-start.28 = (f32[16,512]{1,0:T(8,128)S(1)}, f32[16,512]{1,0:T(8,128)S(1)}, u32[]{:S(2)}, u32[]{:S(2)}) collective-permute-start(f32[16,512]{1,0:T(8,128)S(1)} %get-tuple-element.180), channel_id=1, source_target_pairs={{64,0},{80,16},{96,32},{112,48},{0,64},{16,80},{32,96},{48,112},{6... | collective-permute-start | bytes 98312 | tf_op jit(solution)/shard_map/ppermute | solution.py:35
  146.8 4.2 %shard_grad.1 = bf16[256,1024]{1,0:T(8,128)(2,1)} custom-call(bf16[8,256,640]{2,1,0:T(8,128)(2,1)} %copy-done.2, bf16[1024,4096]{1,0:T(8,128)(2,1)} %w_in_ref.5, bf16[256,1024]{1,0:T(8,128)(2,1)} %bitcast.30, bf16[256,1024]{1,0:T(8,128)(2,1)} %bitcast.34, f32[256,1024]{1,0:T(8,128)} %shard_more.1.before_ref), custom_call_target="tpu_custom_call" | custom-call | flops 536870912 | bytes 8388608 | tf_op jit(solution)/shard_map/shard_grad/pallas_call | solution.py:519
  151.1 1.2 z_place.1
  (86 shorter events, 9.6 us)
Async XLA Ops:
  0.6 7.0 %copy-start.3 = (bf16[1024,1024]{1,0:T(8,128)(2,1)S(1)}, bf16[1024,1024]{1,0:T(8,128)(2,1)}, u32[]{:S(2)}) copy-start(bf16[1024,1024]{1,0:T(8,128)(2,1)} %w_out_ref.1) | copy-start | bytes 6291460
  0.6 15.7 %collective-permute-start = (bf16[256,1024]{1,0:T(8,128)(2,1)}, bf16[256,1024]{1,0:T(8,128)(2,1)S(1)}, u32[]{:S(2)}, u32[]{:S(2)}) collective-permute-start(bf16[256,1024]{1,0:T(8,128)(2,1)} %bitcast.25), channel_id=1, source_target_pairs={{32,0},{48,16},{64,32},{80,48},{96,64},{112,80},{0,96},{16,112},{3... | collective-permute-start | bytes 1572872 | tf_op jit(solution)/shard_map/ppermute | solution.py:35
  4.8 16.6 %collective-permute-start.3 = (bf16[256,1024]{1,0:T(8,128)(2,1)}, bf16[256,1024]{1,0:T(8,128)(2,1)}, u32[]{:S(2)}, u32[]{:S(2)}) collective-permute-start(bf16[256,1024]{1,0:T(8,128)(2,1)} %bitcast.26), channel_id=1, source_target_pairs={{16,0},{0,16},{48,32},{32,48},{80,64},{64,80},{112,96},{96,112},{1... | collective-permute-start | bytes 1572872 | tf_op jit(solution)/shard_map/ppermute | solution.py:35
  6.3 21.7 %collective-permute-start.5 = (bf16[256,1024]{1,0:T(8,128)(2,1)}, bf16[256,1024]{1,0:T(8,128)(2,1)}, u32[]{:S(2)}, u32[]{:S(2)}) collective-permute-start(bf16[256,1024]{1,0:T(8,128)(2,1)} %bitcast.27), channel_id=1, source_target_pairs={{96,0},{112,16},{0,32},{16,48},{32,64},{48,80},{64,96},{80,112},{9... | collective-permute-start | bytes 1572872 | tf_op jit(solution)/shard_map/ppermute | solution.py:35
  10.5 12.1 %copy-start.21 = (s32[1,256]{1,0:T(1,128)S(1)}, s32[1,256]{1,0:T(1,128)}, u32[]{:S(2)}) copy-start(s32[1,256]{1,0:T(1,128)} %param.6) | copy-start | bytes 3076
  16.3 11.7 %copy-start.7 = (bf16[256,1024]{1,0:T(8,128)(2,1)}, bf16[256,1024]{1,0:T(8,128)(2,1)S(1)}, u32[]{:S(2)}) copy-start(bf16[256,1024]{1,0:T(8,128)(2,1)S(1)} %collective-permute-done.refs_1_) | copy-start | bytes 1572868
  16.3 18.2 %collective-permute-start.1 = (bf16[256,1024]{1,0:T(8,128)(2,1)S(1)}, bf16[256,1024]{1,0:T(8,128)(2,1)S(1)}, u32[]{:S(2)}, u32[]{:S(2)}) collective-permute-start(bf16[256,1024]{1,0:T(8,128)(2,1)S(1)} %collective-permute-done.refs_1_), channel_id=1, source_target_pairs={{16,0},{0,16},{48,32},{32,48},{80,64},{64,80},{112,96},{96,112},{1... | collective-permute-start | bytes 1572872 | tf_op jit(solution)/shard_map/ppermute | solution.py:35
  17.8 18.8 %collective-permute-start.2 = (bf16[256,1024]{1,0:T(8,128)(2,1)S(1)}, bf16[256,1024]{1,0:T(8,128)(2,1)}, u32[]{:S(2)}, u32[]{:S(2)}) collective-permute-start(bf16[256,1024]{1,0:T(8,128)(2,1)S(1)} %collective-permute-done.refs_1_), channel_id=1, source_target_pairs={{32,0},{48,16},{64,32},{80,48},{96,64},{112,80},{0,96},{16,112},{3... | collective-permute-start | bytes 1572872 | tf_op jit(solution)/shard_map/ppermute | solution.py:35
  21.4 18.9 %collective-permute-start.4 = (bf16[256,1024]{1,0:T(8,128)(2,1)}, bf16[256,1024]{1,0:T(8,128)(2,1)S(1)}, u32[]{:S(2)}, u32[]{:S(2)}) collective-permute-start(bf16[256,1024]{1,0:T(8,128)(2,1)} %collective-permute-done.3.refs_0_), channel_id=1, source_target_pairs={{96,0},{112,16},{0,32},{16,48},{32,64},{48,80},{64,96},{80,112},{9... | collective-permute-start | bytes 1572872 | tf_op jit(solution)/shard_map/ppermute | solution.py:35
  23.5 20.9 %all-to-all-start = ((bf16[8,272,128]{2,1,0:T(8,128)(2,1)}), bf16[8,272,128]{2,1,0:T(8,128)(2,1)S(1)}, u32[]{:S(2)}, u32[]{:S(2)}) async-start(bf16[8,272,128]{2,1,0:T(8,128)(2,1)} %pad_maximum_fusion.1), calls=%async_computation | async-start | bytes 1114112 | tf_op jit(solution)/shard_map/all_to_all | solution.py:592
  28.0 13.1 %copy-start.4 = (bf16[1,256,1024]{2,1,0:T(8,128)(2,1)S(1)}, bf16[1,256,1024]{2,1,0:T(8,128)(2,1)}, u32[]{:S(2)}) copy-start(bf16[1,256,1024]{2,1,0:T(8,128)(2,1)} %param.9) | copy-start | bytes 1572868
  34.5 5.8 %copy-start.12 = (bf16[256,1024]{1,0:T(8,128)(2,1)}, bf16[256,1024]{1,0:T(8,128)(2,1)S(1)}, u32[]{:S(2)}) copy-start(bf16[256,1024]{1,0:T(8,128)(2,1)S(1)} %collective-permute-done.1.refs_0_) | copy-start | bytes 1572868
  40.3 12.8 %collective-permute-start.6 = (bf16[256,1024]{1,0:T(8,128)(2,1)}, bf16[256,1024]{1,0:T(8,128)(2,1)}, u32[]{:S(2)}, u32[]{:S(2)}) collective-permute-start(bf16[256,1024]{1,0:T(8,128)(2,1)} %collective-permute-done.2.refs_1_), channel_id=1, source_target_pairs={{16,0},{0,16},{48,32},{32,48},{80,64},{64,80},{112,96},{96,112},{1... | collective-permute-start | bytes 1572872 | tf_op jit(solution)/shard_map/ppermute | solution.py:35
  41.1 12.0 %collective-permute-start.7 = (bf16[256,1024]{1,0:T(8,128)(2,1)S(1)}, bf16[256,1024]{1,0:T(8,128)(2,1)S(1)}, u32[]{:S(2)}, u32[]{:S(2)}) collective-permute-start(bf16[256,1024]{1,0:T(8,128)(2,1)S(1)} %bitcast.35), channel_id=1, source_target_pairs={{32,0},{48,16},{64,32},{80,48},{96,64},{112,80},{0,96},{16,112},{3... | collective-permute-start | bytes 1572872 | tf_op jit(solution)/shard_map/ppermute | solution.py:35
  41.3 11.8 %collective-permute-start.8 = (bf16[256,1024]{1,0:T(8,128)(2,1)S(1)}, bf16[256,1024]{1,0:T(8,128)(2,1)S(1)}, u32[]{:S(2)}, u32[]{:S(2)}) collective-permute-start(bf16[256,1024]{1,0:T(8,128)(2,1)S(1)} %bitcast.36), channel_id=1, source_target_pairs={{96,0},{112,16},{0,32},{16,48},{32,64},{48,80},{64,96},{80,112},{9... | collective-permute-start | bytes 1572872 | tf_op jit(solution)/shard_map/ppermute | solution.py:35
  43.1 22.5 %collective-permute-start.9 = (bf16[256,1024]{1,0:T(8,128)(2,1)S(1)}, bf16[256,1024]{1,0:T(8,128)(2,1)S(1)}, u32[]{:S(2)}, u32[]{:S(2)}) collective-permute-start(bf16[256,1024]{1,0:T(8,128)(2,1)S(1)} %bitcast.37), channel_id=1, source_target_pairs={{16,0},{0,16},{48,32},{32,48},{80,64},{64,80},{112,96},{96,112},{1... | collective-permute-start | bytes 1572872 | tf_op jit(solution)/shard_map/ppermute | solution.py:35
  44.4 6.3 %copy-start.6 = (bf16[8,272,128]{2,1,0:T(8,128)(2,1)}, bf16[8,272,128]{2,1,0:T(8,128)(2,1)S(1)}, u32[]{:S(2)}) copy-start(bf16[8,272,128]{2,1,0:T(8,128)(2,1)S(1)} %all-to-all-done.head_ref) | copy-start | bytes 1671172
  53.1 6.0 %copy-start.8 = (bf16[256,1024]{1,0:T(8,128)(2,1)}, bf16[256,1024]{1,0:T(8,128)(2,1)S(1)}, u32[]{:S(2)}) copy-start(bf16[256,1024]{1,0:T(8,128)(2,1)S(1)} %collective-permute-done.7.refs_0_) | copy-start | bytes 1572868
  53.1 6.0 %copy-start.9 = (bf16[256,1024]{1,0:T(8,128)(2,1)}, bf16[256,1024]{1,0:T(8,128)(2,1)S(1)}, u32[]{:S(2)}) copy-start(bf16[256,1024]{1,0:T(8,128)(2,1)S(1)} %collective-permute-done.8.refs_1_) | copy-start | bytes 1572868
  53.1 12.5 %collective-permute-start.10 = (bf16[256,1024]{1,0:T(8,128)(2,1)S(1)}, bf16[256,1024]{1,0:T(8,128)(2,1)S(1)}, u32[]{:S(2)}, u32[]{:S(2)}) collective-permute-start(bf16[256,1024]{1,0:T(8,128)(2,1)S(1)} %collective-permute-done.7.refs_0_), channel_id=1, source_target_pairs={{32,0},{48,16},{64,32},{80,48},{96,64},{112,80},{0,96},{16,112},{3... | collective-permute-start | bytes 1572872 | tf_op jit(solution)/shard_map/ppermute | solution.py:35
  65.6 29.3 %copy-start.10 = (bf16[256,1024]{1,0:T(8,128)(2,1)}, bf16[256,1024]{1,0:T(8,128)(2,1)S(1)}, u32[]{:S(2)}) copy-start(bf16[256,1024]{1,0:T(8,128)(2,1)S(1)} %collective-permute-done.9.refs_2_) | copy-start | bytes 1572868
  65.6 29.3 %copy-start.11 = (bf16[256,1024]{1,0:T(8,128)(2,1)}, bf16[256,1024]{1,0:T(8,128)(2,1)S(1)}, u32[]{:S(2)}) copy-start(bf16[256,1024]{1,0:T(8,128)(2,1)S(1)} %collective-permute-done.10.refs_3_) | copy-start | bytes 1572868
  65.6 4.2 %collective-permute-start.11 = (f32[4,2048]{1,0:T(4,128)}, f32[4,2048]{1,0:T(4,128)S(1)}, u32[]{:S(2)}, u32[]{:S(2)}) collective-permute-start(f32[4,2048]{1,0:T(4,128)} %get-tuple-element.134), channel_id=1, source_target_pairs={{16,0},{0,16},{48,32},{32,48},{80,64},{64,80},{112,96},{96,112},{1... | collective-permute-start | bytes 98312 | tf_op jit(solution)/shard_map/ppermute | solution.py:35
  70.6 11.2 %copy-start.17 = (f32[2,4,2048]{2,1,0:T(4,128)}, f32[2,4,2048]{2,1,0:T(4,128)S(1)}, u32[]{:S(2)}) copy-start(f32[2,4,2048]{2,1,0:T(4,128)S(1)} %pad_maximum_fusion.2.own_ref) | copy-start | bytes 196612
  70.6 5.1 %collective-permute-start.12 = (f32[2,4,2048]{2,1,0:T(4,128)S(1)}, f32[2,4,2048]{2,1,0:T(4,128)S(1)}, u32[]{:S(2)}, u32[]{:S(2)}) collective-permute-start(f32[2,4,2048]{2,1,0:T(4,128)S(1)} %pad_maximum_fusion.2.own_ref), channel_id=1, source_target_pairs={{32,0},{48,16},{64,32},{80,48},{96,64},{112,80},{0,96},{16,112},{3... | collective-permute-start | bytes 196616 | tf_op jit(solution)/shard_map/ppermute | solution.py:35
  71.6 6.2 %collective-permute-start.13 = (f32[2,4,2048]{2,1,0:T(4,128)S(1)}, f32[2,4,2048]{2,1,0:T(4,128)S(1)}, u32[]{:S(2)}, u32[]{:S(2)}) collective-permute-start(f32[2,4,2048]{2,1,0:T(4,128)S(1)} %pad_maximum_fusion.2.own_ref), channel_id=1, source_target_pairs={{96,0},{112,16},{0,32},{16,48},{32,64},{48,80},{64,96},{80,112},{9... | collective-permute-start | bytes 196616 | tf_op jit(solution)/shard_map/ppermute | solution.py:35
  72.7 6.1 %collective-permute-start.14 = (f32[2,4,2048]{2,1,0:T(4,128)S(1)}, f32[2,4,2048]{2,1,0:T(4,128)S(1)}, u32[]{:S(2)}, u32[]{:S(2)}) collective-permute-start(f32[2,4,2048]{2,1,0:T(4,128)S(1)} %pad_maximum_fusion.2.own_ref), channel_id=1, source_target_pairs={{64,0},{80,16},{96,32},{112,48},{0,64},{16,80},{32,96},{48,112},{6... | collective-permute-start | bytes 196616 | tf_op jit(solution)/shard_map/ppermute | solution.py:35
  75.7 6.1 %copy-start.18 = (f32[2,4,2048]{2,1,0:T(4,128)}, f32[2,4,2048]{2,1,0:T(4,128)S(1)}, u32[]{:S(2)}) copy-start(f32[2,4,2048]{2,1,0:T(4,128)S(1)} %collective-permute-done.12.one_ref) | copy-start | bytes 196612
  77.8 4.0 %copy-start.19 = (f32[2,4,2048]{2,1,0:T(4,128)}, f32[2,4,2048]{2,1,0:T(4,128)S(1)}, u32[]{:S(2)}) copy-start(f32[2,4,2048]{2,1,0:T(4,128)S(1)} %collective-permute-done.13.three_ref) | copy-start | bytes 196612
  78.8 3.1 %copy-start.20 = (f32[2,4,2048]{2,1,0:T(4,128)}, f32[2,4,2048]{2,1,0:T(4,128)S(1)}, u32[]{:S(2)}) copy-start(f32[2,4,2048]{2,1,0:T(4,128)S(1)} %collective-permute-done.14.two_ref) | copy-start | bytes 196612
  78.8 16.1 %collective-permute-start.15 = (bf16[256,1024]{1,0:T(8,128)(2,1)S(1)}, bf16[256,1024]{1,0:T(8,128)(2,1)S(1)}, u32[]{:S(2)}, u32[]{:S(2)}) collective-permute-start(bf16[256,1024]{1,0:T(8,128)(2,1)S(1)} %collective-permute-done.9.refs_2_), channel_id=1, source_target_pairs={{32,0},{48,16},{64,32},{80,48},{96,64},{112,80},{0,96},{16,112},{3... | collective-permute-start | bytes 1572872 | tf_op jit(solution)/shard_map/ppermute | solution.py:35
  80.6 15.2 %collective-permute-start.17 = (bf16[256,1024]{1,0:T(8,128)(2,1)S(1)}, bf16[256,1024]{1,0:T(8,128)(2,1)}, u32[]{:S(2)}, u32[]{:S(2)}) collective-permute-start(bf16[256,1024]{1,0:T(8,128)(2,1)S(1)} %collective-permute-done.9.refs_2_), channel_id=1, source_target_pairs={{96,0},{112,16},{0,32},{16,48},{32,64},{48,80},{64,96},{80,112},{9... | collective-permute-start | bytes 1572872 | tf_op jit(solution)/shard_map/ppermute | solution.py:35
  80.8 14.1 %collective-permute-start.16 = (bf16[256,1024]{1,0:T(8,128)(2,1)S(1)}, bf16[256,1024]{1,0:T(8,128)(2,1)S(1)}, u32[]{:S(2)}, u32[]{:S(2)}) collective-permute-start(bf16[256,1024]{1,0:T(8,128)(2,1)S(1)} %collective-permute-done.10.refs_3_), channel_id=1, source_target_pairs={{16,0},{0,16},{48,32},{32,48},{80,64},{64,80},{112,96},{96,112},{1... | collective-permute-start | bytes 1572872 | tf_op jit(solution)/shard_map/ppermute | solution.py:35
  95.9 26.6 %all-to-all-start.1 = ((bf16[8,256,640]{2,1,0:T(8,128)(2,1)}), bf16[8,256,640]{2,1,0:T(8,128)(2,1)S(1)}, u32[]{:S(2)}, u32[]{:S(2)}) async-start(bf16[8,256,640]{2,1,0:T(8,128)(2,1)} %attention_backward.1.grad_ref.gated_ref), calls=%async_computation.1 | async-start | bytes 5242880 | tf_op jit(solution)/shard_map/all_to_all | solution.py:622
  107.2 5.8 %collective-permute-start.18 = (f32[8,64,512]{2,1,0:T(8,128)}, f32[8,64,512]{2,1,0:T(8,128)S(1)}, u32[]{:S(2)}, u32[]{:S(2)}) collective-permute-start(f32[8,64,512]{2,1,0:T(8,128)} %get-tuple-element.151), channel_id=1, source_target_pairs={{1,0},{0,1},{3,2},{2,3},{5,4},{4,5},{7,6},{6,7},{9,8},{8,9},{11,10... | collective-permute-start | bytes 3145736 | tf_op jit(solution)/shard_map/ppermute | solution.py:39
  111.0 2.0 %collective-permute-start.19 = (f32[8,16,512]{2,1,0:T(8,128)}, f32[8,16,512]{2,1,0:T(8,128)S(1)}, u32[]{:S(2)}, u32[]{:S(2)}) collective-permute-start(f32[8,16,512]{2,1,0:T(8,128)} %get-tuple-element.159), channel_id=1, source_target_pairs={{1,0},{0,1},{3,2},{2,3},{5,4},{4,5},{7,6},{6,7},{9,8},{8,9},{11,10... | collective-permute-start | bytes 786440 | tf_op jit(solution)/shard_map/ppermute | solution.py:39
  116.8 12.1 %collective-permute-start.20 = (bf16[2,80,512]{2,1,0:T(8,128)(2,1)}, bf16[2,80,512]{2,1,0:T(8,128)(2,1)S(1)}, u32[]{:S(2)}, u32[]{:S(2)}) collective-permute-start(bf16[2,80,512]{2,1,0:T(8,128)(2,1)} %get-tuple-element.160), channel_id=1, source_target_pairs={{4,0},{5,1},{6,2},{7,3},{8,4},{9,5},{10,6},{11,7},{12,8},{13,9},{1... | collective-permute-start | bytes 491528 | tf_op jit(solution)/shard_map/ppermute | solution.py:39
  119.8 11.1 %collective-permute-start.21 = (bf16[2,80,512]{2,1,0:T(8,128)(2,1)}, bf16[2,80,512]{2,1,0:T(8,128)(2,1)S(1)}, u32[]{:S(2)}, u32[]{:S(2)}) collective-permute-start(bf16[2,80,512]{2,1,0:T(8,128)(2,1)} %get-tuple-element.161), channel_id=1, source_target_pairs={{12,0},{13,1},{14,2},{15,3},{0,4},{1,5},{2,6},{3,7},{4,8},{5,9},{6... | collective-permute-start | bytes 491528 | tf_op jit(solution)/shard_map/ppermute | solution.py:39
  119.8 11.1 %copy-start = (f32[2,80,512]{2,1,0:T(8,128)S(1)}, f32[2,80,512]{2,1,0:T(8,128)}, u32[]{:S(2)}) copy-start(f32[2,80,512]{2,1,0:T(8,128)} %get-tuple-element.166.own_ref) | copy-start | bytes 983044
  119.8 11.1 %copy-start.1 = (s32[4]{0:T(128)S(1)}, s32[4]{0:T(128)}, u32[]{:S(2)}) copy-start(s32[4]{0:T(128)} %pad_add_fusion.2.pos_ref) | copy-start | bytes 52
  119.8 11.1 %collective-permute-start.22 = (bf16[2,80,512]{2,1,0:T(8,128)(2,1)}, bf16[2,80,512]{2,1,0:T(8,128)(2,1)S(1)}, u32[]{:S(2)}, u32[]{:S(2)}) collective-permute-start(bf16[2,80,512]{2,1,0:T(8,128)(2,1)} %get-tuple-element.162), channel_id=1, source_target_pairs={{8,0},{9,1},{10,2},{11,3},{12,4},{13,5},{14,6},{15,7},{0,8},{1,9},... | collective-permute-start | bytes 491528 | tf_op jit(solution)/shard_map/ppermute | solution.py:39
  122.5 1.5 copy-start.2
  131.6 9.6 %collective-permute-start.23 = (f32[48,512]{1,0:T(8,128)S(1)}, f32[48,512]{1,0:T(8,128)S(1)}, u32[]{:S(2)}, u32[]{:S(2)}) collective-permute-start(f32[48,512]{1,0:T(8,128)S(1)} %get-tuple-element.171), channel_id=1, source_target_pairs={{2,0},{3,1},{0,2},{1,3},{6,4},{7,5},{4,6},{5,7},{10,8},{11,9},{8,1... | collective-permute-start | bytes 294920 | tf_op jit(solution)/shard_map/ppermute | solution.py:47
  134.3 6.8 %collective-permute-start.24 = (f32[32,512]{1,0:T(8,128)S(1)}, f32[32,512]{1,0:T(8,128)S(1)}, u32[]{:S(2)}, u32[]{:S(2)}) collective-permute-start(f32[32,512]{1,0:T(8,128)S(1)} %get-tuple-element.172), channel_id=1, source_target_pairs={{16,0},{17,1},{18,2},{19,3},{20,4},{21,5},{22,6},{23,7},{24,8},{25... | collective-permute-start | bytes 196616 | tf_op jit(solution)/shard_map/ppermute | solution.py:47
  135.7 5.5 %collective-permute-start.25 = (f32[32,512]{1,0:T(8,128)S(1)}, f32[32,512]{1,0:T(8,128)S(1)}, u32[]{:S(2)}, u32[]{:S(2)}) collective-permute-start(f32[32,512]{1,0:T(8,128)S(1)} %get-tuple-element.173), channel_id=1, source_target_pairs={{18,0},{19,1},{16,2},{17,3},{22,4},{23,5},{20,6},{21,7},{26,8},{27... | collective-permute-start | bytes 196616 | tf_op jit(solution)/shard_map/ppermute | solution.py:47
  141.7 9.3 %collective-permute-start.26 = (f32[16,512]{1,0:T(8,128)S(1)}, f32[16,512]{1,0:T(8,128)S(1)}, u32[]{:S(2)}, u32[]{:S(2)}) collective-permute-start(f32[16,512]{1,0:T(8,128)S(1)} %get-tuple-element.178), channel_id=1, source_target_pairs={{32,0},{48,16},{64,32},{80,48},{96,64},{112,80},{0,96},{16,112},{3... | collective-permute-start | bytes 98312 | tf_op jit(solution)/shard_map/ppermute | solution.py:35
  144.5 6.6 %collective-permute-start.27 = (f32[16,512]{1,0:T(8,128)S(1)}, f32[16,512]{1,0:T(8,128)S(1)}, u32[]{:S(2)}, u32[]{:S(2)}) collective-permute-start(f32[16,512]{1,0:T(8,128)S(1)} %get-tuple-element.179), channel_id=1, source_target_pairs={{96,0},{112,16},{0,32},{16,48},{32,64},{48,80},{64,96},{80,112},{9... | collective-permute-start | bytes 98312 | tf_op jit(solution)/shard_map/ppermute | solution.py:35
  144.5 6.6 %collective-permute-start.28 = (f32[16,512]{1,0:T(8,128)S(1)}, f32[16,512]{1,0:T(8,128)S(1)}, u32[]{:S(2)}, u32[]{:S(2)}) collective-permute-start(f32[16,512]{1,0:T(8,128)S(1)} %get-tuple-element.180), channel_id=1, source_target_pairs={{64,0},{80,16},{96,32},{112,48},{0,64},{16,80},{32,96},{48,112},{6... | collective-permute-start | bytes 98312 | tf_op jit(solution)/shard_map/ppermute | solution.py:35
  (5 other events, 4.4 us)

commit v3 on v1

--- a/solution.py
+++ b/solution.py
@@ -244,12 +244,14 @@
     )(act, at_head)
 
 
-def backward_kernel(own_ref, one_ref, three_ref, two_ref, act_ref, att_ref, gate_ref, gg_ref, start_ref, slope_hbm, back_ref, dk_ref, dv_ref, slope_ref, sem):
+def backward_kernel(*refs):
+    act_ref, att_ref, gate_ref, gg_ref, start_ref, slope_hbm, back_ref = refs[H : H + 7]
+    dk_ref, dv_ref, slope_ref, sem = refs[H + 7 :]
     length = att_ref.shape[1]
     width = H * HD
     copy = pltpu.make_async_copy(slope_hbm, slope_ref, sem)
     copy.start()
-    heads = [ref[k] for ref in (own_ref, one_ref, three_ref, two_ref) for k in range(NX)]
+    heads = [ref[...] for ref in refs[:H]]
     mean_all = sum(a[0:1] for a in heads) * (1.0 / H)
     apart = [a[0:1] - mean_all for a in heads]
     spread = sum(a[1:2] for a in heads) + HD * sum(d * d for d in apart)
@@ -323,7 +325,7 @@
     shards = NZ * NX
     return pl.pallas_call(
         backward_kernel,
-        in_specs=[vmem()] * 9 + [pl.BlockSpec(memory_space=pl.ANY)],
+        in_specs=[vmem()] * (H + 5) + [pl.BlockSpec(memory_space=pl.ANY)],
         out_specs=vmem(),
         out_shape=jax.ShapeDtypeStruct((shards, length // shards, 5 * HD), BF16),
         scratch_shapes=[pltpu.VMEM((length, HD), F32)] * 2
@@ -352,18 +354,18 @@
     width, length = normed_t.shape
     shards, rows, _ = back.shape
     shape = jax.ShapeDtypeStruct((NY * NXH, 64, 4 * HD), F32)
-    out_spec = pl.BlockSpec((NY * NXH, 16, 4 * HD), lambda g: (0, g, 0))
+    out_spec = pl.BlockSpec((NY * NXH, 32, 4 * HD), lambda g: (0, g, 0))
     return pl.pallas_call(
         terms_in_kernel,
-        grid=(4,),
+        grid=(2,),
         in_specs=[
             smem(),
-            pl.BlockSpec((width // 4, length), lambda g: (g, 0)),
+            pl.BlockSpec((width // 2, length), lambda g: (g, 0)),
             pl.BlockSpec((shards, rows, 4 * HD), lambda g: (0, 0, 0)),
         ],
         out_specs=[out_spec] * 2,
         out_shape=[shape] * 2,
-        scratch_shapes=[pltpu.VMEM((width // 4, 4 * HD), F32)],
+        scratch_shapes=[pltpu.VMEM((width // 2, 4 * HD), F32)],
         compiler_params=params(LIMIT),
         cost_estimate=pl.CostEstimate(
             flops=2 * width * length * 4 * HD, bytes_accessed=9 << 20, transcendentals=0
@@ -632,15 +634,14 @@
     att, gate_t, gg_t, stats, start = forward(act, at_head)
     stats, fresh = tie((stats, fresh))
     cots.update(fresh)
-    pair = jnp.stack([stats, from_seq(stats, 0, 1)])
-    others = [from_seq(pair, dz, 0) for dz in (1, 3, 2)]
-    pair, others, cots = tie((pair, others, cots))
+    others = [from_seq(stats, dz, dx) for dz, dx in ((2, 1), (1, 1), (3, 1), (2, 0), (1, 0), (3, 0), (0, 1))]
+    stats, others, cots = tie((stats, others, cots))
     fresh = {
         (2, 1): from_seq(cots[2, 0], 0, 1),
         (1, 1): from_seq(cots[0, 1], 1, 0),
         (3, 1): from_seq(cots[0, 1], 3, 0),
     }
-    back = backward([pair, *others], act, att, gate_t, gg_t, start, slope)
+    back = backward([stats, *others], act, att, gate_t, gg_t, start, slope)
     back, fresh = tie((back, fresh))
     cots.update(fresh)
     cots[0, 0] = cot

time: 152 us -> 154 us (1.013)
  starting transfers between devices: 46.2 us -> 52.1 us
  waiting for transfers between devices: 26.6 us -> 23.6 us
    ppermute x21 -> x24, starting transfers between devices: 27.8 us -> 32.7 us  [from_seq(): return lax.ppermute(a, 'seq', seq_perm(dz, dx))]
    ppermute x21 -> x24, waiting for transfers between devices: 23.7 us -> 20.8 us  [from_seq(): return lax.ppermute(a, 'seq', seq_perm(dz, dx))]
    unnamed x42 -> x48, local copies, waits for them, and re-layouts: 3.55 us -> 3.55 us
  transfers between devices with their start and end apart: 31 -> 34, of which waited for: 14 -> 14; matrix products, arithmetic and copies ran while one was open for 5% -> 5% of each run, Pallas kernels for 42% -> 41%
where the time goes in v3:
time: 154 us; the launch traced here: 153 us
  Pallas kernels  65.2 us (42%)
  starting transfers between devices  52.1 us (34%)
  waiting for transfers between devices  23.6 us (15%)
  local copies, waits for them, and re-layouts  5.91 us (4%)
  other arithmetic  3.16 us (2%)
  matrix products  2.51 us (2%)
    ppermute x24, starting transfers between devices, from_seq(): return lax.ppermute(a, 'seq', seq_perm(dz, dx))  32.7 us
    ppermute x24, waiting for transfers between devices, from_seq(): return lax.ppermute(a, 'seq', seq_perm(dz, dx))  20.8 us
    pallas_call x4, Pallas kernels, ln_proj(): pl.pallas_call(functools.partial(ln_proj_kernel, len(blocks)), grid_spec=...  18.9 us
    pallas_call x1, Pallas kernels, backward(): pl.pallas_call(backward_kernel, in_specs=[vmem()] * (H + 5) + [pl.BlockSp...  13 us
    pallas_call x1, Pallas kernels, forward(): pl.pallas_call(forward_kernel, in_specs=[vmem()] * 2, out_specs=[vmem()]...  6.5 us
    pallas_call x1, Pallas kernels, shard_out(): pl.pallas_call(shard_out_kernel, grid=(2,), in_specs=[pl.BlockSpec((H, ro...  6.18 us
    pallas_call x1, Pallas kernels, terms_in(): pl.pallas_call(terms_in_kernel, grid=(2,), in_specs=[smem(), pl.BlockSpec...  5.99 us
    ppermute x5, starting transfers between devices, from_user(): return lax.ppermute(a, 'user', user_perm(dy, dh, dc))  5.82 us
  transfers between devices with their start and end apart: 34, of which 14 were waited for; matrix products, arithmetic and copies ran while one was open for 5% of the time, Pallas kernels for 41%

profile of v3, /device:TPU:0, one launch (start us, length us, event | category | flops | bytes accessed | tf_op | source)
XLA Modules:
  0.0 153.3 jit_solution(9086622148020468877)
XLA Ops:
  0.6 1.7 %collective-permute-start = (bf16[256,1024]{1,0:T(8,128)(2,1)}, bf16[256,1024]{1,0:T(8,128)(2,1)S(1)}, u32[]{:S(2)}, u32[]{:S(2)}) collective-permute-start(bf16[256,1024]{1,0:T(8,128)(2,1)} %bitcast.23), channel_id=1, source_target_pairs={{16,0},{0,16},{48,32},{32,48},{80,64},{64,80},{112,96},{96,112},{1... | collective-permute-start | bytes 1572872 | tf_op jit(solution)/shard_map/ppermute | solution.py:35
  2.3 4.0 %collective-permute-start.1 = (bf16[256,1024]{1,0:T(8,128)(2,1)}, bf16[256,1024]{1,0:T(8,128)(2,1)S(1)}, u32[]{:S(2)}, u32[]{:S(2)}) collective-permute-start(bf16[256,1024]{1,0:T(8,128)(2,1)} %bitcast.24), channel_id=1, source_target_pairs={{32,0},{48,16},{64,32},{80,48},{96,64},{112,80},{0,96},{16,112},{3... | collective-permute-start | bytes 1572872 | tf_op jit(solution)/shard_map/ppermute | solution.py:35
  6.3 2.5 %convolution_convert_fusion = bf16[256,1024]{1,0:T(8,128)(2,1)S(1)} fusion(bf16[1024,1024]{1,0:T(8,128)(2,1)} %w_out_ref.1, bf16[1,256,1024]{2,1,0:T(8,128)(2,1)} %param.9), kind=kOutput, calls=%fused_computation | convolution fusion | flops 537133056 | bytes 3145728 | tf_op jit(solution)/shard_map/dot_general | solution.py:68
  9.9 1.3 constant_dynamic-slice_fusion.3
  11.2 1.1 pad_maximum_fusion.refs_1_.refs_3_
  12.3 3.1 %ln_proj.4 = (bf16[1024,2048]{1,0:T(8,128)(2,1)}, bf16[2,8,128,512]{3,2,1,0:T(8,128)(2,1)}, f32[2,8,128,512]{3,2,1,0:T(8,128)}) custom-call(s32[1]{0:T(128)} %bitcast.1.at_ref, bf16[256,1024]{1,0:T(8,128)(2,1)} %bitcast.26, bf16[1024,512]{1,0:T(8,128)(2,1)} %pad_maximum_fusion.refs_1_.refs_3_), custom_call_target="tpu_custom_call" | custom-call | flops 268435456 | bytes 3145728 | tf_op jit(solution)/shard_map/ln_proj/pallas_call | solution.py:115
  16.6 0.9 collective-permute-done.1.refs_1_
  17.5 3.3 %collective-permute-done.2.refs_2_ = bf16[256,1024]{1,0:T(8,128)(2,1)S(1)} collective-permute-done((bf16[256,1024]{1,0:T(8,128)(2,1)}, bf16[256,1024]{1,0:T(8,128)(2,1)S(1)}, u32[]{:S(2)}, u32[]{:S(2)}) %collective-permute-start.2) | collective-permute-done | bytes 524320 | tf_op jit(solution)/shard_map/ppermute | solution.py:35
  21.7 1.7 %collective-permute-start.5 = (bf16[256,1024]{1,0:T(8,128)(2,1)S(1)}, bf16[256,1024]{1,0:T(8,128)(2,1)}, u32[]{:S(2)}, u32[]{:S(2)}) collective-permute-start(bf16[256,1024]{1,0:T(8,128)(2,1)S(1)} %collective-permute-done.refs_0_), channel_id=1, source_target_pairs={{96,0},{112,16},{0,32},{16,48},{32,64},{48,80},{64,96},{80,112},{9... | collective-permute-start | bytes 1572872 | tf_op jit(solution)/shard_map/ppermute | solution.py:35
  23.5 0.9 pad_maximum_fusion.1
  24.3 3.8 %all-to-all-start = ((bf16[8,272,128]{2,1,0:T(8,128)(2,1)}), bf16[8,272,128]{2,1,0:T(8,128)(2,1)S(1)}, u32[]{:S(2)}, u32[]{:S(2)}) async-start(bf16[8,272,128]{2,1,0:T(8,128)(2,1)} %pad_maximum_fusion.1), calls=%async_computation | async-start | bytes 1114112 | tf_op jit(solution)/shard_map/all_to_all | solution.py:619
  28.1 6.4 %ln_proj.5 = (bf16[1024,2048]{1,0:T(8,128)(2,1)}, bf16[2,8,128,512]{3,2,1,0:T(8,128)(2,1)}, f32[2,8,128,512]{3,2,1,0:T(8,128)}) custom-call(s32[3]{0:T(128)} %get-tuple-element.108.at_ref, bf16[256,1024]{1,0:T(8,128)(2,1)} %copy-done.6, bf16[256,1024]{1,0:T(8,128)(2,1)} %copy-done.7, ...), custom_call_target="tpu_custom_call", output_to_operand_aliasing={{0}: (5, {}), {1}: (6, {}), {2}: (7, {})} | custom-call | flops 805306368 | bytes 9437184 | tf_op jit(solution)/shard_map/ln_proj/pallas_call | solution.py:115
  34.6 1.2 collective-permute-done.3.refs_0_
  35.8 2.4 %collective-permute-done.4.refs_1_ = bf16[256,1024]{1,0:T(8,128)(2,1)} collective-permute-done((bf16[256,1024]{1,0:T(8,128)(2,1)S(1)}, bf16[256,1024]{1,0:T(8,128)(2,1)}, u32[]{:S(2)}, u32[]{:S(2)}) %collective-permute-start.4) | collective-permute-done | bytes 524320 | tf_op jit(solution)/shard_map/ppermute | solution.py:35
  38.7 3.3 %collective-permute-start.6 = (bf16[256,1024]{1,0:T(8,128)(2,1)}, bf16[256,1024]{1,0:T(8,128)(2,1)}, u32[]{:S(2)}, u32[]{:S(2)}) collective-permute-start(bf16[256,1024]{1,0:T(8,128)(2,1)} %collective-permute-done.4.refs_1_), channel_id=1, source_target_pairs={{16,0},{0,16},{48,32},{32,48},{80,64},{64,80},{112,96},{96,112},{1... | collective-permute-start | bytes 1572872 | tf_op jit(solution)/shard_map/ppermute | solution.py:35
  42.0 2.0 %collective-permute-start.8 = (bf16[256,1024]{1,0:T(8,128)(2,1)S(1)}, bf16[256,1024]{1,0:T(8,128)(2,1)S(1)}, u32[]{:S(2)}, u32[]{:S(2)}) collective-permute-start(bf16[256,1024]{1,0:T(8,128)(2,1)S(1)} %bitcast.34), channel_id=1, source_target_pairs={{96,0},{112,16},{0,32},{16,48},{32,64},{48,80},{64,96},{80,112},{9... | collective-permute-start | bytes 1572872 | tf_op jit(solution)/shard_map/ppermute | solution.py:35
  44.0 6.2 %ln_proj.6 = (bf16[1024,2048]{1,0:T(8,128)(2,1)}, bf16[2,8,128,512]{3,2,1,0:T(8,128)(2,1)}, f32[2,8,128,512]{3,2,1,0:T(8,128)}) custom-call(s32[3]{0:T(128)} %get-tuple-element.118.at_ref, bf16[256,1024]{1,0:T(8,128)(2,1)} %collective-permute-done.3.refs_0_, ...), custom_call_target="tpu_custom_call", output_to_operand_aliasing={{0}: (5, {}), {1}: (6, {}), {2}: (7, {})} | custom-call | flops 805306368 | bytes 9437184 | tf_op jit(solution)/shard_map/ln_proj/pallas_call | solution.py:115
  50.2 4.9 %collective-permute-done.6.refs_0_ = bf16[256,1024]{1,0:T(8,128)(2,1)} collective-permute-done((bf16[256,1024]{1,0:T(8,128)(2,1)}, bf16[256,1024]{1,0:T(8,128)(2,1)}, u32[]{:S(2)}, u32[]{:S(2)}) %collective-permute-start.6) | collective-permute-done | bytes 524320 | tf_op jit(solution)/shard_map/ppermute | solution.py:35
  55.4 3.2 %ln_proj.7 = (bf16[1024,2048]{1,0:T(8,128)(2,1)}, bf16[2,8,128,512]{3,2,1,0:T(8,128)(2,1)}, f32[2,8,128,512]{3,2,1,0:T(8,128)}) custom-call(s32[1]{0:T(128)} %bitcast.11.at_ref, bf16[256,1024]{1,0:T(8,128)(2,1)} %collective-permute-done.6.refs_0_, ...), custom_call_target="tpu_custom_call", output_to_operand_aliasing={{0}: (3, {}), {1}: (4, {}), {2}: (5, {})} | custom-call | flops 268435456 | bytes 3145728 | tf_op jit(solution)/shard_map/ln_proj/pallas_call | solution.py:115
  58.6 6.5 %attention_forward.1 = (f32[128,2048]{1,0:T(8,128)}, bf16[128,2048]{1,0:T(8,128)(2,1)}, bf16[128,2048]{1,0:T(8,128)(2,1)}, f32[4,2048]{1,0:T(4,128)}, s32[1,2048]{1,0:T(1,128)}) custom-call(bf16[2,8,128,512]{3,2,1,0:T(8,128)(2,1)} %get-tuple-element.136.act_ref.refs_8_, bf16[8,272,128]{2,1,0:T(8,128)(2,1)} %copy-done.5), custom_call_target="tpu_custom_call" | custom-call | flops 4294967296 | bytes 6291456 | tf_op jit(solution)/shard_map/attention_forward/pallas_call | solution.py:228
  65.3 2.1 %collective-permute-start.11 = (f32[4,2048]{1,0:T(4,128)}, f32[4,2048]{1,0:T(4,128)S(1)}, u32[]{:S(2)}, u32[]{:S(2)}) collective-permute-start(f32[4,2048]{1,0:T(4,128)} %get-tuple-element.144.refs_0_), channel_id=1, source_target_pairs={{80,0},{64,16},{112,32},{96,48},{16,64},{0,80},{48,96},{32,112},{8... | collective-permute-start | bytes 98312 | tf_op jit(solution)/shard_map/ppermute | solution.py:35
  67.3 3.4 %collective-permute-start.12 = (f32[4,2048]{1,0:T(4,128)}, f32[4,2048]{1,0:T(4,128)S(1)}, u32[]{:S(2)}, u32[]{:S(2)}) collective-permute-start(f32[4,2048]{1,0:T(4,128)} %get-tuple-element.144.refs_0_), channel_id=1, source_target_pairs={{48,0},{32,16},{80,32},{64,48},{112,64},{96,80},{16,96},{0,112},{4... | collective-permute-start | bytes 98312 | tf_op jit(solution)/shard_map/ppermute | solution.py:35
  70.7 1.8 %collective-permute-start.14 = (f32[4,2048]{1,0:T(4,128)}, f32[4,2048]{1,0:T(4,128)S(1)}, u32[]{:S(2)}, u32[]{:S(2)}) collective-permute-start(f32[4,2048]{1,0:T(4,128)} %get-tuple-element.144.refs_0_), channel_id=1, source_target_pairs={{64,0},{80,16},{96,32},{112,48},{0,64},{16,80},{32,96},{48,112},{6... | collective-permute-start | bytes 98312 | tf_op jit(solution)/shard_map/ppermute | solution.py:35
  72.5 2.2 %collective-permute-start.15 = (f32[4,2048]{1,0:T(4,128)}, f32[4,2048]{1,0:T(4,128)S(1)}, u32[]{:S(2)}, u32[]{:S(2)}) collective-permute-start(f32[4,2048]{1,0:T(4,128)} %get-tuple-element.144.refs_0_), channel_id=1, source_target_pairs={{32,0},{48,16},{64,32},{80,48},{96,64},{112,80},{0,96},{16,112},{3... | collective-permute-start | bytes 98312 | tf_op jit(solution)/shard_map/ppermute | solution.py:35
  74.8 0.9 collective-permute-start.16
  76.4 0.9 collective-permute-done.13.refs_3_
  77.3 1.6 %collective-permute-done.15.refs_5_ = f32[4,2048]{1,0:T(4,128)S(1)} collective-permute-done((f32[4,2048]{1,0:T(4,128)}, f32[4,2048]{1,0:T(4,128)S(1)}, u32[]{:S(2)}, u32[]{:S(2)}) %collective-permute-start.15) | collective-permute-done | bytes 32800 | tf_op jit(solution)/shard_map/ppermute | solution.py:35
  78.8 1.7 %collective-permute-done.16.refs_6_ = f32[4,2048]{1,0:T(4,128)S(1)} collective-permute-done((f32[4,2048]{1,0:T(4,128)}, f32[4,2048]{1,0:T(4,128)S(1)}, u32[]{:S(2)}, u32[]{:S(2)}) %collective-permute-start.16) | collective-permute-done | bytes 32800 | tf_op jit(solution)/shard_map/ppermute | solution.py:35
  80.5 2.0 %collective-permute-start.18 = (bf16[256,1024]{1,0:T(8,128)(2,1)S(1)}, bf16[256,1024]{1,0:T(8,128)(2,1)S(1)}, u32[]{:S(2)}, u32[]{:S(2)}) collective-permute-start(bf16[256,1024]{1,0:T(8,128)(2,1)S(1)} %collective-permute-done.9.refs_2_), channel_id=1, source_target_pairs={{32,0},{48,16},{64,32},{80,48},{96,64},{112,80},{0,96},{16,112},{3... | collective-permute-start | bytes 1572872 | tf_op jit(solution)/shard_map/ppermute | solution.py:35
  83.3 13.0 %attention_backward.1.grad_ref.gated_ref = bf16[8,256,640]{2,1,0:T(8,128)(2,1)} custom-call(f32[4,2048]{1,0:T(4,128)} %get-tuple-element.144.refs_0_, f32[4,2048]{1,0:T(4,128)} %copy-done.16, f32[4,2048]{1,0:T(4,128)} %copy-done.17, f32[4,2048]{1,0:T(4,128)} %copy-done.18, f32[4,2048]{1,0:T(4,128)} %copy-done.19, f32[4,2048]{1,0:T(4,128)} %copy-done.20, ...), custom_call_target="tpu_custom_call" | custom-call | flops 8053063680 | bytes 10485760 | tf_op jit(solution)/shard_map/attention_backward/pallas_call | solution.py:326
  96.4 0.8 copy-done.14
  97.4 5.2 %all-to-all-start.1 = ((bf16[8,256,640]{2,1,0:T(8,128)(2,1)}), bf16[8,256,640]{2,1,0:T(8,128)(2,1)S(1)}, u32[]{:S(2)}, u32[]{:S(2)}) async-start(bf16[8,256,640]{2,1,0:T(8,128)(2,1)} %attention_backward.1.grad_ref.gated_ref), calls=%async_computation.1 | async-start | bytes 5242880 | tf_op jit(solution)/shard_map/all_to_all | solution.py:648
  102.6 6.0 %terms_in.1 = (f32[8,64,512]{2,1,0:T(8,128)}, f32[8,64,512]{2,1,0:T(8,128)}) custom-call(s32[1]{0:T(128)} %bitcast.12.core_ref, bf16[1024,2048]{1,0:T(8,128)(2,1)} %get-tuple-element.135.normed_ref, bf16[8,256,640]{2,1,0:T(8,128)(2,1)} %attention_backward.1.grad_ref.gated_ref), custom_call_target="tpu_custom_call" | custom-call | flops 2147483648 | bytes 9437184 | tf_op jit(solution)/shard_map/terms_in/pallas_call | solution.py:358
  108.6 3.9 %terms_out.1 = (f32[8,16,512]{2,1,0:T(8,128)}, f32[8,16,512]{2,1,0:T(8,128)}) custom-call(s32[1]{0:T(128)} %bitcast.12.core_ref, s32[8]{0:T(128)} %stack.66.at_ref, bf16[8,256,640]{2,1,0:T(8,128)(2,1)} %attention_backward.1.grad_ref.gated_ref, bf16[256,1024]{1,0:T(8,128)(2,1)} %copy-done.9, bf16[256,1024]{1,0:T(8,128)(2,1)} %copy-done.10, ...), custom_call_target="tpu_custom_call" | custom-call | flops 536870912 | bytes 6291456 | tf_op jit(solution)/shard_map/terms_out/pallas_call | solution.py:403
  113.0 1.4 collective-permute-done.22.got_out_ref
  115.5 2.7 %core_sum.1 = (f32[2,80,512]{2,1,0:T(8,128)}, bf16[2,80,512]{2,1,0:T(8,128)(2,1)}, bf16[2,80,512]{2,1,0:T(8,128)(2,1)}, bf16[2,80,512]{2,1,0:T(8,128)(2,1)}) custom-call(s32[4]{0:T(128)} %pad_add_fusion.2.pos_ref, f32[8,64,512]{2,1,0:T(8,128)} %get-tuple-element.160.keep_ref, f32[8,64,512]{2,1,0:T(8,128)} %copy-done.4, ...), custom_call_target="tpu_custom_call" | custom-call | flops 2621440 | bytes 5242880 | tf_op jit(solution)/shard_map/core_sum/pallas_call | solution.py:421
  118.2 3.0 %collective-permute-start.23 = (bf16[2,80,512]{2,1,0:T(8,128)(2,1)}, bf16[2,80,512]{2,1,0:T(8,128)(2,1)S(1)}, u32[]{:S(2)}, u32[]{:S(2)}) collective-permute-start(bf16[2,80,512]{2,1,0:T(8,128)(2,1)} %get-tuple-element.170), channel_id=1, source_target_pairs={{4,0},{5,1},{6,2},{7,3},{8,4},{9,5},{10,6},{11,7},{12,8},{13,9},{1... | collective-permute-start | bytes 491528 | tf_op jit(solution)/shard_map/ppermute | solution.py:39
  121.2 2.2 %collective-permute-start.25 = (bf16[2,80,512]{2,1,0:T(8,128)(2,1)}, bf16[2,80,512]{2,1,0:T(8,128)(2,1)S(1)}, u32[]{:S(2)}, u32[]{:S(2)}) collective-permute-start(bf16[2,80,512]{2,1,0:T(8,128)(2,1)} %get-tuple-element.172), channel_id=1, source_target_pairs={{8,0},{9,1},{10,2},{11,3},{12,4},{13,5},{14,6},{15,7},{0,8},{1,9},... | collective-permute-start | bytes 491528 | tf_op jit(solution)/shard_map/ppermute | solution.py:39
  123.4 1.4 all-to-all-done.1.gated_ref.grad_ref
  124.9 1.5 copy-done.2
  126.3 6.2 %shard_out.1 = (bf16[256,1024]{1,0:T(8,128)(2,1)}, f32[256,1024]{1,0:T(8,128)}) custom-call(bf16[8,256,640]{2,1,0:T(8,128)(2,1)} %copy-done.2, bf16[8,256,640]{2,1,0:T(8,128)(2,1)} %copy-done.2, bf16[1024,4096]{1,0:T(8,128)(2,1)} %w_in_ref.3, bf16[1024,1024]{1,0:T(8,128)(2,1)} %w_out_ref.1, bf16[256,1024]{1,0:T(8,128)(2,1)} %bitcast.27), custom_call_target="tpu_custom_call" | custom-call | flops 1610612736 | bytes 8388608 | tf_op jit(solution)/shard_map/shard_out/pallas_call | solution.py:521
  133.2 2.9 %collective-permute-start.26 = (f32[48,512]{1,0:T(8,128)S(1)}, f32[48,512]{1,0:T(8,128)S(1)}, u32[]{:S(2)}, u32[]{:S(2)}) collective-permute-start(f32[48,512]{1,0:T(8,128)S(1)} %get-tuple-element.180), channel_id=1, source_target_pairs={{2,0},{3,1},{0,2},{1,3},{6,4},{7,5},{4,6},{5,7},{10,8},{11,9},{8,1... | collective-permute-start | bytes 294920 | tf_op jit(solution)/shard_map/ppermute | solution.py:47
  136.1 1.4 collective-permute-start.27
  137.8 5.5 %shard_grad.1 = bf16[256,1024]{1,0:T(8,128)(2,1)} custom-call(bf16[8,256,640]{2,1,0:T(8,128)(2,1)} %copy-done.2, bf16[1024,4096]{1,0:T(8,128)(2,1)} %w_in_ref.3, bf16[256,1024]{1,0:T(8,128)(2,1)} %bitcast.28, bf16[256,1024]{1,0:T(8,128)(2,1)} %bitcast.32, f32[256,1024]{1,0:T(8,128)} %get-tuple-element.183.half_ref), custom_call_target="tpu_custom_call" | custom-call | flops 1073741824 | bytes 8388608 | tf_op jit(solution)/shard_map/shard_grad/pallas_call | solution.py:544
  143.9 2.7 %collective-permute-start.29 = (f32[16,512]{1,0:T(8,128)S(1)}, f32[16,512]{1,0:T(8,128)S(1)}, u32[]{:S(2)}, u32[]{:S(2)}) collective-permute-start(f32[16,512]{1,0:T(8,128)S(1)} %get-tuple-element.190), channel_id=1, source_target_pairs={{32,0},{48,16},{64,32},{80,48},{96,64},{112,80},{0,96},{16,112},{3... | collective-permute-start | bytes 98312 | tf_op jit(solution)/shard_map/ppermute | solution.py:35
  146.6 2.3 %collective-permute-start.31 = (f32[16,512]{1,0:T(8,128)S(1)}, f32[16,512]{1,0:T(8,128)S(1)}, u32[]{:S(2)}, u32[]{:S(2)}) collective-permute-start(f32[16,512]{1,0:T(8,128)S(1)} %get-tuple-element.192), channel_id=1, source_target_pairs={{64,0},{80,16},{96,32},{112,48},{0,64},{16,80},{32,96},{48,112},{6... | collective-permute-start | bytes 98312 | tf_op jit(solution)/shard_map/ppermute | solution.py:35
  148.9 2.8 %collective-permute-done.30.three_ref = f32[16,512]{1,0:T(8,128)S(1)} collective-permute-done((f32[16,512]{1,0:T(8,128)S(1)}, f32[16,512]{1,0:T(8,128)S(1)}, u32[]{:S(2)}, u32[]{:S(2)}) %collective-permute-start.30) | collective-permute-done | bytes 32800 | tf_op jit(solution)/shard_map/ppermute | solution.py:35
  152.1 1.2 z_place.1
  (94 shorter events, 9.3 us)
Async XLA Ops:
  0.6 16.0 %collective-permute-start = (bf16[256,1024]{1,0:T(8,128)(2,1)}, bf16[256,1024]{1,0:T(8,128)(2,1)S(1)}, u32[]{:S(2)}, u32[]{:S(2)}) collective-permute-start(bf16[256,1024]{1,0:T(8,128)(2,1)} %bitcast.23), channel_id=1, source_target_pairs={{16,0},{0,16},{48,32},{32,48},{80,64},{64,80},{112,96},{96,112},{1... | collective-permute-start | bytes 1572872 | tf_op jit(solution)/shard_map/ppermute | solution.py:35
  2.3 15.3 %collective-permute-start.1 = (bf16[256,1024]{1,0:T(8,128)(2,1)}, bf16[256,1024]{1,0:T(8,128)(2,1)S(1)}, u32[]{:S(2)}, u32[]{:S(2)}) collective-permute-start(bf16[256,1024]{1,0:T(8,128)(2,1)} %bitcast.24), channel_id=1, source_target_pairs={{32,0},{48,16},{64,32},{80,48},{96,64},{112,80},{0,96},{16,112},{3... | collective-permute-start | bytes 1572872 | tf_op jit(solution)/shard_map/ppermute | solution.py:35
  6.3 14.5 %collective-permute-start.2 = (bf16[256,1024]{1,0:T(8,128)(2,1)}, bf16[256,1024]{1,0:T(8,128)(2,1)S(1)}, u32[]{:S(2)}, u32[]{:S(2)}) collective-permute-start(bf16[256,1024]{1,0:T(8,128)(2,1)} %bitcast.25), channel_id=1, source_target_pairs={{96,0},{112,16},{0,32},{16,48},{32,64},{48,80},{64,96},{80,112},{9... | collective-permute-start | bytes 1572872 | tf_op jit(solution)/shard_map/ppermute | solution.py:35
  11.2 12.2 %copy-start.23 = (s32[1,256]{1,0:T(1,128)S(1)}, s32[1,256]{1,0:T(1,128)}, u32[]{:S(2)}) copy-start(s32[1,256]{1,0:T(1,128)} %param.6) | copy-start | bytes 3076
  16.6 11.5 %copy-start.6 = (bf16[256,1024]{1,0:T(8,128)(2,1)}, bf16[256,1024]{1,0:T(8,128)(2,1)S(1)}, u32[]{:S(2)}) copy-start(bf16[256,1024]{1,0:T(8,128)(2,1)S(1)} %collective-permute-done.refs_0_) | copy-start | bytes 1572868
  17.5 10.6 %copy-start.7 = (bf16[256,1024]{1,0:T(8,128)(2,1)}, bf16[256,1024]{1,0:T(8,128)(2,1)S(1)}, u32[]{:S(2)}) copy-start(bf16[256,1024]{1,0:T(8,128)(2,1)S(1)} %collective-permute-done.1.refs_1_) | copy-start | bytes 1572868
  20.8 7.3 %copy-start.8 = (bf16[256,1024]{1,0:T(8,128)(2,1)}, bf16[256,1024]{1,0:T(8,128)(2,1)S(1)}, u32[]{:S(2)}) copy-start(bf16[256,1024]{1,0:T(8,128)(2,1)S(1)} %collective-permute-done.2.refs_2_) | copy-start | bytes 1572868
  20.8 15.0 %collective-permute-start.3 = (bf16[256,1024]{1,0:T(8,128)(2,1)S(1)}, bf16[256,1024]{1,0:T(8,128)(2,1)}, u32[]{:S(2)}, u32[]{:S(2)}) collective-permute-start(bf16[256,1024]{1,0:T(8,128)(2,1)S(1)} %collective-permute-done.1.refs_1_), channel_id=1, source_target_pairs={{16,0},{0,16},{48,32},{32,48},{80,64},{64,80},{112,96},{96,112},{1... | collective-permute-start | bytes 1572872 | tf_op jit(solution)/shard_map/ppermute | solution.py:35
  21.4 16.9 %collective-permute-start.4 = (bf16[256,1024]{1,0:T(8,128)(2,1)S(1)}, bf16[256,1024]{1,0:T(8,128)(2,1)}, u32[]{:S(2)}, u32[]{:S(2)}) collective-permute-start(bf16[256,1024]{1,0:T(8,128)(2,1)S(1)} %collective-permute-done.1.refs_1_), channel_id=1, source_target_pairs={{32,0},{48,16},{64,32},{80,48},{96,64},{112,80},{0,96},{16,112},{3... | collective-permute-start | bytes 1572872 | tf_op jit(solution)/shard_map/ppermute | solution.py:35
  21.7 17.0 %collective-permute-start.5 = (bf16[256,1024]{1,0:T(8,128)(2,1)S(1)}, bf16[256,1024]{1,0:T(8,128)(2,1)}, u32[]{:S(2)}, u32[]{:S(2)}) collective-permute-start(bf16[256,1024]{1,0:T(8,128)(2,1)S(1)} %collective-permute-done.refs_0_), channel_id=1, source_target_pairs={{96,0},{112,16},{0,32},{16,48},{32,64},{48,80},{64,96},{80,112},{9... | collective-permute-start | bytes 1572872 | tf_op jit(solution)/shard_map/ppermute | solution.py:35
  24.3 19.7 %all-to-all-start = ((bf16[8,272,128]{2,1,0:T(8,128)(2,1)}), bf16[8,272,128]{2,1,0:T(8,128)(2,1)S(1)}, u32[]{:S(2)}, u32[]{:S(2)}) async-start(bf16[8,272,128]{2,1,0:T(8,128)(2,1)} %pad_maximum_fusion.1), calls=%async_computation | async-start | bytes 1114112 | tf_op jit(solution)/shard_map/all_to_all | solution.py:619
  28.1 13.9 %copy-start.3 = (bf16[1,256,1024]{2,1,0:T(8,128)(2,1)S(1)}, bf16[1,256,1024]{2,1,0:T(8,128)(2,1)}, u32[]{:S(2)}) copy-start(bf16[1,256,1024]{2,1,0:T(8,128)(2,1)} %param.9) | copy-start | bytes 1572868
  38.7 16.4 %collective-permute-start.6 = (bf16[256,1024]{1,0:T(8,128)(2,1)}, bf16[256,1024]{1,0:T(8,128)(2,1)}, u32[]{:S(2)}, u32[]{:S(2)}) collective-permute-start(bf16[256,1024]{1,0:T(8,128)(2,1)} %collective-permute-done.4.refs_1_), channel_id=1, source_target_pairs={{16,0},{0,16},{48,32},{32,48},{80,64},{64,80},{112,96},{96,112},{1... | collective-permute-start | bytes 1572872 | tf_op jit(solution)/shard_map/ppermute | solution.py:35
  42.0 13.2 %collective-permute-start.7 = (bf16[256,1024]{1,0:T(8,128)(2,1)S(1)}, bf16[256,1024]{1,0:T(8,128)(2,1)S(1)}, u32[]{:S(2)}, u32[]{:S(2)}) collective-permute-start(bf16[256,1024]{1,0:T(8,128)(2,1)S(1)} %bitcast.33), channel_id=1, source_target_pairs={{32,0},{48,16},{64,32},{80,48},{96,64},{112,80},{0,96},{16,112},{3... | collective-permute-start | bytes 1572872 | tf_op jit(solution)/shard_map/ppermute | solution.py:35
  42.0 13.2 %collective-permute-start.8 = (bf16[256,1024]{1,0:T(8,128)(2,1)S(1)}, bf16[256,1024]{1,0:T(8,128)(2,1)S(1)}, u32[]{:S(2)}, u32[]{:S(2)}) collective-permute-start(bf16[256,1024]{1,0:T(8,128)(2,1)S(1)} %bitcast.34), channel_id=1, source_target_pairs={{96,0},{112,16},{0,32},{16,48},{32,64},{48,80},{64,96},{80,112},{9... | collective-permute-start | bytes 1572872 | tf_op jit(solution)/shard_map/ppermute | solution.py:35
  44.0 21.1 %collective-permute-start.9 = (bf16[256,1024]{1,0:T(8,128)(2,1)S(1)}, bf16[256,1024]{1,0:T(8,128)(2,1)S(1)}, u32[]{:S(2)}, u32[]{:S(2)}) collective-permute-start(bf16[256,1024]{1,0:T(8,128)(2,1)S(1)} %bitcast.35), channel_id=1, source_target_pairs={{16,0},{0,16},{48,32},{32,48},{80,64},{64,80},{112,96},{96,112},{1... | collective-permute-start | bytes 1572872 | tf_op jit(solution)/shard_map/ppermute | solution.py:35
  44.0 6.2 %copy-start.5 = (bf16[8,272,128]{2,1,0:T(8,128)(2,1)}, bf16[8,272,128]{2,1,0:T(8,128)(2,1)S(1)}, u32[]{:S(2)}) copy-start(bf16[8,272,128]{2,1,0:T(8,128)(2,1)S(1)} %all-to-all-done.head_ref) | copy-start | bytes 1671172
  55.1 10.1 %collective-permute-start.10 = (bf16[256,1024]{1,0:T(8,128)(2,1)S(1)}, bf16[256,1024]{1,0:T(8,128)(2,1)S(1)}, u32[]{:S(2)}, u32[]{:S(2)}) collective-permute-start(bf16[256,1024]{1,0:T(8,128)(2,1)S(1)} %collective-permute-done.7.refs_0_), channel_id=1, source_target_pairs={{32,0},{48,16},{64,32},{80,48},{96,64},{112,80},{0,96},{16,112},{3... | collective-permute-start | bytes 1572872 | tf_op jit(solution)/shard_map/ppermute | solution.py:35
  65.1 31.3 %copy-start.11 = (bf16[256,1024]{1,0:T(8,128)(2,1)}, bf16[256,1024]{1,0:T(8,128)(2,1)S(1)}, u32[]{:S(2)}) copy-start(bf16[256,1024]{1,0:T(8,128)(2,1)S(1)} %collective-permute-done.9.refs_2_) | copy-start | bytes 1572868
  65.3 31.1 %copy-start.12 = (bf16[256,1024]{1,0:T(8,128)(2,1)}, bf16[256,1024]{1,0:T(8,128)(2,1)S(1)}, u32[]{:S(2)}) copy-start(bf16[256,1024]{1,0:T(8,128)(2,1)S(1)} %collective-permute-done.10.refs_3_) | copy-start | bytes 1572868
  65.3 9.5 %collective-permute-start.11 = (f32[4,2048]{1,0:T(4,128)}, f32[4,2048]{1,0:T(4,128)S(1)}, u32[]{:S(2)}, u32[]{:S(2)}) collective-permute-start(f32[4,2048]{1,0:T(4,128)} %get-tuple-element.144.refs_0_), channel_id=1, source_target_pairs={{80,0},{64,16},{112,32},{96,48},{16,64},{0,80},{48,96},{32,112},{8... | collective-permute-start | bytes 98312 | tf_op jit(solution)/shard_map/ppermute | solution.py:35
  67.3 8.4 %collective-permute-start.12 = (f32[4,2048]{1,0:T(4,128)}, f32[4,2048]{1,0:T(4,128)S(1)}, u32[]{:S(2)}, u32[]{:S(2)}) collective-permute-start(f32[4,2048]{1,0:T(4,128)} %get-tuple-element.144.refs_0_), channel_id=1, source_target_pairs={{48,0},{32,16},{80,32},{64,48},{112,64},{96,80},{16,96},{0,112},{4... | collective-permute-start | bytes 98312 | tf_op jit(solution)/shard_map/ppermute | solution.py:35
  70.7 6.5 %collective-permute-start.13 = (f32[4,2048]{1,0:T(4,128)}, f32[4,2048]{1,0:T(4,128)S(1)}, u32[]{:S(2)}, u32[]{:S(2)}) collective-permute-start(f32[4,2048]{1,0:T(4,128)} %get-tuple-element.144.refs_0_), channel_id=1, source_target_pairs={{112,0},{96,16},{16,32},{0,48},{48,64},{32,80},{80,96},{64,112},{1... | collective-permute-start | bytes 98312 | tf_op jit(solution)/shard_map/ppermute | solution.py:35
  70.7 6.5 %collective-permute-start.14 = (f32[4,2048]{1,0:T(4,128)}, f32[4,2048]{1,0:T(4,128)S(1)}, u32[]{:S(2)}, u32[]{:S(2)}) collective-permute-start(f32[4,2048]{1,0:T(4,128)} %get-tuple-element.144.refs_0_), channel_id=1, source_target_pairs={{64,0},{80,16},{96,32},{112,48},{0,64},{16,80},{32,96},{48,112},{6... | collective-permute-start | bytes 98312 | tf_op jit(solution)/shard_map/ppermute | solution.py:35
  72.5 6.3 %collective-permute-start.15 = (f32[4,2048]{1,0:T(4,128)}, f32[4,2048]{1,0:T(4,128)S(1)}, u32[]{:S(2)}, u32[]{:S(2)}) collective-permute-start(f32[4,2048]{1,0:T(4,128)} %get-tuple-element.144.refs_0_), channel_id=1, source_target_pairs={{32,0},{48,16},{64,32},{80,48},{96,64},{112,80},{0,96},{16,112},{3... | collective-permute-start | bytes 98312 | tf_op jit(solution)/shard_map/ppermute | solution.py:35
  74.8 8.5 %copy-start.16 = (f32[4,2048]{1,0:T(4,128)}, f32[4,2048]{1,0:T(4,128)S(1)}, u32[]{:S(2)}) copy-start(f32[4,2048]{1,0:T(4,128)S(1)} %collective-permute-done.11.refs_1_) | copy-start | bytes 98308
  74.8 5.7 %collective-permute-start.16 = (f32[4,2048]{1,0:T(4,128)}, f32[4,2048]{1,0:T(4,128)S(1)}, u32[]{:S(2)}, u32[]{:S(2)}) collective-permute-start(f32[4,2048]{1,0:T(4,128)} %get-tuple-element.144.refs_0_), channel_id=1, source_target_pairs={{96,0},{112,16},{0,32},{16,48},{32,64},{48,80},{64,96},{80,112},{9... | collective-permute-start | bytes 98312 | tf_op jit(solution)/shard_map/ppermute | solution.py:35
  75.7 7.6 %copy-start.17 = (f32[4,2048]{1,0:T(4,128)}, f32[4,2048]{1,0:T(4,128)S(1)}, u32[]{:S(2)}) copy-start(f32[4,2048]{1,0:T(4,128)S(1)} %collective-permute-done.12.refs_2_) | copy-start | bytes 98308
  75.7 4.8 %collective-permute-start.17 = (f32[4,2048]{1,0:T(4,128)}, f32[4,2048]{1,0:T(4,128)S(1)}, u32[]{:S(2)}, u32[]{:S(2)}) collective-permute-start(f32[4,2048]{1,0:T(4,128)} %get-tuple-element.144.refs_0_), channel_id=1, source_target_pairs={{16,0},{0,16},{48,32},{32,48},{80,64},{64,80},{112,96},{96,112},{1... | collective-permute-start | bytes 98312 | tf_op jit(solution)/shard_map/ppermute | solution.py:35
  77.3 6.0 %copy-start.18 = (f32[4,2048]{1,0:T(4,128)}, f32[4,2048]{1,0:T(4,128)S(1)}, u32[]{:S(2)}) copy-start(f32[4,2048]{1,0:T(4,128)S(1)} %collective-permute-done.13.refs_3_) | copy-start | bytes 98308
  77.3 6.0 %copy-start.19 = (f32[4,2048]{1,0:T(4,128)}, f32[4,2048]{1,0:T(4,128)S(1)}, u32[]{:S(2)}) copy-start(f32[4,2048]{1,0:T(4,128)S(1)} %collective-permute-done.14.refs_4_) | copy-start | bytes 98308
  80.5 15.9 %collective-permute-start.18 = (bf16[256,1024]{1,0:T(8,128)(2,1)S(1)}, bf16[256,1024]{1,0:T(8,128)(2,1)S(1)}, u32[]{:S(2)}, u32[]{:S(2)}) collective-permute-start(bf16[256,1024]{1,0:T(8,128)(2,1)S(1)} %collective-permute-done.9.refs_2_), channel_id=1, source_target_pairs={{32,0},{48,16},{64,32},{80,48},{96,64},{112,80},{0,96},{16,112},{3... | collective-permute-start | bytes 1572872 | tf_op jit(solution)/shard_map/ppermute | solution.py:35
  82.6 14.7 %collective-permute-start.20 = (bf16[256,1024]{1,0:T(8,128)(2,1)S(1)}, bf16[256,1024]{1,0:T(8,128)(2,1)}, u32[]{:S(2)}, u32[]{:S(2)}) collective-permute-start(bf16[256,1024]{1,0:T(8,128)(2,1)S(1)} %collective-permute-done.9.refs_2_), channel_id=1, source_target_pairs={{96,0},{112,16},{0,32},{16,48},{32,64},{48,80},{64,96},{80,112},{9... | collective-permute-start | bytes 1572872 | tf_op jit(solution)/shard_map/ppermute | solution.py:35
  82.6 13.8 %collective-permute-start.19 = (bf16[256,1024]{1,0:T(8,128)(2,1)S(1)}, bf16[256,1024]{1,0:T(8,128)(2,1)S(1)}, u32[]{:S(2)}, u32[]{:S(2)}) collective-permute-start(bf16[256,1024]{1,0:T(8,128)(2,1)S(1)} %collective-permute-done.10.refs_3_), channel_id=1, source_target_pairs={{16,0},{0,16},{48,32},{32,48},{80,64},{64,80},{112,96},{96,112},{1... | collective-permute-start | bytes 1572872 | tf_op jit(solution)/shard_map/ppermute | solution.py:35
  97.4 27.5 %all-to-all-start.1 = ((bf16[8,256,640]{2,1,0:T(8,128)(2,1)}), bf16[8,256,640]{2,1,0:T(8,128)(2,1)S(1)}, u32[]{:S(2)}, u32[]{:S(2)}) async-start(bf16[8,256,640]{2,1,0:T(8,128)(2,1)} %attention_backward.1.grad_ref.gated_ref), calls=%async_computation.1 | async-start | bytes 5242880 | tf_op jit(solution)/shard_map/all_to_all | solution.py:648
  108.6 5.8 %collective-permute-start.21 = (f32[8,64,512]{2,1,0:T(8,128)}, f32[8,64,512]{2,1,0:T(8,128)S(1)}, u32[]{:S(2)}, u32[]{:S(2)}) collective-permute-start(f32[8,64,512]{2,1,0:T(8,128)} %get-tuple-element.161), channel_id=1, source_target_pairs={{1,0},{0,1},{3,2},{2,3},{5,4},{4,5},{7,6},{6,7},{9,8},{8,9},{11,10... | collective-permute-start | bytes 3145736 | tf_op jit(solution)/shard_map/ppermute | solution.py:39
  112.5 1.9 %collective-permute-start.22 = (f32[8,16,512]{2,1,0:T(8,128)}, f32[8,16,512]{2,1,0:T(8,128)S(1)}, u32[]{:S(2)}, u32[]{:S(2)}) collective-permute-start(f32[8,16,512]{2,1,0:T(8,128)} %get-tuple-element.169), channel_id=1, source_target_pairs={{1,0},{0,1},{3,2},{2,3},{5,4},{4,5},{7,6},{6,7},{9,8},{8,9},{11,10... | collective-permute-start | bytes 786440 | tf_op jit(solution)/shard_map/ppermute | solution.py:39
  118.2 14.3 %collective-permute-start.23 = (bf16[2,80,512]{2,1,0:T(8,128)(2,1)}, bf16[2,80,512]{2,1,0:T(8,128)(2,1)S(1)}, u32[]{:S(2)}, u32[]{:S(2)}) collective-permute-start(bf16[2,80,512]{2,1,0:T(8,128)(2,1)} %get-tuple-element.170), channel_id=1, source_target_pairs={{4,0},{5,1},{6,2},{7,3},{8,4},{9,5},{10,6},{11,7},{12,8},{13,9},{1... | collective-permute-start | bytes 491528 | tf_op jit(solution)/shard_map/ppermute | solution.py:39
  121.2 11.3 %collective-permute-start.24 = (bf16[2,80,512]{2,1,0:T(8,128)(2,1)}, bf16[2,80,512]{2,1,0:T(8,128)(2,1)S(1)}, u32[]{:S(2)}, u32[]{:S(2)}) collective-permute-start(bf16[2,80,512]{2,1,0:T(8,128)(2,1)} %get-tuple-element.171), channel_id=1, source_target_pairs={{12,0},{13,1},{14,2},{15,3},{0,4},{1,5},{2,6},{3,7},{4,8},{5,9},{6... | collective-permute-start | bytes 491528 | tf_op jit(solution)/shard_map/ppermute | solution.py:39
  121.2 11.3 %copy-start = (f32[2,80,512]{2,1,0:T(8,128)S(1)}, f32[2,80,512]{2,1,0:T(8,128)}, u32[]{:S(2)}) copy-start(f32[2,80,512]{2,1,0:T(8,128)} %get-tuple-element.176.own_ref) | copy-start | bytes 983044
  121.2 11.3 %copy-start.1 = (s32[4]{0:T(128)S(1)}, s32[4]{0:T(128)}, u32[]{:S(2)}) copy-start(s32[4]{0:T(128)} %pad_add_fusion.2.pos_ref) | copy-start | bytes 52
  121.2 11.3 %collective-permute-start.25 = (bf16[2,80,512]{2,1,0:T(8,128)(2,1)}, bf16[2,80,512]{2,1,0:T(8,128)(2,1)S(1)}, u32[]{:S(2)}, u32[]{:S(2)}) collective-permute-start(bf16[2,80,512]{2,1,0:T(8,128)(2,1)} %get-tuple-element.172), channel_id=1, source_target_pairs={{8,0},{9,1},{10,2},{11,3},{12,4},{13,5},{14,6},{15,7},{0,8},{1,9},... | collective-permute-start | bytes 491528 | tf_op jit(solution)/shard_map/ppermute | solution.py:39
  133.2 10.0 %collective-permute-start.26 = (f32[48,512]{1,0:T(8,128)S(1)}, f32[48,512]{1,0:T(8,128)S(1)}, u32[]{:S(2)}, u32[]{:S(2)}) collective-permute-start(f32[48,512]{1,0:T(8,128)S(1)} %get-tuple-element.180), channel_id=1, source_target_pairs={{2,0},{3,1},{0,2},{1,3},{6,4},{7,5},{4,6},{5,7},{10,8},{11,9},{8,1... | collective-permute-start | bytes 294920 | tf_op jit(solution)/shard_map/ppermute | solution.py:47
  136.1 7.1 %collective-permute-start.27 = (f32[32,512]{1,0:T(8,128)S(1)}, f32[32,512]{1,0:T(8,128)S(1)}, u32[]{:S(2)}, u32[]{:S(2)}) collective-permute-start(f32[32,512]{1,0:T(8,128)S(1)} %get-tuple-element.181), channel_id=1, source_target_pairs={{16,0},{17,1},{18,2},{19,3},{20,4},{21,5},{22,6},{23,7},{24,8},{25... | collective-permute-start | bytes 196616 | tf_op jit(solution)/shard_map/ppermute | solution.py:47
  137.5 5.7 %collective-permute-start.28 = (f32[32,512]{1,0:T(8,128)S(1)}, f32[32,512]{1,0:T(8,128)S(1)}, u32[]{:S(2)}, u32[]{:S(2)}) collective-permute-start(f32[32,512]{1,0:T(8,128)S(1)} %get-tuple-element.182), channel_id=1, source_target_pairs={{18,0},{19,1},{16,2},{17,3},{22,4},{23,5},{20,6},{21,7},{26,8},{27... | collective-permute-start | bytes 196616 | tf_op jit(solution)/shard_map/ppermute | solution.py:47
  143.9 5.1 %collective-permute-start.29 = (f32[16,512]{1,0:T(8,128)S(1)}, f32[16,512]{1,0:T(8,128)S(1)}, u32[]{:S(2)}, u32[]{:S(2)}) collective-permute-start(f32[16,512]{1,0:T(8,128)S(1)} %get-tuple-element.190), channel_id=1, source_target_pairs={{32,0},{48,16},{64,32},{80,48},{96,64},{112,80},{0,96},{16,112},{3... | collective-permute-start | bytes 98312 | tf_op jit(solution)/shard_map/ppermute | solution.py:35
  146.6 5.1 %collective-permute-start.30 = (f32[16,512]{1,0:T(8,128)S(1)}, f32[16,512]{1,0:T(8,128)S(1)}, u32[]{:S(2)}, u32[]{:S(2)}) collective-permute-start(f32[16,512]{1,0:T(8,128)S(1)} %get-tuple-element.191), channel_id=1, source_target_pairs={{96,0},{112,16},{0,32},{16,48},{32,64},{48,80},{64,96},{80,112},{9... | collective-permute-start | bytes 98312 | tf_op jit(solution)/shard_map/ppermute | solution.py:35
  146.6 5.5 %collective-permute-start.31 = (f32[16,512]{1,0:T(8,128)S(1)}, f32[16,512]{1,0:T(8,128)S(1)}, u32[]{:S(2)}, u32[]{:S(2)}) collective-permute-start(f32[16,512]{1,0:T(8,128)S(1)} %get-tuple-element.192), channel_id=1, source_target_pairs={{64,0},{80,16},{96,32},{112,48},{0,64},{16,80},{32,96},{48,112},{6... | collective-permute-start | bytes 98312 | tf_op jit(solution)/shard_map/ppermute | solution.py:35
  (10 other events, 22.0 us)

commit v4 on v1

--- a/solution.py
+++ b/solution.py
@@ -352,18 +352,18 @@
     width, length = normed_t.shape
     shards, rows, _ = back.shape
     shape = jax.ShapeDtypeStruct((NY * NXH, 64, 4 * HD), F32)
-    out_spec = pl.BlockSpec((NY * NXH, 16, 4 * HD), lambda g: (0, g, 0))
+    out_spec = pl.BlockSpec((NY * NXH, 32, 4 * HD), lambda g: (0, g, 0))
     return pl.pallas_call(
         terms_in_kernel,
-        grid=(4,),
+        grid=(2,),
         in_specs=[
             smem(),
-            pl.BlockSpec((width // 4, length), lambda g: (g, 0)),
+            pl.BlockSpec((width // 2, length), lambda g: (g, 0)),
             pl.BlockSpec((shards, rows, 4 * HD), lambda g: (0, 0, 0)),
         ],
         out_specs=[out_spec] * 2,
         out_shape=[shape] * 2,
-        scratch_shapes=[pltpu.VMEM((width // 4, 4 * HD), F32)],
+        scratch_shapes=[pltpu.VMEM((width // 2, 4 * HD), F32)],
         compiler_params=params(LIMIT),
         cost_estimate=pl.CostEstimate(
             flops=2 * width * length * 4 * HD, bytes_accessed=9 << 20, transcendentals=0
@@ -657,7 +657,7 @@
         at,
         [keep, got, keep_out, got_out],
         [((NXH, 80, n), F32)] + [((NXH, 80, n), BF16)] * 3,
-        limit=LIMIT,
+        limit=32,
     )
     own, sends = tie((own, sends))
     sends = [from_user(a, d, 0, 0) for a, d in zip(sends, (1, 3, 2))]

time: 152 us -> 151 us (level)
  waiting for transfers between devices: 26.6 us -> 30.4 us
  Pallas kernels: 65.7 us -> 63.2 us
  starting transfers between devices: 46.2 us -> 44.4 us
    all_to_all x1, waiting for transfers between devices: 1.5 us -> 4.04 us  [local(): back_tok = lax.all_to_all(back, 'seq', 0, 0, tiled=True)]
    pallas_call x4, Pallas kernels: 5.18 us -> 3.19 us  [small(): pl.pallas_call(kernel, in_specs=[smem()] + [vmem()] * len(arrays), out_sp...]
  transfers between devices with their start and end apart: 31 -> 31, of which waited for: 14 -> 14; matrix products, arithmetic and copies ran while one was open for 5% -> 5% of each run, Pallas kernels for 42% -> 40%
where the time goes in v4:
time: 151 us; the launch traced here: 150 us
  Pallas kernels  63.2 us (42%)
  starting transfers between devices  44.4 us (29%)
  waiting for transfers between devices  30.4 us (20%)
  local copies, waits for them, and re-layouts  5.05 us (3%)
  other arithmetic  3.4 us (2%)
  matrix products  2.51 us (2%)
    ppermute x21, starting transfers between devices, from_seq(): return lax.ppermute(a, 'seq', seq_perm(dz, dx))  26.3 us
    ppermute x21, waiting for transfers between devices, from_seq(): return lax.ppermute(a, 'seq', seq_perm(dz, dx))  25 us
    pallas_call x4, Pallas kernels, ln_proj(): pl.pallas_call(functools.partial(ln_proj_kernel, len(blocks)), grid_spec=...  18.9 us
    pallas_call x1, Pallas kernels, backward(): pl.pallas_call(backward_kernel, in_specs=[vmem()] * 9 + [pl.BlockSpec(mem...  13 us
    pallas_call x1, Pallas kernels, forward(): pl.pallas_call(forward_kernel, in_specs=[vmem()] * 2, out_specs=[vmem()]...  6.49 us
    pallas_call x1, Pallas kernels, shard_out(): pl.pallas_call(shard_out_kernel, grid=(2,), in_specs=[pl.BlockSpec((H, ro...  6.21 us
    pallas_call x1, Pallas kernels, terms_in(): pl.pallas_call(terms_in_kernel, grid=(2,), in_specs=[smem(), pl.BlockSpec...  5.93 us
    ppermute x5, starting transfers between devices, from_user(): return lax.ppermute(a, 'user', user_perm(dy, dh, dc))  5.78 us
  transfers between devices with their start and end apart: 31, of which 14 were waited for; matrix products, arithmetic and copies ran while one was open for 5% of the time, Pallas kernels for 40%

profile of v4, /device:TPU:0, one launch (start us, length us, event | category | flops | bytes accessed | tf_op | source)
XLA Modules:
  0.0 149.9 jit_solution(425311696423352238)
XLA Ops:
  0.6 1.7 %collective-permute-start = (bf16[256,1024]{1,0:T(8,128)(2,1)}, bf16[256,1024]{1,0:T(8,128)(2,1)S(1)}, u32[]{:S(2)}, u32[]{:S(2)}) collective-permute-start(bf16[256,1024]{1,0:T(8,128)(2,1)} %bitcast.25), channel_id=1, source_target_pairs={{16,0},{0,16},{48,32},{32,48},{80,64},{64,80},{112,96},{96,112},{1... | collective-permute-start | bytes 1572872 | tf_op jit(solution)/shard_map/ppermute | solution.py:35
  2.3 4.0 %collective-permute-start.1 = (bf16[256,1024]{1,0:T(8,128)(2,1)}, bf16[256,1024]{1,0:T(8,128)(2,1)S(1)}, u32[]{:S(2)}, u32[]{:S(2)}) collective-permute-start(bf16[256,1024]{1,0:T(8,128)(2,1)} %bitcast.26), channel_id=1, source_target_pairs={{32,0},{48,16},{64,32},{80,48},{96,64},{112,80},{0,96},{16,112},{3... | collective-permute-start | bytes 1572872 | tf_op jit(solution)/shard_map/ppermute | solution.py:35
  6.3 2.5 %convolution_convert_fusion = bf16[256,1024]{1,0:T(8,128)(2,1)S(1)} fusion(bf16[1024,1024]{1,0:T(8,128)(2,1)} %w_out_ref.1, bf16[1,256,1024]{2,1,0:T(8,128)(2,1)} %param.9), kind=kOutput, calls=%fused_computation | convolution fusion | flops 537133056 | bytes 3145728 | tf_op jit(solution)/shard_map/dot_general | solution.py:68
  9.9 1.3 constant_dynamic-slice_fusion.3
  11.2 1.1 pad_maximum_fusion.refs_1_.refs_3_
  12.3 3.1 %ln_proj.4 = (bf16[1024,2048]{1,0:T(8,128)(2,1)}, bf16[2,8,128,512]{3,2,1,0:T(8,128)(2,1)}, f32[2,8,128,512]{3,2,1,0:T(8,128)}) custom-call(s32[1]{0:T(128)} %bitcast.1.at_ref, bf16[256,1024]{1,0:T(8,128)(2,1)} %bitcast.28, bf16[1024,512]{1,0:T(8,128)(2,1)} %pad_maximum_fusion.refs_1_.refs_3_), custom_call_target="tpu_custom_call" | custom-call | flops 268435456 | bytes 3145728 | tf_op jit(solution)/shard_map/ln_proj/pallas_call | solution.py:115
  16.1 1.4 collective-permute-done.1.refs_1_
  17.5 3.3 %collective-permute-done.2.refs_2_ = bf16[256,1024]{1,0:T(8,128)(2,1)S(1)} collective-permute-done((bf16[256,1024]{1,0:T(8,128)(2,1)}, bf16[256,1024]{1,0:T(8,128)(2,1)S(1)}, u32[]{:S(2)}, u32[]{:S(2)}) %collective-permute-start.2) | collective-permute-done | bytes 524320 | tf_op jit(solution)/shard_map/ppermute | solution.py:35
  21.7 1.7 %collective-permute-start.5 = (bf16[256,1024]{1,0:T(8,128)(2,1)S(1)}, bf16[256,1024]{1,0:T(8,128)(2,1)}, u32[]{:S(2)}, u32[]{:S(2)}) collective-permute-start(bf16[256,1024]{1,0:T(8,128)(2,1)S(1)} %collective-permute-done.refs_0_), channel_id=1, source_target_pairs={{96,0},{112,16},{0,32},{16,48},{32,64},{48,80},{64,96},{80,112},{9... | collective-permute-start | bytes 1572872 | tf_op jit(solution)/shard_map/ppermute | solution.py:35
  23.5 0.9 pad_maximum_fusion.1
  24.3 3.8 %all-to-all-start = ((bf16[8,272,128]{2,1,0:T(8,128)(2,1)}), bf16[8,272,128]{2,1,0:T(8,128)(2,1)S(1)}, u32[]{:S(2)}, u32[]{:S(2)}) async-start(bf16[8,272,128]{2,1,0:T(8,128)(2,1)} %pad_maximum_fusion.1), calls=%async_computation | async-start | bytes 1114112 | tf_op jit(solution)/shard_map/all_to_all | solution.py:617
  28.1 6.4 %ln_proj.5 = (bf16[1024,2048]{1,0:T(8,128)(2,1)}, bf16[2,8,128,512]{3,2,1,0:T(8,128)(2,1)}, f32[2,8,128,512]{3,2,1,0:T(8,128)}) custom-call(s32[3]{0:T(128)} %get-tuple-element.104.at_ref, bf16[256,1024]{1,0:T(8,128)(2,1)} %copy-done.4, bf16[256,1024]{1,0:T(8,128)(2,1)} %copy-done.5, ...), custom_call_target="tpu_custom_call", output_to_operand_aliasing={{0}: (5, {}), {1}: (6, {}), {2}: (7, {})} | custom-call | flops 805306368 | bytes 9437184 | tf_op jit(solution)/shard_map/ln_proj/pallas_call | solution.py:115
  34.6 1.2 collective-permute-done.3.refs_0_
  35.7 2.7 %collective-permute-done.4.refs_1_ = bf16[256,1024]{1,0:T(8,128)(2,1)} collective-permute-done((bf16[256,1024]{1,0:T(8,128)(2,1)S(1)}, bf16[256,1024]{1,0:T(8,128)(2,1)}, u32[]{:S(2)}, u32[]{:S(2)}) %collective-permute-start.4) | collective-permute-done | bytes 524320 | tf_op jit(solution)/shard_map/ppermute | solution.py:35
  38.7 3.2 %collective-permute-start.6 = (bf16[256,1024]{1,0:T(8,128)(2,1)}, bf16[256,1024]{1,0:T(8,128)(2,1)S(1)}, u32[]{:S(2)}, u32[]{:S(2)}) collective-permute-start(bf16[256,1024]{1,0:T(8,128)(2,1)} %collective-permute-done.4.refs_1_), channel_id=1, source_target_pairs={{16,0},{0,16},{48,32},{32,48},{80,64},{64,80},{112,96},{96,112},{1... | collective-permute-start | bytes 1572872 | tf_op jit(solution)/shard_map/ppermute | solution.py:35
  42.0 2.0 %collective-permute-start.8 = (bf16[256,1024]{1,0:T(8,128)(2,1)S(1)}, bf16[256,1024]{1,0:T(8,128)(2,1)S(1)}, u32[]{:S(2)}, u32[]{:S(2)}) collective-permute-start(bf16[256,1024]{1,0:T(8,128)(2,1)S(1)} %bitcast.36), channel_id=1, source_target_pairs={{96,0},{112,16},{0,32},{16,48},{32,64},{48,80},{64,96},{80,112},{9... | collective-permute-start | bytes 1572872 | tf_op jit(solution)/shard_map/ppermute | solution.py:35
  44.1 6.3 %ln_proj.6 = (bf16[1024,2048]{1,0:T(8,128)(2,1)}, bf16[2,8,128,512]{3,2,1,0:T(8,128)(2,1)}, f32[2,8,128,512]{3,2,1,0:T(8,128)}) custom-call(s32[3]{0:T(128)} %get-tuple-element.114.at_ref, bf16[256,1024]{1,0:T(8,128)(2,1)} %copy-done.11, ...), custom_call_target="tpu_custom_call", output_to_operand_aliasing={{0}: (5, {}), {1}: (6, {}), {2}: (7, {})} | custom-call | flops 805306368 | bytes 9437184 | tf_op jit(solution)/shard_map/ln_proj/pallas_call | solution.py:115
  50.3 4.7 %collective-permute-done.6.refs_0_ = bf16[256,1024]{1,0:T(8,128)(2,1)S(1)} collective-permute-done((bf16[256,1024]{1,0:T(8,128)(2,1)}, bf16[256,1024]{1,0:T(8,128)(2,1)S(1)}, u32[]{:S(2)}, u32[]{:S(2)}) %collective-permute-start.6) | collective-permute-done | bytes 524320 | tf_op jit(solution)/shard_map/ppermute | solution.py:35
  55.8 3.1 %ln_proj.7 = (bf16[1024,2048]{1,0:T(8,128)(2,1)}, bf16[2,8,128,512]{3,2,1,0:T(8,128)(2,1)}, f32[2,8,128,512]{3,2,1,0:T(8,128)}) custom-call(s32[1]{0:T(128)} %bitcast.11.at_ref, bf16[256,1024]{1,0:T(8,128)(2,1)} %copy-done.14, bf16[1024,512]{1,0:T(8,128)(2,1)} %pad_maximum_fusion.refs_1_.refs_3_, ...), custom_call_target="tpu_custom_call", output_to_operand_aliasing={{0}: (3, {}), {1}: (4, {}), {2}: (5, {})} | custom-call | flops 268435456 | bytes 3145728 | tf_op jit(solution)/shard_map/ln_proj/pallas_call | solution.py:115
  58.9 6.5 %attention_forward.1 = (f32[128,2048]{1,0:T(8,128)}, bf16[128,2048]{1,0:T(8,128)(2,1)}, bf16[128,2048]{1,0:T(8,128)(2,1)}, f32[4,2048]{1,0:T(4,128)}, s32[1,2048]{1,0:T(1,128)}) custom-call(bf16[2,8,128,512]{3,2,1,0:T(8,128)(2,1)} %get-tuple-element.132.act_ref, bf16[8,272,128]{2,1,0:T(8,128)(2,1)} %copy-done.3), custom_call_target="tpu_custom_call" | custom-call | flops 4294967296 | bytes 6291456 | tf_op jit(solution)/shard_map/attention_forward/pallas_call | solution.py:228
  65.5 1.4 collective-permute-start.11
  66.9 2.8 %collective-permute-done.11 = f32[4,2048]{1,0:T(4,128)S(1)} collective-permute-done((f32[4,2048]{1,0:T(4,128)}, f32[4,2048]{1,0:T(4,128)S(1)}, u32[]{:S(2)}, u32[]{:S(2)}) %collective-permute-start.11) | collective-permute-done | bytes 32800 | tf_op jit(solution)/shard_map/ppermute | solution.py:35
  69.7 0.8 pad_maximum_fusion.2.own_ref
  70.7 1.9 %collective-permute-start.13 = (f32[2,4,2048]{2,1,0:T(4,128)S(1)}, f32[2,4,2048]{2,1,0:T(4,128)S(1)}, u32[]{:S(2)}, u32[]{:S(2)}) collective-permute-start(f32[2,4,2048]{2,1,0:T(4,128)S(1)} %pad_maximum_fusion.2.own_ref), channel_id=1, source_target_pairs={{96,0},{112,16},{0,32},{16,48},{32,64},{48,80},{64,96},{80,112},{9... | collective-permute-start | bytes 196616 | tf_op jit(solution)/shard_map/ppermute | solution.py:35
  72.6 1.5 %collective-permute-start.14 = (f32[2,4,2048]{2,1,0:T(4,128)S(1)}, f32[2,4,2048]{2,1,0:T(4,128)S(1)}, u32[]{:S(2)}, u32[]{:S(2)}) collective-permute-start(f32[2,4,2048]{2,1,0:T(4,128)S(1)} %pad_maximum_fusion.2.own_ref), channel_id=1, source_target_pairs={{64,0},{80,16},{96,32},{112,48},{0,64},{16,80},{32,96},{48,112},{6... | collective-permute-start | bytes 196616 | tf_op jit(solution)/shard_map/ppermute | solution.py:35
  74.1 1.5 collective-permute-done.12.one_ref
  75.6 1.3 collective-permute-done.13.three_ref
  76.9 2.2 %collective-permute-done.14.two_ref = f32[2,4,2048]{2,1,0:T(4,128)S(1)} collective-permute-done((f32[2,4,2048]{2,1,0:T(4,128)S(1)}, f32[2,4,2048]{2,1,0:T(4,128)S(1)}, u32[]{:S(2)}, u32[]{:S(2)}) %collective-permute-start.14) | collective-permute-done | bytes 65568 | tf_op jit(solution)/shard_map/ppermute | solution.py:35
  79.1 1.4 collective-permute-start.15
  81.1 1.4 collective-permute-start.16
  82.6 13.0 %attention_backward.1.grad_ref.gated_ref = bf16[8,256,640]{2,1,0:T(8,128)(2,1)} custom-call(f32[2,4,2048]{2,1,0:T(4,128)} %copy-done.16, f32[2,4,2048]{2,1,0:T(4,128)} %copy-done.17, f32[2,4,2048]{2,1,0:T(4,128)} %copy-done.18, f32[2,4,2048]{2,1,0:T(4,128)} %copy-done.19, bf16[2,8,128,512]{3,2,1,0:T(8,128)(2,1)} %get-tuple-element.132.act_ref, ...), custom_call_target="tpu_custom_call" | custom-call | flops 8053063680 | bytes 10485760 | tf_op jit(solution)/shard_map/attention_backward/pallas_call | solution.py:324
  95.7 0.7 copy-done.12
  96.8 4.4 %all-to-all-start.1 = ((bf16[8,256,640]{2,1,0:T(8,128)(2,1)}), bf16[8,256,640]{2,1,0:T(8,128)(2,1)}, u32[]{:S(2)}, u32[]{:S(2)}) async-start(bf16[8,256,640]{2,1,0:T(8,128)(2,1)} %attention_backward.1.grad_ref.gated_ref), calls=%async_computation.1 | async-start | bytes 5242880 | tf_op jit(solution)/shard_map/all_to_all | solution.py:647
  101.2 5.9 %terms_in.1 = (f32[8,64,512]{2,1,0:T(8,128)}, f32[8,64,512]{2,1,0:T(8,128)}) custom-call(s32[1]{0:T(128)} %bitcast.12.core_ref, bf16[1024,2048]{1,0:T(8,128)(2,1)} %get-tuple-element.131.normed_ref, bf16[8,256,640]{2,1,0:T(8,128)(2,1)} %attention_backward.1.grad_ref.gated_ref), custom_call_target="tpu_custom_call" | custom-call | flops 2147483648 | bytes 9437184 | tf_op jit(solution)/shard_map/terms_in/pallas_call | solution.py:356
  107.2 3.9 %terms_out.1 = (f32[8,16,512]{2,1,0:T(8,128)}, f32[8,16,512]{2,1,0:T(8,128)}) custom-call(s32[1]{0:T(128)} %bitcast.12.core_ref, s32[8]{0:T(128)} %stack.75.at_ref, bf16[8,256,640]{2,1,0:T(8,128)(2,1)} %attention_backward.1.grad_ref.gated_ref, bf16[256,1024]{1,0:T(8,128)(2,1)} %copy-done.7, bf16[256,1024]{1,0:T(8,128)(2,1)} %copy-done.8, ...), custom_call_target="tpu_custom_call" | custom-call | flops 536870912 | bytes 6291456 | tf_op jit(solution)/shard_map/terms_out/pallas_call | solution.py:401
  111.6 1.4 collective-permute-done.19.got_out_ref
  113.0 0.9 copy-done.1
  114.6 3.1 %collective-permute-start.20 = (bf16[2,80,512]{2,1,0:T(8,128)(2,1)S(1)}, bf16[2,80,512]{2,1,0:T(8,128)(2,1)S(1)}, u32[]{:S(2)}, u32[]{:S(2)}) collective-permute-start(bf16[2,80,512]{2,1,0:T(8,128)(2,1)S(1)} %get-tuple-element.162), channel_id=1, source_target_pairs={{4,0},{5,1},{6,2},{7,3},{8,4},{9,5},{10,6},{11,7},{12,8},{13,9},{1... | collective-permute-start | bytes 491528 | tf_op jit(solution)/shard_map/ppermute | solution.py:39
  117.7 2.2 %collective-permute-start.22 = (bf16[2,80,512]{2,1,0:T(8,128)(2,1)S(1)}, bf16[2,80,512]{2,1,0:T(8,128)(2,1)S(1)}, u32[]{:S(2)}, u32[]{:S(2)}) collective-permute-start(bf16[2,80,512]{2,1,0:T(8,128)(2,1)S(1)} %get-tuple-element.164), channel_id=1, source_target_pairs={{8,0},{9,1},{10,2},{11,3},{12,4},{13,5},{14,6},{15,7},{0,8},{1,9},... | collective-permute-start | bytes 491528 | tf_op jit(solution)/shard_map/ppermute | solution.py:39
  119.9 4.0 %all-to-all-done.1.gated_ref.grad_ref = bf16[8,256,640]{2,1,0:T(8,128)(2,1)} async-done(((bf16[8,256,640]{2,1,0:T(8,128)(2,1)}), bf16[8,256,640]{2,1,0:T(8,128)(2,1)}, u32[]{:S(2)}, u32[]{:S(2)}) %all-to-all-start.1) | async-done | bytes 2621472 | tf_op jit(solution)/shard_map/all_to_all | solution.py:647
  123.9 6.2 %shard_out.1 = (bf16[256,1024]{1,0:T(8,128)(2,1)}, f32[256,1024]{1,0:T(8,128)}) custom-call(bf16[8,256,640]{2,1,0:T(8,128)(2,1)} %all-to-all-done.1.gated_ref.grad_ref, bf16[8,256,640]{2,1,0:T(8,128)(2,1)} %all-to-all-done.1.gated_ref.grad_ref, bf16[1024,4096]{1,0:T(8,128)(2,1)} %w_in_ref.3, bf16[1024,1024]{1,0:T(8,128)(2,1)} %w_out_ref.1, ...), custom_call_target="tpu_custom_call" | custom-call | flops 1610612736 | bytes 8388608 | tf_op jit(solution)/shard_map/shard_out/pallas_call | solution.py:519
  130.9 2.8 %collective-permute-start.23 = (f32[48,512]{1,0:T(8,128)S(1)}, f32[48,512]{1,0:T(8,128)S(1)}, u32[]{:S(2)}, u32[]{:S(2)}) collective-permute-start(f32[48,512]{1,0:T(8,128)S(1)} %get-tuple-element.172), channel_id=1, source_target_pairs={{2,0},{3,1},{0,2},{1,3},{6,4},{7,5},{4,6},{5,7},{10,8},{11,9},{8,1... | collective-permute-start | bytes 294920 | tf_op jit(solution)/shard_map/ppermute | solution.py:47
  133.7 1.3 collective-permute-start.25
  135.0 5.5 %shard_grad.1 = bf16[256,1024]{1,0:T(8,128)(2,1)} custom-call(bf16[8,256,640]{2,1,0:T(8,128)(2,1)} %all-to-all-done.1.gated_ref.grad_ref, bf16[1024,4096]{1,0:T(8,128)(2,1)} %w_in_ref.3, bf16[256,1024]{1,0:T(8,128)(2,1)} %bitcast.30, bf16[256,1024]{1,0:T(8,128)(2,1)} %bitcast.34, f32[256,1024]{1,0:T(8,128)} %get-tuple-element.175.half_ref), custom_call_target="tpu_custom_call" | custom-call | flops 1073741824 | bytes 8388608 | tf_op jit(solution)/shard_map/shard_grad/pallas_call | solution.py:542
  141.1 1.7 %collective-permute-start.26 = (f32[16,512]{1,0:T(8,128)S(1)}, f32[16,512]{1,0:T(8,128)S(1)}, u32[]{:S(2)}, u32[]{:S(2)}) collective-permute-start(f32[16,512]{1,0:T(8,128)S(1)} %get-tuple-element.182), channel_id=1, source_target_pairs={{32,0},{48,16},{64,32},{80,48},{96,64},{112,80},{0,96},{16,112},{3... | collective-permute-start | bytes 98312 | tf_op jit(solution)/shard_map/ppermute | solution.py:35
  143.2 1.9 %collective-permute-start.28 = (f32[16,512]{1,0:T(8,128)S(1)}, f32[16,512]{1,0:T(8,128)S(1)}, u32[]{:S(2)}, u32[]{:S(2)}) collective-permute-start(f32[16,512]{1,0:T(8,128)S(1)} %get-tuple-element.184), channel_id=1, source_target_pairs={{64,0},{80,16},{96,32},{112,48},{0,64},{16,80},{32,96},{48,112},{6... | collective-permute-start | bytes 98312 | tf_op jit(solution)/shard_map/ppermute | solution.py:35
  145.1 2.8 %collective-permute-done.27.three_ref = f32[16,512]{1,0:T(8,128)S(1)} collective-permute-done((f32[16,512]{1,0:T(8,128)S(1)}, f32[16,512]{1,0:T(8,128)S(1)}, u32[]{:S(2)}, u32[]{:S(2)}) %collective-permute-start.27) | collective-permute-done | bytes 32800 | tf_op jit(solution)/shard_map/ppermute | solution.py:35
  148.6 1.2 z_place.1
  (83 shorter events, 8.9 us)
Async XLA Ops:
  0.6 15.5 %collective-permute-start = (bf16[256,1024]{1,0:T(8,128)(2,1)}, bf16[256,1024]{1,0:T(8,128)(2,1)S(1)}, u32[]{:S(2)}, u32[]{:S(2)}) collective-permute-start(bf16[256,1024]{1,0:T(8,128)(2,1)} %bitcast.25), channel_id=1, source_target_pairs={{16,0},{0,16},{48,32},{32,48},{80,64},{64,80},{112,96},{96,112},{1... | collective-permute-start | bytes 1572872 | tf_op jit(solution)/shard_map/ppermute | solution.py:35
  2.3 15.3 %collective-permute-start.1 = (bf16[256,1024]{1,0:T(8,128)(2,1)}, bf16[256,1024]{1,0:T(8,128)(2,1)S(1)}, u32[]{:S(2)}, u32[]{:S(2)}) collective-permute-start(bf16[256,1024]{1,0:T(8,128)(2,1)} %bitcast.26), channel_id=1, source_target_pairs={{32,0},{48,16},{64,32},{80,48},{96,64},{112,80},{0,96},{16,112},{3... | collective-permute-start | bytes 1572872 | tf_op jit(solution)/shard_map/ppermute | solution.py:35
  6.3 14.5 %collective-permute-start.2 = (bf16[256,1024]{1,0:T(8,128)(2,1)}, bf16[256,1024]{1,0:T(8,128)(2,1)S(1)}, u32[]{:S(2)}, u32[]{:S(2)}) collective-permute-start(bf16[256,1024]{1,0:T(8,128)(2,1)} %bitcast.27), channel_id=1, source_target_pairs={{96,0},{112,16},{0,32},{16,48},{32,64},{48,80},{64,96},{80,112},{9... | collective-permute-start | bytes 1572872 | tf_op jit(solution)/shard_map/ppermute | solution.py:35
  11.2 12.2 %copy-start.20 = (s32[1,256]{1,0:T(1,128)S(1)}, s32[1,256]{1,0:T(1,128)}, u32[]{:S(2)}) copy-start(s32[1,256]{1,0:T(1,128)} %param.6) | copy-start | bytes 3076
  16.1 12.0 %copy-start.4 = (bf16[256,1024]{1,0:T(8,128)(2,1)}, bf16[256,1024]{1,0:T(8,128)(2,1)S(1)}, u32[]{:S(2)}) copy-start(bf16[256,1024]{1,0:T(8,128)(2,1)S(1)} %collective-permute-done.refs_0_) | copy-start | bytes 1572868
  17.5 10.6 %copy-start.5 = (bf16[256,1024]{1,0:T(8,128)(2,1)}, bf16[256,1024]{1,0:T(8,128)(2,1)S(1)}, u32[]{:S(2)}) copy-start(bf16[256,1024]{1,0:T(8,128)(2,1)S(1)} %collective-permute-done.1.refs_1_) | copy-start | bytes 1572868
  20.8 7.3 %copy-start.6 = (bf16[256,1024]{1,0:T(8,128)(2,1)}, bf16[256,1024]{1,0:T(8,128)(2,1)S(1)}, u32[]{:S(2)}) copy-start(bf16[256,1024]{1,0:T(8,128)(2,1)S(1)} %collective-permute-done.2.refs_2_) | copy-start | bytes 1572868
  20.8 14.9 %collective-permute-start.3 = (bf16[256,1024]{1,0:T(8,128)(2,1)S(1)}, bf16[256,1024]{1,0:T(8,128)(2,1)S(1)}, u32[]{:S(2)}, u32[]{:S(2)}) collective-permute-start(bf16[256,1024]{1,0:T(8,128)(2,1)S(1)} %collective-permute-done.1.refs_1_), channel_id=1, source_target_pairs={{16,0},{0,16},{48,32},{32,48},{80,64},{64,80},{112,96},{96,112},{1... | collective-permute-start | bytes 1572872 | tf_op jit(solution)/shard_map/ppermute | solution.py:35
  21.4 17.0 %collective-permute-start.4 = (bf16[256,1024]{1,0:T(8,128)(2,1)S(1)}, bf16[256,1024]{1,0:T(8,128)(2,1)}, u32[]{:S(2)}, u32[]{:S(2)}) collective-permute-start(bf16[256,1024]{1,0:T(8,128)(2,1)S(1)} %collective-permute-done.1.refs_1_), channel_id=1, source_target_pairs={{32,0},{48,16},{64,32},{80,48},{96,64},{112,80},{0,96},{16,112},{3... | collective-permute-start | bytes 1572872 | tf_op jit(solution)/shard_map/ppermute | solution.py:35
  21.7 17.0 %collective-permute-start.5 = (bf16[256,1024]{1,0:T(8,128)(2,1)S(1)}, bf16[256,1024]{1,0:T(8,128)(2,1)}, u32[]{:S(2)}, u32[]{:S(2)}) collective-permute-start(bf16[256,1024]{1,0:T(8,128)(2,1)S(1)} %collective-permute-done.refs_0_), channel_id=1, source_target_pairs={{96,0},{112,16},{0,32},{16,48},{32,64},{48,80},{64,96},{80,112},{9... | collective-permute-start | bytes 1572872 | tf_op jit(solution)/shard_map/ppermute | solution.py:35
  24.3 19.8 %all-to-all-start = ((bf16[8,272,128]{2,1,0:T(8,128)(2,1)}), bf16[8,272,128]{2,1,0:T(8,128)(2,1)S(1)}, u32[]{:S(2)}, u32[]{:S(2)}) async-start(bf16[8,272,128]{2,1,0:T(8,128)(2,1)} %pad_maximum_fusion.1), calls=%async_computation | async-start | bytes 1114112 | tf_op jit(solution)/shard_map/all_to_all | solution.py:617
  28.1 13.9 %copy-start.2 = (bf16[1,256,1024]{2,1,0:T(8,128)(2,1)S(1)}, bf16[1,256,1024]{2,1,0:T(8,128)(2,1)}, u32[]{:S(2)}) copy-start(bf16[1,256,1024]{2,1,0:T(8,128)(2,1)} %param.9) | copy-start | bytes 1572868
  35.7 3.0 %copy-start.11 = (bf16[256,1024]{1,0:T(8,128)(2,1)}, bf16[256,1024]{1,0:T(8,128)(2,1)S(1)}, u32[]{:S(2)}) copy-start(bf16[256,1024]{1,0:T(8,128)(2,1)S(1)} %collective-permute-done.3.refs_0_) | copy-start | bytes 1572868
  38.7 16.3 %collective-permute-start.6 = (bf16[256,1024]{1,0:T(8,128)(2,1)}, bf16[256,1024]{1,0:T(8,128)(2,1)S(1)}, u32[]{:S(2)}, u32[]{:S(2)}) collective-permute-start(bf16[256,1024]{1,0:T(8,128)(2,1)} %collective-permute-done.4.refs_1_), channel_id=1, source_target_pairs={{16,0},{0,16},{48,32},{32,48},{80,64},{64,80},{112,96},{96,112},{1... | collective-permute-start | bytes 1572872 | tf_op jit(solution)/shard_map/ppermute | solution.py:35
  42.0 13.1 %collective-permute-start.7 = (bf16[256,1024]{1,0:T(8,128)(2,1)S(1)}, bf16[256,1024]{1,0:T(8,128)(2,1)S(1)}, u32[]{:S(2)}, u32[]{:S(2)}) collective-permute-start(bf16[256,1024]{1,0:T(8,128)(2,1)S(1)} %bitcast.35), channel_id=1, source_target_pairs={{32,0},{48,16},{64,32},{80,48},{96,64},{112,80},{0,96},{16,112},{3... | collective-permute-start | bytes 1572872 | tf_op jit(solution)/shard_map/ppermute | solution.py:35
  42.0 13.1 %collective-permute-start.8 = (bf16[256,1024]{1,0:T(8,128)(2,1)S(1)}, bf16[256,1024]{1,0:T(8,128)(2,1)S(1)}, u32[]{:S(2)}, u32[]{:S(2)}) collective-permute-start(bf16[256,1024]{1,0:T(8,128)(2,1)S(1)} %bitcast.36), channel_id=1, source_target_pairs={{96,0},{112,16},{0,32},{16,48},{32,64},{48,80},{64,96},{80,112},{9... | collective-permute-start | bytes 1572872 | tf_op jit(solution)/shard_map/ppermute | solution.py:35
  44.0 21.4 %collective-permute-start.9 = (bf16[256,1024]{1,0:T(8,128)(2,1)S(1)}, bf16[256,1024]{1,0:T(8,128)(2,1)S(1)}, u32[]{:S(2)}, u32[]{:S(2)}) collective-permute-start(bf16[256,1024]{1,0:T(8,128)(2,1)S(1)} %bitcast.37), channel_id=1, source_target_pairs={{16,0},{0,16},{48,32},{32,48},{80,64},{64,80},{112,96},{96,112},{1... | collective-permute-start | bytes 1572872 | tf_op jit(solution)/shard_map/ppermute | solution.py:35
  44.1 6.3 %copy-start.3 = (bf16[8,272,128]{2,1,0:T(8,128)(2,1)}, bf16[8,272,128]{2,1,0:T(8,128)(2,1)S(1)}, u32[]{:S(2)}) copy-start(bf16[8,272,128]{2,1,0:T(8,128)(2,1)S(1)} %all-to-all-done.head_ref) | copy-start | bytes 1671172
  55.0 3.9 %copy-start.7 = (bf16[256,1024]{1,0:T(8,128)(2,1)}, bf16[256,1024]{1,0:T(8,128)(2,1)S(1)}, u32[]{:S(2)}) copy-start(bf16[256,1024]{1,0:T(8,128)(2,1)S(1)} %collective-permute-done.7.refs_0_) | copy-start | bytes 1572868
  55.0 3.9 %copy-start.8 = (bf16[256,1024]{1,0:T(8,128)(2,1)}, bf16[256,1024]{1,0:T(8,128)(2,1)S(1)}, u32[]{:S(2)}) copy-start(bf16[256,1024]{1,0:T(8,128)(2,1)S(1)} %collective-permute-done.8.refs_1_) | copy-start | bytes 1572868
  55.0 10.4 %collective-permute-start.10 = (bf16[256,1024]{1,0:T(8,128)(2,1)S(1)}, bf16[256,1024]{1,0:T(8,128)(2,1)S(1)}, u32[]{:S(2)}, u32[]{:S(2)}) collective-permute-start(bf16[256,1024]{1,0:T(8,128)(2,1)S(1)} %collective-permute-done.7.refs_0_), channel_id=1, source_target_pairs={{32,0},{48,16},{64,32},{80,48},{96,64},{112,80},{0,96},{16,112},{3... | collective-permute-start | bytes 1572872 | tf_op jit(solution)/shard_map/ppermute | solution.py:35
  65.4 30.2 %copy-start.9 = (bf16[256,1024]{1,0:T(8,128)(2,1)}, bf16[256,1024]{1,0:T(8,128)(2,1)S(1)}, u32[]{:S(2)}) copy-start(bf16[256,1024]{1,0:T(8,128)(2,1)S(1)} %collective-permute-done.9.refs_2_) | copy-start | bytes 1572868
  65.5 30.2 %copy-start.10 = (bf16[256,1024]{1,0:T(8,128)(2,1)}, bf16[256,1024]{1,0:T(8,128)(2,1)S(1)}, u32[]{:S(2)}) copy-start(bf16[256,1024]{1,0:T(8,128)(2,1)S(1)} %collective-permute-done.10.refs_3_) | copy-start | bytes 1572868
  65.5 4.2 %collective-permute-start.11 = (f32[4,2048]{1,0:T(4,128)}, f32[4,2048]{1,0:T(4,128)S(1)}, u32[]{:S(2)}, u32[]{:S(2)}) collective-permute-start(f32[4,2048]{1,0:T(4,128)} %get-tuple-element.136), channel_id=1, source_target_pairs={{16,0},{0,16},{48,32},{32,48},{80,64},{64,80},{112,96},{96,112},{1... | collective-permute-start | bytes 98312 | tf_op jit(solution)/shard_map/ppermute | solution.py:35
  70.4 12.1 %copy-start.16 = (f32[2,4,2048]{2,1,0:T(4,128)}, f32[2,4,2048]{2,1,0:T(4,128)S(1)}, u32[]{:S(2)}) copy-start(f32[2,4,2048]{2,1,0:T(4,128)S(1)} %pad_maximum_fusion.2.own_ref) | copy-start | bytes 196612
  70.5 5.1 %collective-permute-start.12 = (f32[2,4,2048]{2,1,0:T(4,128)S(1)}, f32[2,4,2048]{2,1,0:T(4,128)S(1)}, u32[]{:S(2)}, u32[]{:S(2)}) collective-permute-start(f32[2,4,2048]{2,1,0:T(4,128)S(1)} %pad_maximum_fusion.2.own_ref), channel_id=1, source_target_pairs={{32,0},{48,16},{64,32},{80,48},{96,64},{112,80},{0,96},{16,112},{3... | collective-permute-start | bytes 196616 | tf_op jit(solution)/shard_map/ppermute | solution.py:35
  70.7 6.2 %collective-permute-start.13 = (f32[2,4,2048]{2,1,0:T(4,128)S(1)}, f32[2,4,2048]{2,1,0:T(4,128)S(1)}, u32[]{:S(2)}, u32[]{:S(2)}) collective-permute-start(f32[2,4,2048]{2,1,0:T(4,128)S(1)} %pad_maximum_fusion.2.own_ref), channel_id=1, source_target_pairs={{96,0},{112,16},{0,32},{16,48},{32,64},{48,80},{64,96},{80,112},{9... | collective-permute-start | bytes 196616 | tf_op jit(solution)/shard_map/ppermute | solution.py:35
  72.6 6.5 %collective-permute-start.14 = (f32[2,4,2048]{2,1,0:T(4,128)S(1)}, f32[2,4,2048]{2,1,0:T(4,128)S(1)}, u32[]{:S(2)}, u32[]{:S(2)}) collective-permute-start(f32[2,4,2048]{2,1,0:T(4,128)S(1)} %pad_maximum_fusion.2.own_ref), channel_id=1, source_target_pairs={{64,0},{80,16},{96,32},{112,48},{0,64},{16,80},{32,96},{48,112},{6... | collective-permute-start | bytes 196616 | tf_op jit(solution)/shard_map/ppermute | solution.py:35
  75.6 7.0 %copy-start.17 = (f32[2,4,2048]{2,1,0:T(4,128)}, f32[2,4,2048]{2,1,0:T(4,128)S(1)}, u32[]{:S(2)}) copy-start(f32[2,4,2048]{2,1,0:T(4,128)S(1)} %collective-permute-done.12.one_ref) | copy-start | bytes 196612
  76.9 5.7 %copy-start.18 = (f32[2,4,2048]{2,1,0:T(4,128)}, f32[2,4,2048]{2,1,0:T(4,128)S(1)}, u32[]{:S(2)}) copy-start(f32[2,4,2048]{2,1,0:T(4,128)S(1)} %collective-permute-done.13.three_ref) | copy-start | bytes 196612
  79.1 3.5 %copy-start.19 = (f32[2,4,2048]{2,1,0:T(4,128)}, f32[2,4,2048]{2,1,0:T(4,128)S(1)}, u32[]{:S(2)}) copy-start(f32[2,4,2048]{2,1,0:T(4,128)S(1)} %collective-permute-done.14.two_ref) | copy-start | bytes 196612
  79.1 16.5 %collective-permute-start.15 = (bf16[256,1024]{1,0:T(8,128)(2,1)S(1)}, bf16[256,1024]{1,0:T(8,128)(2,1)S(1)}, u32[]{:S(2)}, u32[]{:S(2)}) collective-permute-start(bf16[256,1024]{1,0:T(8,128)(2,1)S(1)} %collective-permute-done.9.refs_2_), channel_id=1, source_target_pairs={{32,0},{48,16},{64,32},{80,48},{96,64},{112,80},{0,96},{16,112},{3... | collective-permute-start | bytes 1572872 | tf_op jit(solution)/shard_map/ppermute | solution.py:35
  80.4 15.2 %collective-permute-start.17 = (bf16[256,1024]{1,0:T(8,128)(2,1)S(1)}, bf16[256,1024]{1,0:T(8,128)(2,1)S(1)}, u32[]{:S(2)}, u32[]{:S(2)}) collective-permute-start(bf16[256,1024]{1,0:T(8,128)(2,1)S(1)} %collective-permute-done.9.refs_2_), channel_id=1, source_target_pairs={{96,0},{112,16},{0,32},{16,48},{32,64},{48,80},{64,96},{80,112},{9... | collective-permute-start | bytes 1572872 | tf_op jit(solution)/shard_map/ppermute | solution.py:35
  81.1 14.5 %collective-permute-start.16 = (bf16[256,1024]{1,0:T(8,128)(2,1)S(1)}, bf16[256,1024]{1,0:T(8,128)(2,1)S(1)}, u32[]{:S(2)}, u32[]{:S(2)}) collective-permute-start(bf16[256,1024]{1,0:T(8,128)(2,1)S(1)} %collective-permute-done.10.refs_3_), channel_id=1, source_target_pairs={{16,0},{0,16},{48,32},{32,48},{80,64},{64,80},{112,96},{96,112},{1... | collective-permute-start | bytes 1572872 | tf_op jit(solution)/shard_map/ppermute | solution.py:35
  95.7 1.1 copy-start.13
  96.8 27.1 %all-to-all-start.1 = ((bf16[8,256,640]{2,1,0:T(8,128)(2,1)}), bf16[8,256,640]{2,1,0:T(8,128)(2,1)}, u32[]{:S(2)}, u32[]{:S(2)}) async-start(bf16[8,256,640]{2,1,0:T(8,128)(2,1)} %attention_backward.1.grad_ref.gated_ref), calls=%async_computation.1 | async-start | bytes 5242880 | tf_op jit(solution)/shard_map/all_to_all | solution.py:647
  107.2 5.8 %copy-start = (f32[8,64,512]{2,1,0:T(8,128)S(1)}, f32[8,64,512]{2,1,0:T(8,128)}, u32[]{:S(2)}) copy-start(f32[8,64,512]{2,1,0:T(8,128)} %get-tuple-element.152.keep_ref) | copy-start | bytes 3145732
  107.2 5.8 %collective-permute-start.18 = (f32[8,64,512]{2,1,0:T(8,128)}, f32[8,64,512]{2,1,0:T(8,128)S(1)}, u32[]{:S(2)}, u32[]{:S(2)}) collective-permute-start(f32[8,64,512]{2,1,0:T(8,128)} %get-tuple-element.153), channel_id=1, source_target_pairs={{1,0},{0,1},{3,2},{2,3},{5,4},{4,5},{7,6},{6,7},{9,8},{8,9},{11,10... | collective-permute-start | bytes 3145736 | tf_op jit(solution)/shard_map/ppermute | solution.py:39
  111.1 1.9 %collective-permute-start.19 = (f32[8,16,512]{2,1,0:T(8,128)}, f32[8,16,512]{2,1,0:T(8,128)S(1)}, u32[]{:S(2)}, u32[]{:S(2)}) collective-permute-start(f32[8,16,512]{2,1,0:T(8,128)} %get-tuple-element.161), channel_id=1, source_target_pairs={{1,0},{0,1},{3,2},{2,3},{5,4},{4,5},{7,6},{6,7},{9,8},{8,9},{11,10... | collective-permute-start | bytes 786440 | tf_op jit(solution)/shard_map/ppermute | solution.py:39
  114.6 15.5 %collective-permute-start.20 = (bf16[2,80,512]{2,1,0:T(8,128)(2,1)S(1)}, bf16[2,80,512]{2,1,0:T(8,128)(2,1)S(1)}, u32[]{:S(2)}, u32[]{:S(2)}) collective-permute-start(bf16[2,80,512]{2,1,0:T(8,128)(2,1)S(1)} %get-tuple-element.162), channel_id=1, source_target_pairs={{4,0},{5,1},{6,2},{7,3},{8,4},{9,5},{10,6},{11,7},{12,8},{13,9},{1... | collective-permute-start | bytes 491528 | tf_op jit(solution)/shard_map/ppermute | solution.py:39
  117.7 12.5 %collective-permute-start.21 = (bf16[2,80,512]{2,1,0:T(8,128)(2,1)S(1)}, bf16[2,80,512]{2,1,0:T(8,128)(2,1)S(1)}, u32[]{:S(2)}, u32[]{:S(2)}) collective-permute-start(bf16[2,80,512]{2,1,0:T(8,128)(2,1)S(1)} %get-tuple-element.163), channel_id=1, source_target_pairs={{12,0},{13,1},{14,2},{15,3},{0,4},{1,5},{2,6},{3,7},{4,8},{5,9},{6... | collective-permute-start | bytes 491528 | tf_op jit(solution)/shard_map/ppermute | solution.py:39
  117.7 12.5 %collective-permute-start.22 = (bf16[2,80,512]{2,1,0:T(8,128)(2,1)S(1)}, bf16[2,80,512]{2,1,0:T(8,128)(2,1)S(1)}, u32[]{:S(2)}, u32[]{:S(2)}) collective-permute-start(bf16[2,80,512]{2,1,0:T(8,128)(2,1)S(1)} %get-tuple-element.164), channel_id=1, source_target_pairs={{8,0},{9,1},{10,2},{11,3},{12,4},{13,5},{14,6},{15,7},{0,8},{1,9},... | collective-permute-start | bytes 491528 | tf_op jit(solution)/shard_map/ppermute | solution.py:39
  130.9 9.7 %collective-permute-start.23 = (f32[48,512]{1,0:T(8,128)S(1)}, f32[48,512]{1,0:T(8,128)S(1)}, u32[]{:S(2)}, u32[]{:S(2)}) collective-permute-start(f32[48,512]{1,0:T(8,128)S(1)} %get-tuple-element.172), channel_id=1, source_target_pairs={{2,0},{3,1},{0,2},{1,3},{6,4},{7,5},{4,6},{5,7},{10,8},{11,9},{8,1... | collective-permute-start | bytes 294920 | tf_op jit(solution)/shard_map/ppermute | solution.py:47
  133.7 6.8 %collective-permute-start.24 = (f32[32,512]{1,0:T(8,128)S(1)}, f32[32,512]{1,0:T(8,128)S(1)}, u32[]{:S(2)}, u32[]{:S(2)}) collective-permute-start(f32[32,512]{1,0:T(8,128)S(1)} %get-tuple-element.173), channel_id=1, source_target_pairs={{16,0},{17,1},{18,2},{19,3},{20,4},{21,5},{22,6},{23,7},{24,8},{25... | collective-permute-start | bytes 196616 | tf_op jit(solution)/shard_map/ppermute | solution.py:47
  133.7 6.8 %collective-permute-start.25 = (f32[32,512]{1,0:T(8,128)S(1)}, f32[32,512]{1,0:T(8,128)S(1)}, u32[]{:S(2)}, u32[]{:S(2)}) collective-permute-start(f32[32,512]{1,0:T(8,128)S(1)} %get-tuple-element.174), channel_id=1, source_target_pairs={{18,0},{19,1},{16,2},{17,3},{22,4},{23,5},{20,6},{21,7},{26,8},{27... | collective-permute-start | bytes 196616 | tf_op jit(solution)/shard_map/ppermute | solution.py:47
  141.1 4.0 %collective-permute-start.26 = (f32[16,512]{1,0:T(8,128)S(1)}, f32[16,512]{1,0:T(8,128)S(1)}, u32[]{:S(2)}, u32[]{:S(2)}) collective-permute-start(f32[16,512]{1,0:T(8,128)S(1)} %get-tuple-element.182), channel_id=1, source_target_pairs={{32,0},{48,16},{64,32},{80,48},{96,64},{112,80},{0,96},{16,112},{3... | collective-permute-start | bytes 98312 | tf_op jit(solution)/shard_map/ppermute | solution.py:35
  142.8 5.1 %collective-permute-start.27 = (f32[16,512]{1,0:T(8,128)S(1)}, f32[16,512]{1,0:T(8,128)S(1)}, u32[]{:S(2)}, u32[]{:S(2)}) collective-permute-start(f32[16,512]{1,0:T(8,128)S(1)} %get-tuple-element.183), channel_id=1, source_target_pairs={{96,0},{112,16},{0,32},{16,48},{32,64},{48,80},{64,96},{80,112},{9... | collective-permute-start | bytes 98312 | tf_op jit(solution)/shard_map/ppermute | solution.py:35
  143.2 5.4 %collective-permute-start.28 = (f32[16,512]{1,0:T(8,128)S(1)}, f32[16,512]{1,0:T(8,128)S(1)}, u32[]{:S(2)}, u32[]{:S(2)}) collective-permute-start(f32[16,512]{1,0:T(8,128)S(1)} %get-tuple-element.184), channel_id=1, source_target_pairs={{64,0},{80,16},{96,32},{112,48},{0,64},{16,80},{32,96},{48,112},{6... | collective-permute-start | bytes 98312 | tf_op jit(solution)/shard_map/ppermute | solution.py:35
  (4 other events, 3.5 us)
